TPU v7x, 32 devices: a whole 2x2x4 slice. The times are simulated.
32 devices in a mesh: dp: 8 (over z, core), expert: 4 (over y, x).
Axes of the slice: x: 2, y: 2, z: 4, core: 2. Of those that a mesh axis runs over, the one named last changes fastest.
Arguments:
- tokens: bfloat16 [2, 8, 256, 2048], P(None, 'dp', 'expert'), may hold values from -6 to 6
- lengths: int32 [2, 8], P(None, 'dp'), may hold values from 193 to 256, as said below
- attention_routes: int32 [2, 8, 256, 2], P(None, 'dp', 'expert'), may hold values from 0 to 7, all different within a row; in each aligned block of 64 rows (0 to 63, 64 to 127, ..., all dimensions but the last counted through in order) at most 24 rows name the same one
- feedforward_routes: int32 [2, 8, 256, 2], P(None, 'dp', 'expert'), may hold values from 0 to 7, all different within a row; in each aligned block of 64 rows (0 to 63, 64 to 127, ..., all dimensions but the last counted through in order) at most 24 rows name the same one
- norm_gains: bfloat16 [2048, 2], P(('dp', 'expert')), may hold values from 0.5 to 1.5
- router_weight: bfloat16 [2048, 16], P(('dp', 'expert')), may hold values from -0.09375 to 0.09375
- key_value_weight: bfloat16 [2048, 4096], P(('dp', 'expert')), may hold values from -0.125 to 0.125
- query_weight: bfloat16 [8, 2048, 2048], P('expert', 'dp'), may hold values from -0.125 to 0.125
- output_weight: bfloat16 [8, 2048, 2048], P('expert', 'dp'), may hold values from -0.75 to 0.75
- input_weight: bfloat16 [8, 2048, 11264], P('expert', 'dp'), may hold values from -0.125 to 0.125
- down_weight: bfloat16 [8, 5632, 2048], P('expert', 'dp'), may hold values from -0.15625 to 0.15625
- cotangent: bfloat16 [2, 8, 256, 2048], P(None, 'dp', 'expert'), may hold values from -6 to 6
Outputs:
- result: bfloat16 [2, 8, 256, 2048], P(None, 'dp', 'expert')
- grad_tokens: bfloat16 [2, 8, 256, 2048], P(None, 'dp', 'expert')
- grad_norm_gains: float32 [2048, 2], P(('dp', 'expert'))
- grad_router_weight: float32 [2048, 16], P(('dp', 'expert'))
- grad_key_value_weight: float32 [2048, 4096], P(('dp', 'expert'))
- grad_query_weight: float32 [8, 2048, 2048], P('expert', 'dp')
- grad_output_weight: float32 [8, 2048, 2048], P('expert', 'dp')
- grad_input_weight: float32 [8, 2048, 11264], P('expert', 'dp')
- grad_down_weight: float32 [8, 5632, 2048], P('expert', 'dp')
Inputs may be any that keep to these rules, and one draw needn't show every extreme that they name: `lengths`: each row fills more than 192 slots; in every draw some row fills all 256. `attention_routes`: A slot's 2 experts differ. Among the 64 slots of one device in one micro-batch no expert is named more than 24 times, a bound that some block reaches. `feedforward_routes`: A slot's 2 experts differ. Among the 64 slots of one device in one micro-batch no expert is named more than 24 times, a bound that some block reaches.
All inputs are finite; a program needn't handle non-finite values.
Results may differ from a plain program's by a relative error of at most 0.02.
Values may be sent and summed in bfloat16 or wider, within the bound.
A program may use at most 704 MiB of HBM per device.

v0:
```python
import jax
import jax.numpy as jnp
from jax import lax
from jax.sharding import PartitionSpec as P

D = 2048
KVH = 16
HD = 128
FF = 5632
NEXP = 8
MB = 2
TOK_MB = 64
CAP = 24


EPSILON = 1e-06
HIGHEST = lax.Precision.HIGHEST


def rotate(values, places, direction):
    half_size = HD // 2
    frequency = 10000.0 ** (-(jnp.arange(half_size, dtype=jnp.float32) * (2.0 / HD)))
    angles = places.astype(jnp.float32)[..., None] * frequency
    cosine = jnp.cos(angles)[..., None, :]
    sine_part = direction * jnp.sin(angles)[..., None, :]
    shaped = values.reshape(values.shape[:-1] + (KVH, HD))
    former = shaped[..., :half_size]
    latter = shaped[..., half_size:]
    turned = jnp.concatenate(
        [former * cosine - latter * sine_part, latter * cosine + former * sine_part], axis=-1
    )
    return turned.reshape(values.shape)


def product(pattern, operand, factor):
    return jnp.einsum(pattern, operand, factor, preferred_element_type=jnp.float32)


def norm_forward(values, norm_gain):
    inverse = lax.rsqrt(jnp.mean(values * values, axis=-1, keepdims=True) + EPSILON)
    return (values * inverse * norm_gain, inverse)


def norm_backward(values, inverse, norm_gain, grad_normed):
    scaled = grad_normed * norm_gain
    grad_gain = jnp.sum(grad_normed * values * inverse, axis=0)
    grad_values = inverse * scaled - values * inverse**3 * jnp.mean(
        scaled * values, axis=-1, keepdims=True
    )
    return (grad_values, grad_gain)


def route_tables(routes):
    flattened = routes.reshape(-1)
    onehot = (flattened[:, None] == jnp.arange(NEXP, dtype=jnp.int32)[None, :]).astype(jnp.int32)
    earlier = jnp.sum((jnp.cumsum(onehot, axis=0) - onehot) * onehot, axis=1)
    target = (flattened * CAP + earlier).reshape(routes.shape)
    slot_ids = jnp.arange(NEXP * CAP, dtype=jnp.int32)
    matches = slot_ids[None, :, None] == jnp.transpose(target)[:, None, :]
    choose = (routes[:, :, None] == jnp.arange(NEXP, dtype=jnp.int32)[None, None, :]).astype(
        jnp.float32
    )
    return (matches, choose)


def gate_values(logits, choose):
    picked = jnp.sum(choose * logits[:, None, :], axis=-1)
    highest = jnp.max(picked, axis=-1, keepdims=True)
    exponent = jnp.exp(picked - highest)
    return exponent / jnp.sum(exponent, axis=-1, keepdims=True)


def gate_grads(gate_probs, grad_gate_probs, choose):
    weighted = jnp.sum(gate_probs * grad_gate_probs, axis=-1, keepdims=True)
    grad_picked = gate_probs * (grad_gate_probs - weighted)
    return jnp.sum(grad_picked[:, :, None] * choose, axis=1)


def shards(
    tokens,
    lengths,
    attention_routes,
    feedforward_routes,
    norm_gains,
    router_weight,
    key_value_weight,
    query_weight,
    output_weight,
    input_weight,
    down_weight,
    cotangent,
):
    owners = lax.axis_size("expert")
    local_count = NEXP // owners
    row_length = owners * TOK_MB
    att_width = KVH * HD
    scaling = HD ** (-0.5)
    home_places = lax.axis_index("expert") * TOK_MB + jnp.arange(TOK_MB, dtype=jnp.int32)
    key_places = jnp.arange(row_length, dtype=jnp.int32)

    def by_expert(received):
        return (
            received.reshape(owners, local_count, CAP, -1)
            .transpose(1, 0, 2, 3)
            .reshape(local_count, owners * CAP, -1)
        )

    def to_owners(slot_rows):
        return by_expert(
            lax.all_to_all(
                slot_rows.reshape(owners, local_count * CAP, D),
                "expert",
                split_axis=0,
                concat_axis=0,
                tiled=True,
            )
        )

    def to_sources(expert_rows):
        merged = (
            expert_rows.reshape(local_count, owners, CAP, D)
            .transpose(1, 0, 2, 3)
            .reshape(owners, local_count * CAP, D)
        )
        return lax.all_to_all(merged, "expert", split_axis=0, concat_axis=0, tiled=True).reshape(
            NEXP * CAP, D
        )

    result_rows = []
    grad_token_rows = []
    shared_total = None
    expert_total = None
    for micro_batch in range(MB):
        weights_now = (
            (
                lax.all_gather(norm_gains, ("dp", "expert"), axis=0, tiled=True),
                lax.all_gather(router_weight, ("dp", "expert"), axis=0, tiled=True),
                lax.all_gather(key_value_weight, ("dp", "expert"), axis=0, tiled=True),
            ),
            (
                lax.all_gather(query_weight, "dp", axis=1, tiled=True),
                lax.all_gather(output_weight, "dp", axis=1, tiled=True),
                lax.all_gather(input_weight, "dp", axis=1, tiled=True),
                lax.all_gather(down_weight, "dp", axis=1, tiled=True),
            ),
        )
        norm_full, router_full, key_value_full = weights_now[0]
        query_full, output_full, input_full, down_full = weights_now[1]
        gain_mixer = norm_full[:, 0].astype(jnp.float32)
        gain_feed = norm_full[:, 1].astype(jnp.float32)
        router_mixer = router_full[:, :NEXP]
        router_feed = router_full[:, NEXP:]
        row_tokens = tokens[micro_batch, 0].astype(jnp.float32)
        length = lengths[micro_batch, 0]
        valid_mask = (home_places < length).astype(jnp.float32)
        matches_mixer, choose_mixer = route_tables(attention_routes[micro_batch, 0])
        matches_feed, choose_feed = route_tables(feedforward_routes[micro_batch, 0])
        slot_places = jnp.sum(jnp.where(matches_mixer, home_places[None, None, :], 0), axis=(0, 2))
        matches_mixer = matches_mixer.astype(jnp.bfloat16)
        matches_feed = matches_feed.astype(jnp.bfloat16)
        normed_mixer, inverse_mixer = norm_forward(row_tokens, gain_mixer)
        normed_mixer = normed_mixer.astype(jnp.bfloat16)
        logits_mixer = jnp.dot(normed_mixer, router_mixer, preferred_element_type=jnp.float32)
        gates_mixer = gate_values(logits_mixer, choose_mixer)
        key_value = jnp.dot(normed_mixer, key_value_full, preferred_element_type=jnp.float32)
        key_home = rotate(key_value[:, :att_width], home_places, 1.0).astype(jnp.bfloat16)
        value_home = key_value[:, att_width:].astype(jnp.bfloat16)
        key_rows = lax.all_gather(key_home, "expert", axis=0, tiled=True)
        value_rows = lax.all_gather(value_home, "expert", axis=0, tiled=True)
        received_places = lax.all_to_all(
            slot_places.reshape(owners, local_count * CAP),
            "expert",
            split_axis=0,
            concat_axis=0,
            tiled=True,
        )
        query_places = by_expert(received_places[..., None])[..., 0]
        rows_mixer = to_owners(
            product("kst,td->sd", matches_mixer, normed_mixer).astype(jnp.bfloat16)
        )
        query_pre = product("erd,eda->era", rows_mixer, query_full)
        queries = (rotate(query_pre, query_places, 1.0) * scaling).astype(jnp.bfloat16)
        query_heads = queries.reshape(local_count, -1, KVH, HD)
        key_heads = key_rows.reshape(row_length, KVH, HD)
        value_heads = value_rows.reshape(row_length, KVH, HD)
        allowed = (key_places[None, None, :] <= query_places[:, :, None]) & (
            key_places[None, None, :] < length
        )

        def masked_scores():
            raw_scores = product("erhd,khd->ehrk", query_heads, key_heads)
            return jnp.where(allowed[:, None], raw_scores, -1e30)

        scores = masked_scores()
        highest = jnp.max(scores, axis=-1, keepdims=True)
        exponent = jnp.exp(scores - highest)
        totals = jnp.sum(exponent, axis=-1, keepdims=True)
        log_total = highest + jnp.log(totals)
        attn_probs = (exponent / totals).astype(jnp.bfloat16)
        mixture = (
            product("ehrk,khd->erhd", attn_probs, value_heads)
            .reshape(local_count, -1, att_width)
            .astype(jnp.bfloat16)
        )
        mixer_rows = product("era,ead->erd", mixture, output_full).astype(jnp.bfloat16)
        routed_mixer = product("kst,sd->ktd", matches_mixer, to_sources(mixer_rows))
        second = row_tokens + jnp.sum(jnp.transpose(gates_mixer)[:, :, None] * routed_mixer, axis=0)
        normed_feed, inverse_feed = norm_forward(second, gain_feed)
        normed_feed = normed_feed.astype(jnp.bfloat16)
        logits_feed = jnp.dot(normed_feed, router_feed, preferred_element_type=jnp.float32)
        gates_feed = gate_values(logits_feed, choose_feed)
        rows_feed = to_owners(product("kst,td->sd", matches_feed, normed_feed).astype(jnp.bfloat16))
        hidden = product("erd,edf->erf", rows_feed, input_full)
        gate_part = hidden[..., :FF]
        up_part = hidden[..., FF:]
        active = (jax.nn.silu(gate_part) * up_part).astype(jnp.bfloat16)
        feed_rows = product("erf,efd->erd", active, down_full).astype(jnp.bfloat16)
        routed_feed = product("kst,sd->ktd", matches_feed, to_sources(feed_rows))
        result = second + jnp.sum(jnp.transpose(gates_feed)[:, :, None] * routed_feed, axis=0)
        grad_result = cotangent[micro_batch, 0].astype(jnp.float32) * valid_mask[:, None]
        grad_gates_feed = jnp.transpose(jnp.sum(routed_feed * grad_result[None], axis=-1))
        grad_logits_feed = gate_grads(gates_feed, grad_gates_feed, choose_feed)
        route_grads_feed = (jnp.transpose(gates_feed)[:, :, None] * grad_result[None]).astype(
            jnp.bfloat16
        )
        grad_feed_rows = to_owners(
            product("kst,ktd->sd", matches_feed, route_grads_feed).astype(jnp.bfloat16)
        )
        grad_active = product("erd,efd->erf", grad_feed_rows, down_full)
        grad_down = product("erf,erd->efd", active, grad_feed_rows)
        sigmoid = jax.nn.sigmoid(gate_part)
        grad_gate = grad_active * up_part * sigmoid * (1.0 + gate_part * (1.0 - sigmoid))
        grad_up = grad_active * jax.nn.silu(gate_part)
        grad_hidden = jnp.concatenate([grad_gate, grad_up], axis=-1).astype(jnp.bfloat16)
        grad_input = product("erd,erf->edf", rows_feed, grad_hidden)
        grad_rows_feed = product("erf,edf->erd", grad_hidden, input_full).astype(jnp.bfloat16)
        back_feed = to_sources(grad_rows_feed)
        grad_normed_feed = jnp.sum(product("kst,sd->ktd", matches_feed, back_feed), axis=0)
        grad_normed_feed = grad_normed_feed + jnp.dot(
            grad_logits_feed, router_feed.astype(jnp.float32).T, precision=HIGHEST
        )
        grad_router_feed = jnp.dot(
            normed_feed.astype(jnp.float32).T, grad_logits_feed, precision=HIGHEST
        )
        grad_second, grad_gain_feed = norm_backward(
            second, inverse_feed, gain_feed, grad_normed_feed
        )
        grad_second = grad_second + grad_result
        grad_gates_mixer = jnp.transpose(jnp.sum(routed_mixer * grad_second[None], axis=-1))
        grad_logits_mixer = gate_grads(gates_mixer, grad_gates_mixer, choose_mixer)
        route_grads_mixer = (jnp.transpose(gates_mixer)[:, :, None] * grad_second[None]).astype(
            jnp.bfloat16
        )
        grad_mixer_rows = to_owners(
            product("kst,ktd->sd", matches_mixer, route_grads_mixer).astype(jnp.bfloat16)
        )
        grad_mixture = product("erd,ead->era", grad_mixer_rows, output_full).astype(jnp.bfloat16)
        grad_output = product("era,erd->ead", mixture, grad_mixer_rows)
        recomputed = jnp.exp(masked_scores() - log_total)
        grad_mixture_heads = grad_mixture.reshape(local_count, -1, KVH, HD)
        grad_probs = product("erhd,khd->ehrk", grad_mixture_heads, value_heads)
        grad_value_rows = product(
            "ehrk,erhd->khd", recomputed.astype(jnp.bfloat16), grad_mixture_heads
        ).reshape(row_length, att_width)
        row_dot = jnp.sum(recomputed * grad_probs, axis=-1, keepdims=True)
        grad_scores = (recomputed * (grad_probs - row_dot)).astype(jnp.bfloat16)
        grad_queries = product("ehrk,khd->erhd", grad_scores, key_heads).reshape(
            local_count, -1, att_width
        )
        grad_key_rows = product("ehrk,erhd->khd", grad_scores, query_heads).reshape(
            row_length, att_width
        )
        grad_query_pre = (rotate(grad_queries, query_places, -1.0) * scaling).astype(jnp.bfloat16)
        grad_query = product("erd,era->eda", rows_mixer, grad_query_pre)
        grad_rows_mixer = product("era,eda->erd", grad_query_pre, query_full).astype(jnp.bfloat16)
        back_mixer = to_sources(grad_rows_mixer)
        grad_key_home = lax.psum_scatter(
            grad_key_rows.astype(jnp.bfloat16), "expert", scatter_dimension=0, tiled=True
        ).astype(jnp.float32)
        grad_value_home = lax.psum_scatter(
            grad_value_rows.astype(jnp.bfloat16), "expert", scatter_dimension=0, tiled=True
        ).astype(jnp.float32)
        grad_key_value = jnp.concatenate(
            [rotate(grad_key_home, home_places, -1.0), grad_value_home], axis=-1
        ).astype(jnp.bfloat16)
        grad_key_value_w = product("td,tc->dc", normed_mixer, grad_key_value)
        grad_normed_mixer = product("tc,dc->td", grad_key_value, key_value_full)
        grad_normed_mixer = grad_normed_mixer + jnp.sum(
            product("kst,sd->ktd", matches_mixer, back_mixer), axis=0
        )
        grad_normed_mixer = grad_normed_mixer + jnp.dot(
            grad_logits_mixer, router_mixer.astype(jnp.float32).T, precision=HIGHEST
        )
        grad_router_mixer = jnp.dot(
            normed_mixer.astype(jnp.float32).T, grad_logits_mixer, precision=HIGHEST
        )
        grad_row_tokens, grad_gain_mixer = norm_backward(
            row_tokens, inverse_mixer, gain_mixer, grad_normed_mixer
        )
        grad_row_tokens = grad_row_tokens + grad_second
        gain_terms = jnp.stack([grad_gain_mixer, grad_gain_feed], axis=1)
        router_terms = jnp.concatenate([grad_router_mixer, grad_router_feed], axis=1)
        shared_terms = (gain_terms, router_terms, grad_key_value_w)
        expert_terms = (grad_query, grad_output, grad_input, grad_down)
        result_now, grad_now, shared_terms, expert_terms = (
            result.astype(jnp.bfloat16),
            grad_row_tokens.astype(jnp.bfloat16),
            shared_terms,
            expert_terms,
        )
        result_rows.append(result_now)
        grad_token_rows.append(grad_now)
        shared_terms = (
            lax.psum_scatter(shared_terms[0], ("dp", "expert"), scatter_dimension=0, tiled=True),
            lax.psum_scatter(shared_terms[1], ("dp", "expert"), scatter_dimension=0, tiled=True),
            lax.psum_scatter(shared_terms[2], ("dp", "expert"), scatter_dimension=0, tiled=True),
        )
        expert_terms = (
            lax.psum_scatter(
                expert_terms[0].astype(jnp.bfloat16), "dp", scatter_dimension=1, tiled=True
            ).astype(jnp.float32),
            lax.psum_scatter(
                expert_terms[1].astype(jnp.bfloat16), "dp", scatter_dimension=1, tiled=True
            ).astype(jnp.float32),
            lax.psum_scatter(
                expert_terms[2].astype(jnp.bfloat16), "dp", scatter_dimension=1, tiled=True
            ).astype(jnp.float32),
            lax.psum_scatter(
                expert_terms[3].astype(jnp.bfloat16), "dp", scatter_dimension=1, tiled=True
            ).astype(jnp.float32),
        )
        if micro_batch == 0:
            shared_total = shared_terms
            expert_total = expert_terms
        else:
            shared_total = jax.tree.map(jnp.add, shared_total, shared_terms)
            expert_total = jax.tree.map(jnp.add, expert_total, expert_terms)
    result_all = jnp.stack(result_rows)[:, None]
    grad_all = jnp.stack(grad_token_rows)[:, None]
    return (
        result_all,
        grad_all,
        shared_total[0],
        shared_total[1],
        shared_total[2],
        expert_total[0],
        expert_total[1],
        expert_total[2],
        expert_total[3],
    )


def solution(mesh):
    return jax.shard_map(
        shards,
        mesh=mesh,
        in_specs=(
            P(None, "dp", "expert", None),
            P(None, "dp"),
            P(None, "dp", "expert", None),
            P(None, "dp", "expert", None),
            P(("dp", "expert"), None),
            P(("dp", "expert"), None),
            P(("dp", "expert"), None),
            P("expert", "dp", None),
            P("expert", "dp", None),
            P("expert", "dp", None),
            P("expert", "dp", None),
            P(None, "dp", "expert", None),
        ),
        out_specs=(
            P(None, "dp", "expert", None),
            P(None, "dp", "expert", None),
            P(("dp", "expert"), None),
            P(("dp", "expert"), None),
            P(("dp", "expert"), None),
            P("expert", "dp", None),
            P("expert", "dp", None),
            P("expert", "dp", None),
            P("expert", "dp", None),
        ),
        check_vma=False,
    )
```

profile of v0, /device:TPU:1, one launch (start us, length us, event | category | flops | bytes accessed | tf_op | source)
XLA Modules:
  0.0 6463.8 jit_solution(4201157867235907885)
XLA Ops:
  8.7 64.6 all-gather
  75.3 53.2 all-gather.12.cloned.1.call-done
  161.1 80.0 %all-gather.1 = bf16[32,64,16]{1,2,0:T(8,128)(2,1)S(1)} all-gather(bf16[1,64,16]{1,2,0:T(8,128)(2,1)S(1)} %bitcast.704), channel_id=1, replica_groups=mesh['dp'=8,'expert'=4] {'dp','expert'}, dimensions={0}, use_global_device_ids=true | all-gather | bytes 67584 | tf_op jit(solution)/shard_map/all_gather | solution.py:137
  246.0 34.0 all-gather.18.cloned.1.call-done
  309.3 26.5 all-gather.16.cloned.1.call-done
  341.4 147.4 %all-gather.20.cloned.1.call-done = bf16[2,2048,2048]{2,1,0:T(8,128)(2,1)} async-done(((bf16[2,256,2048]{2,1,0:T(8,128)(2,1)}), bf16[2,2048,2048]{2,1,0:T(8,128)(2,1)}) %all-gather.20.cloned.1.call-update) | async-done | bytes 16777232 | tf_op jit(solution)/shard_map/all_gather | solution.py:142
  674.8 679.6 %all-gather.22.cloned.1.call-done = bf16[2,2048,11264]{2,1,0:T(8,128)(2,1)} async-done(((bf16[2,256,11264]{2,1,0:T(8,128)(2,1)}), bf16[2,2048,11264]{2,1,0:T(8,128)(2,1)}) %all-gather.22.cloned.1.call-update) | async-done | bytes 92274704 | tf_op jit(solution)/shard_map/all_gather | solution.py:143
  1354.4 42.8 fusion.185
  1397.1 349.2 %all-gather.24.cloned.1.call-done = bf16[2,5632,2048]{2,1,0:T(8,128)(2,1)} async-done(((bf16[2,704,2048]{2,1,0:T(8,128)(2,1)}), bf16[2,5632,2048]{2,1,0:T(8,128)(2,1)}) %all-gather.24.cloned.1.call-update) | async-done | bytes 46137360 | tf_op jit(solution)/shard_map/all_gather | solution.py:144
  1796.0 35.1 fusion.188
  1878.5 37.5 fusion.11
  1921.6 37.6 fusion.10
  2261.1 35.0 convolution_convert_fusion
  2298.0 35.2 convolution_convert_fusion.1
  2380.3 47.3 reduce-scatter.54.cloned.1.call-done
  2429.0 168.3 %reduce-scatter.30.cloned.1.call-done = bf16[2,256,2048]{2,1,0:T(8,128)(2,1)} async-done(((bf16[2,2048,2048]{2,1,0:T(8,128)(2,1)}), bf16[2,256,2048]{2,1,0:T(8,128)(2,1)}) %reduce-scatter.30.cloned.1.call-update) | async-done | bytes 2097168 | tf_op jit(solution)/shard_map/reduce_scatter | solution.py:319
  2597.3 168.9 %reduce-scatter.28.cloned.1.call-done = bf16[2,256,2048]{2,1,0:T(8,128)(2,1)} async-done(((bf16[2,2048,2048]{2,1,0:T(8,128)(2,1)}), bf16[2,256,2048]{2,1,0:T(8,128)(2,1)}) %reduce-scatter.28.cloned.1.call-update) | async-done | bytes 2097168 | tf_op jit(solution)/shard_map/reduce_scatter | solution.py:319
  2771.2 163.8 %reduce-scatter.34.cloned.1.call-done = bf16[2,256,2048]{2,1,0:T(8,128)(2,1)} async-done(((bf16[2,2048,2048]{2,1,0:T(8,128)(2,1)}), bf16[2,256,2048]{2,1,0:T(8,128)(2,1)}) %reduce-scatter.34.cloned.1.call-update) | async-done | bytes 2097168 | tf_op jit(solution)/shard_map/reduce_scatter | solution.py:322
  2935.0 169.0 %reduce-scatter.32.cloned.1.call-done = bf16[2,256,2048]{2,1,0:T(8,128)(2,1)} async-done(((bf16[2,2048,2048]{2,1,0:T(8,128)(2,1)}), bf16[2,256,2048]{2,1,0:T(8,128)(2,1)}) %reduce-scatter.32.cloned.1.call-update) | async-done | bytes 2097168 | tf_op jit(solution)/shard_map/reduce_scatter | solution.py:322
  3109.0 439.3 %reduce-scatter.42.cloned.1.call-done = bf16[2,704,2048]{2,1,0:T(8,128)(2,1)} async-done(((bf16[2,5632,2048]{2,1,0:T(8,128)(2,1)}), bf16[2,704,2048]{2,1,0:T(8,128)(2,1)}) %reduce-scatter.42.cloned.1.call-update) | async-done | bytes 5767184 | tf_op jit(solution)/shard_map/reduce_scatter | solution.py:328
  3548.3 444.6 %reduce-scatter.40.cloned.1.call-done = bf16[2,704,2048]{2,1,0:T(8,128)(2,1)} async-done(((bf16[2,5632,2048]{2,1,0:T(8,128)(2,1)}), bf16[2,704,2048]{2,1,0:T(8,128)(2,1)}) %reduce-scatter.40.cloned.1.call-update) | async-done | bytes 5767184 | tf_op jit(solution)/shard_map/reduce_scatter | solution.py:328
  4004.9 865.1 %reduce-scatter.38.cloned.1.call-done = bf16[2,256,11264]{2,1,0:T(8,128)(2,1)} async-done(((bf16[2,2048,11264]{2,1,0:T(8,128)(2,1)}), bf16[2,256,11264]{2,1,0:T(8,128)(2,1)}) %reduce-scatter.38.cloned.1.call-update) | async-done | bytes 11534352 | tf_op jit(solution)/shard_map/reduce_scatter | solution.py:325
  4870.0 877.2 %reduce-scatter.36.cloned.1.call-done = bf16[2,256,11264]{2,1,0:T(8,128)(2,1)} async-done(((bf16[2,2048,11264]{2,1,0:T(8,128)(2,1)}), bf16[2,256,11264]{2,1,0:T(8,128)(2,1)}) %reduce-scatter.36.cloned.1.call-update) | async-done | bytes 11534352 | tf_op jit(solution)/shard_map/reduce_scatter | solution.py:325
  5763.6 693.2 %reduce-scatter.44.cloned.1.call-done = f32[64,4096]{1,0:T(8,128)} async-done(((f32[2048,4096]{1,0:T(8,128)}), f32[64,4096]{1,0:T(8,128)}) %reduce-scatter.44.cloned.1.call-update) | async-done | bytes 1048592 | tf_op jit(solution)/shard_map/reduce_scatter | solution.py:316
  (732 shorter events, 752.2 us)
Async XLA Ops:
  7.2 121.3 %all-gather.12.cloned.1.call-start = ((), (), s32[]{:S(2)}) async-start(), calls=%async_computation.33 | async-start | bytes 17301504 | tf_op jit(solution)/shard_map/all_gather | solution.py:138
  7.9 272.1 %all-gather.18.cloned.1.call-start = ((), (), s32[]{:S(2)}) async-start(), calls=%async_computation.36 | async-start | bytes 18874368 | tf_op jit(solution)/shard_map/all_gather | solution.py:141
  8.7 298.2 %all-gather.14.cloned.1.call-start = ((), (), s32[]{:S(2)}) async-start(), calls=%async_computation.34 | async-start | bytes 1310720 | tf_op jit(solution)/shard_map/all_gather | solution.py:169
  138.0 197.8 %all-gather.16.cloned.1.call-start = ((), (), s32[]{:S(2)}) async-start(), calls=%async_computation.35 | async-start | bytes 1310720 | tf_op jit(solution)/shard_map/all_gather | solution.py:168
  140.3 348.5 %all-gather.20.cloned.1.call-start = ((), (), s32[]{:S(2)}) async-start(), calls=%async_computation.37 | async-start | bytes 18874368 | tf_op jit(solution)/shard_map/all_gather | solution.py:142
  157.6 88.3 %all-to-all-start.1 = ((bf16[4,48,2048]{2,1,0:T(8,128)(2,1)}), bf16[4,48,2048]{2,1,0:T(8,128)(2,1)S(1)}, u32[]{:S(2)}, u32[]{:S(2)}) async-start(bf16[4,48,2048]{2,1,0:T(8,128)(2,1)} %bitcast.12), calls=%async_computation.1 | async-start | bytes 1572864 | tf_op jit(solution)/shard_map/all_to_all | solution.py:110
  526.2 828.2 %all-gather.22.cloned.1.call-start = ((), (), s32[]{:S(2)}) async-start(), calls=%async_computation.38 | async-start | bytes 103809024 | tf_op jit(solution)/shard_map/all_gather | solution.py:143
  527.0 1219.4 %all-gather.24.cloned.1.call-start = ((), (), s32[]{:S(2)}) async-start(), calls=%async_computation.39 | async-start | bytes 51904512 | tf_op jit(solution)/shard_map/all_gather | solution.py:144
  1791.6 82.8 %all-to-all-start.4 = ((bf16[4,48,2048]{2,1,0:T(8,128)(2,1)}), bf16[4,48,2048]{2,1,0:T(8,128)(2,1)}, u32[]{:S(2)}, u32[]{:S(2)}) async-start(bf16[4,48,2048]{2,1,0:T(8,128)(2,1)} %bitcast.37), calls=%async_computation.4 | async-start | bytes 1572864 | tf_op jit(solution)/shard_map/all_to_all | solution.py:125
  1999.9 133.8 %reduce-scatter.46.cloned.1.call-start = ((), (), s32[]{:S(2)}) async-start(), calls=%async_computation.51 | async-start | bytes 1310720
  2034.9 102.6 %reduce-scatter.50.cloned.1.call-start = ((), (), s32[]{:S(2)}) async-start(), calls=%async_computation.53 | async-start | bytes 1310720
  2058.3 87.7 %reduce-scatter.52.cloned.1.call-start = ((), (), s32[]{:S(2)}) async-start(), calls=%async_computation.54 | async-start | bytes 1310720
  2099.0 63.7 reduce-scatter.48.cloned.1.call-start
  2123.1 253.3 %reduce-scatter.56.cloned.1.call-start = ((), (), s32[]{:S(2)}) async-start(), calls=%async_computation.56 | async-start | bytes 1081344
  2124.8 302.8 %reduce-scatter.54.cloned.1.call-start = ((), (), s32[]{:S(2)}) async-start(), calls=%async_computation.55 | async-start | bytes 1081344
  2181.7 415.6 %reduce-scatter.30.cloned.1.call-start = ((), (), s32[]{:S(2)}) async-start(), calls=%async_computation.43 | async-start | bytes 18874368 | tf_op jit(solution)/shard_map/reduce_scatter | solution.py:319
  2190.4 575.8 %reduce-scatter.28.cloned.1.call-start = ((), (), s32[]{:S(2)}) async-start(), calls=%async_computation.42 | async-start | bytes 18874368 | tf_op jit(solution)/shard_map/reduce_scatter | solution.py:319
  2199.7 735.3 %reduce-scatter.34.cloned.1.call-start = ((), (), s32[]{:S(2)}) async-start(), calls=%async_computation.45 | async-start | bytes 18874368 | tf_op jit(solution)/shard_map/reduce_scatter | solution.py:322
  2209.3 894.6 %reduce-scatter.32.cloned.1.call-start = ((), (), s32[]{:S(2)}) async-start(), calls=%async_computation.44 | async-start | bytes 18874368 | tf_op jit(solution)/shard_map/reduce_scatter | solution.py:322
  2218.9 1329.3 %reduce-scatter.42.cloned.1.call-start = ((), (), s32[]{:S(2)}) async-start(), calls=%async_computation.49 | async-start | bytes 51904512 | tf_op jit(solution)/shard_map/reduce_scatter | solution.py:328
  2239.1 1753.8 %reduce-scatter.40.cloned.1.call-start = ((), (), s32[]{:S(2)}) async-start(), calls=%async_computation.48 | async-start | bytes 51904512 | tf_op jit(solution)/shard_map/reduce_scatter | solution.py:328
  2259.2 2610.7 %reduce-scatter.38.cloned.1.call-start = ((), (), s32[]{:S(2)}) async-start(), calls=%async_computation.47 | async-start | bytes 103809024 | tf_op jit(solution)/shard_map/reduce_scatter | solution.py:325
  2296.1 3451.0 %reduce-scatter.36.cloned.1.call-start = ((), (), s32[]{:S(2)}) async-start(), calls=%async_computation.46 | async-start | bytes 103809024 | tf_op jit(solution)/shard_map/reduce_scatter | solution.py:325
  2333.2 4123.6 %reduce-scatter.44.cloned.1.call-start = ((), (), s32[]{:S(2)}) async-start(), calls=%async_computation.50 | async-start | bytes 34603008 | tf_op jit(solution)/shard_map/reduce_scatter | solution.py:316
  (207 other events, 9015.3 us)
Sparse Core Ops, SparseCore 0:
  10.9 117.5 all-gather.11
  130.1 149.8 all-gather.17
  282.4 24.3 all-gather.13
  309.1 26.6 all-gather.15
  337.2 151.5 all-gather.19
  524.9 29.2 all-gather.25
  556.7 23.7 all-gather.27
  582.1 772.2 all-gather.21
  1356.0 390.2 all-gather.23
  2035.0 25.8 reduce-scatter.45
  2064.1 27.7 reduce-scatter.49
  2095.2 29.8 reduce-scatter.51
  2128.8 32.4 reduce-scatter.47
  2163.4 130.3 reduce-scatter.55
  2296.6 130.9 reduce-scatter.53
  2430.4 166.8 reduce-scatter.29
  2599.5 166.6 reduce-scatter.27
  2768.4 166.5 reduce-scatter.33
  2937.3 166.5 reduce-scatter.31
  3106.2 442.0 reduce-scatter.41
  3550.8 442.0 reduce-scatter.39
  3995.3 874.6 reduce-scatter.37
  4872.5 874.6 reduce-scatter.35
  5749.9 706.8 reduce-scatter.43
where the time goes:
time: 6470 us; the launch traced here: 6460 us
  waiting for transfers between devices  5460 us (84%)
  matrix products  600 us (9%)
  blocking collectives  145 us (2%)
  other arithmetic  85.4 us (1%)
  local copies, waits for them, and re-layouts  82.4 us (1%)
  starting transfers between devices  70.8 us (1%)
    reduce_scatter x2, waiting for transfers between devices, shards(): lax.psum_scatter(expert_terms[2].astype(jnp.bfloat16), 'dp', scatter_dime...  1740 us
    reduce_scatter x2, waiting for transfers between devices, shards(): lax.psum_scatter(expert_terms[3].astype(jnp.bfloat16), 'dp', scatter_dime...  884 us
    reduce_scatter x1, waiting for transfers between devices, shards(): lax.psum_scatter(shared_terms[2], ('dp', 'expert'), scatter_dimension=0,...  693 us
    all_gather x1, waiting for transfers between devices, shards(): lax.all_gather(input_weight, 'dp', axis=1, tiled=True)  680 us
    dot_general x52, matrix products, product(): jnp.einsum(pattern, operand, factor, preferred_element_type=jnp.float32)  565 us
    all_gather x1, waiting for transfers between devices, shards(): lax.all_gather(down_weight, 'dp', axis=1, tiled=True)  349 us
    reduce_scatter x2, waiting for transfers between devices, shards(): lax.psum_scatter(expert_terms[0].astype(jnp.bfloat16), 'dp', scatter_dime...  337 us
    reduce_scatter x2, waiting for transfers between devices, shards(): lax.psum_scatter(expert_terms[1].astype(jnp.bfloat16), 'dp', scatter_dime...  333 us
  transfers between devices with their start and end apart: 42, of which 31 were waited for; matrix products, arithmetic and copies ran while one was open for 10% of the time, Pallas kernels for 0%

commit v1 on v0

v1 whole, which is shorter than its diff:
```python
import functools
import jax
import jax.numpy as jnp
from jax import lax
from jax.experimental import pallas as pl
from jax.experimental.pallas import tpu as pltpu
from jax.sharding import PartitionSpec as P

MESH = pl.DeviceIdType.MESH
BF16 = jnp.bfloat16
F32 = jnp.float32


def expert_factors(owners):
    return (2, owners // 2) if owners % 2 == 0 and owners > 2 else (1, owners)


class Place:
    def __init__(self, chips, first, second):
        dp = lax.axis_index("dp")
        ex = lax.axis_index("expert")
        self.chips, self.first, self.second = chips, first, second
        self.dp, self.ex = dp, ex
        self.z, self.k = dp // 2, dp % 2
        self.a, self.b = ex // second, ex % second

    def at(self, z=None, k=None, a=None, b=None):
        z = self.z if z is None else z
        k = self.k if k is None else k
        a = self.a if a is None else a
        b = self.b if b is None else b
        return (z * 2 + k, a * self.second + b)

    def greet(self):
        barrier = pltpu.get_barrier_semaphore()

        def hello(target):
            pl.semaphore_signal(barrier, inc=1, device_id=target, device_id_type=MESH)

        hello(self.at(k=1 - self.k))
        for i in range(1, self.first):
            hello(self.at(a=(self.a + i) % self.first))
        for i in range(1, self.second):
            hello(self.at(b=(self.b + i) % self.second))
        pl.when(self.z > 0)(lambda: hello(self.at(z=self.z - 1)))
        pl.when(self.z < self.chips - 1)(lambda: hello(self.at(z=self.z + 1)))
        along = (self.z > 0).astype(jnp.int32) + (self.z < self.chips - 1).astype(jnp.int32)
        pl.semaphore_wait(barrier, self.first + self.second - 1 + along)


def gather_kernel(chips, first, second, by_row, x_ref, out_ref, own_sem, recv, sends):
    me = Place(chips, first, second)
    owners = first * second
    me.greet()

    def index(z, k, a, b):
        return (z * 2 + k) * owners + a * second + b

    def piece(blk, h):
        return out_ref.at[h, blk] if by_row else out_ref.at[blk, h]

    pending = []

    def push(src, blk, h, target, when=None):
        copy = pltpu.make_async_remote_copy(
            src_ref=src,
            dst_ref=piece(blk, h),
            send_sem=sends.at[len(pending)],
            recv_sem=recv.at[blk, h],
            device_id=target,
            device_id_type=MESH,
        )
        pending.append((copy, when))
        copy.start() if when is None else pl.when(when)(copy.start)

    def landed(blk, h, when=None):
        copy = pltpu.make_async_remote_copy(
            src_ref=piece(blk, h),
            dst_ref=piece(blk, h),
            send_sem=sends.at[0],
            recv_sem=recv.at[blk, h],
            device_id=me.at(),
            device_id_type=MESH,
        )
        copy.wait_recv() if when is None else pl.when(when)(copy.wait_recv)

    own = index(me.z, me.k, me.a, me.b)
    stays = [pltpu.make_async_copy(x_ref.at[h], piece(own, h), own_sem.at[h]) for h in range(2)]
    for stay in stays:
        stay.start()

    def spread(z, blk, source, when=None):
        for h in range(2):
            for i in range(1, second):
                push(source(h), blk, h, me.at(b=(me.b + i) % second), when)
            for i in range(1, first):
                push(source(h), blk, h, me.at(a=(me.a + i) % first), when)
        for h in range(2):
            push(source(h), blk, h, me.at(k=1 - me.k), when)

    def relay(z, when=None):
        for h in range(2):
            if h == 0:
                froms = [(me.a, (me.b + i) % second) for i in range(1, second)]
                onward = [dict(a=(me.a + i) % first) for i in range(1, first)]
            else:
                froms = [((me.a + i) % first, me.b) for i in range(1, first)]
                onward = [dict(b=(me.b + i) % second) for i in range(1, second)]
            for a, b in froms:
                blk = index(z, me.k, a, b)
                landed(blk, h, when)
                for target in onward:
                    push(piece(blk, h), blk, h, me.at(**target), when)
                push(piece(blk, h), blk, h, me.at(k=1 - me.k), when)

    def finish(z, when=None):
        for h in range(2):
            for i in range(1, second if h else first):
                if h == 0:
                    a, bs = (me.a + i) % first, [(me.b + j) % second for j in range(second)]
                    spots = [(a, b) for b in bs]
                else:
                    b = (me.b + i) % second
                    spots = [((me.a + j) % first, b) for j in range(first)]
                for a, b in spots:
                    blk = index(z, me.k, a, b)
                    landed(blk, h, when)
                    push(piece(blk, h), blk, h, me.at(k=1 - me.k), when)

    def own_half(h):
        return x_ref.at[h]

    for h in range(2):
        push(own_half(h), own, h, me.at(z=me.z + 1), me.z < chips - 1)
        push(own_half(h), own, h, me.at(z=me.z - 1), me.z > 0)
    spread(me.z, own, own_half)
    queue = [(me.z, None)]
    for t in range(1, chips):
        fresh = []
        for sign in (-1, 1):
            z = me.z + sign * t
            there = (z >= 0) if sign < 0 else (z < chips)
            blk = index(z, me.k, me.a, me.b)
            further = (me.z < chips - 1) if sign < 0 else (me.z > 0)
            for h in range(2):
                landed(blk, h, there)
                push(piece(blk, h), blk, h, me.at(z=me.z - sign), there & further)
            spread(z, blk, lambda h, blk=blk: piece(blk, h), there)
            fresh.append((z, there))
        for z, there in queue:
            relay(z, there)
        for z, there in queue:
            finish(z, there)
        queue = fresh
    for z, there in queue:
        relay(z, there)
    for z, there in queue:
        finish(z, there)
    for stay in stays:
        stay.wait()
    for z in range(chips):
        for e in range(owners):
            for h in range(2):
                landed((z * 2 + 1 - me.k) * owners + e, h)
    for copy, when in pending:
        copy.wait_send() if when is None else pl.when(when)(copy.wait_send)


def gather_all(x, chips, owners, by_row, collective_id):
    first, second = expert_factors(owners)
    _, rows, width = x.shape
    blocks = chips * 2 * owners
    sends = 4 + (2 * chips - 1) * (
        2 + 2 * (first + second - 1) + 2 * (second - 1) * first + 2 * (first - 1) * second
    )
    shape = (2, blocks, rows, width) if by_row else (blocks, 2, rows, width)
    return pl.pallas_call(
        functools.partial(gather_kernel, chips, first, second, by_row),
        out_shape=jax.ShapeDtypeStruct(shape, x.dtype),
        in_specs=[pl.BlockSpec(memory_space=pl.ANY)],
        out_specs=pl.BlockSpec(memory_space=pl.ANY),
        scratch_shapes=[
            pltpu.SemaphoreType.DMA((2,)),
            pltpu.SemaphoreType.DMA((blocks, 2)),
            pltpu.SemaphoreType.DMA((sends,)),
        ],
        compiler_params=pltpu.CompilerParams(collective_id=collective_id, has_side_effects=True),
    )(x)


def scatter_kernel(
    chips, first, second, by_row, column, width, p_ref, out_ref,
    mine, fromk, a0, b0, b1, a1, fromz, total, load_sem, ks, a0s, b0s, b1s, a1s, zs, sends,
):
    me = Place(chips, first, second)
    owners = first * second
    me.greet()
    pending = []

    def push(src, dst, sem, target, when=None):
        copy = pltpu.make_async_remote_copy(
            src_ref=src, dst_ref=dst, send_sem=sends.at[len(pending)], recv_sem=sem,
            device_id=target, device_id_type=MESH,
        )
        pending.append((copy, when))
        copy.start() if when is None else pl.when(when)(copy.start)

    def landed(dst, sem):
        pltpu.make_async_remote_copy(
            src_ref=dst, dst_ref=dst, send_sem=sends.at[0], recv_sem=sem,
            device_id=me.at(), device_id_type=MESH,
        ).wait_recv()

    low = me.z < chips // 2

    def line(t):
        return jnp.where(
            low,
            jnp.where(t < chips - 1 - me.z, chips - 1 - t, t - (chips - 1 - me.z)),
            jnp.where(t < me.z, t, chips - 1 - (t - me.z)),
        )

    cut = pl.ds(column, width)

    def block(z, k, e):
        blk = (z * 2 + k) * owners + e
        return p_ref.at[:, blk, :, cut] if by_row else p_ref.at[blk, :, :, cut]

    loads = {}
    for t in range(chips):
        z = line(t)
        for e in range(owners):
            load = pltpu.make_async_copy(
                block(z, me.k, e), mine.at[t, e], load_sem.at[t, e]
            )
            load.start()
            loads[t, e] = load
            push(
                block(z, 1 - me.k, e),
                fromk.at[t, e], ks.at[t, e], me.at(k=1 - me.k),
            )

    def add(*terms):
        value = terms[0].astype(F32)
        for term in terms[1:]:
            value = value + term.astype(F32)
        return value

    def step_one(t):
        for i in range(first):
            for j in range(second):
                a, b = (me.a + 1 + i) % first, (me.b + 1 + j) % second
                e = a * second + b
                loads_sem = load_sem.at[t, e]
                pltpu.make_async_copy(mine.at[t, e], mine.at[t, e], loads_sem).wait()
                landed(fromk.at[t, e], ks.at[t, e])
                mine[t, e] = add(mine[t, e], fromk[t, e]).astype(BF16)
                if i < first - 1:
                    push(
                        mine.at[t, e, 0], a0.at[t, first - 2 - i, b],
                        a0s.at[t, first - 2 - i, b], me.at(a=a),
                    )
                if j < second - 1:
                    push(
                        mine.at[t, e, 1], b1.at[t, second - 2 - j, a],
                        b1s.at[t, second - 2 - j, a], me.at(b=b),
                    )

    def step_two(t):
        for j in range(second - 1):
            b = (me.b + 1 + j) % second
            e = me.a * second + b
            for i in range(first - 1):
                landed(a0.at[t, i, b], a0s.at[t, i, b])
            mine[t, e, 0] = add(
                mine[t, e, 0], *[a0[t, i, b] for i in range(first - 1)]
            ).astype(BF16)
            push(
                mine.at[t, e, 0], b0.at[t, second - 2 - j],
                b0s.at[t, second - 2 - j], me.at(b=b),
            )
        for i in range(first - 1):
            a = (me.a + 1 + i) % first
            e = a * second + me.b
            for j in range(second - 1):
                landed(b1.at[t, j, a], b1s.at[t, j, a])
            mine[t, e, 1] = add(
                mine[t, e, 1], *[b1[t, j, a] for j in range(second - 1)]
            ).astype(BF16)
            push(
                mine.at[t, e, 1], a1.at[t, first - 2 - i],
                a1s.at[t, first - 2 - i], me.at(a=a),
            )

    def step_three(t):
        z = line(t)
        e = me.ex
        for i in range(first - 1):
            landed(a0.at[t, i, me.b], a0s.at[t, i, me.b])
            landed(a1.at[t, i], a1s.at[t, i])
        for j in range(second - 1):
            landed(b1.at[t, j, me.a], b1s.at[t, j, me.a])
            landed(b0.at[t, j], b0s.at[t, j])
        total[t, 0] = add(
            mine[t, e, 0], *[a0[t, i, me.b] for i in range(first - 1)],
            *[b0[t, j] for j in range(second - 1)],
        )
        total[t, 1] = add(
            mine[t, e, 1], *[b1[t, j, me.a] for j in range(second - 1)],
            *[a1[t, i] for i in range(first - 1)],
        )
        if t < chips - 1:
            up = z > me.z
            from_beyond = jnp.where(up, me.z > 0, me.z < chips - 1)

            @pl.when(from_beyond)
            def _():
                landed(fromz.at[z], zs.at[z])
                total[t] = total[t] + fromz[z].astype(F32)

            mine[t, e] = total[t].astype(BF16)
            push(mine.at[t, e], fromz.at[z], zs.at[z], me.at(z=me.z + 1), up)
            slot = jnp.where(z == me.z - 1, chips, z)
            push(mine.at[t, e], fromz.at[slot], zs.at[slot], me.at(z=me.z - 1), jnp.logical_not(up))
        else:

            @pl.when(me.z > 0)
            def _():
                landed(fromz.at[me.z], zs.at[me.z])
                total[t] = total[t] + fromz[me.z].astype(F32)

            @pl.when(me.z < chips - 1)
            def _():
                landed(fromz.at[chips], zs.at[chips])
                total[t] = total[t] + fromz[chips].astype(F32)

            out_ref[...] = total[t]

    for t in range(chips + 2):
        if t < chips:
            step_one(t)
        if 0 <= t - 1 < chips:
            step_two(t - 1)
        if 0 <= t - 2 < chips:
            step_three(t - 2)
    for copy, when in pending:
        copy.wait_send() if when is None else pl.when(when)(copy.wait_send)


def scatter_sum(p, chips, owners, by_row, collective_id):
    first, second = expert_factors(owners)
    half, full = p.shape[2:]
    parts = 1
    while chips * owners * half * (full // parts) * 8 > 20 * 2**20:
        parts *= 2
    width = full // parts
    one = max(first - 1, 1), max(second - 1, 1)
    sends = chips * (owners + 2 + 2 * (first - 1) * second + 2 * (second - 1) * first)
    sends += chips * (first + second)

    def call(part):
        sem = pltpu.SemaphoreType.DMA
        return pl.pallas_call(
            functools.partial(scatter_kernel, chips, first, second, by_row, part * width, width),
            out_shape=jax.ShapeDtypeStruct((2, half, width), F32),
            in_specs=[pl.BlockSpec(memory_space=pl.ANY)],
            out_specs=pl.BlockSpec(memory_space=pltpu.VMEM),
            scratch_shapes=[
                pltpu.VMEM((chips, owners, 2, half, width), BF16),
                pltpu.VMEM((chips, owners, 2, half, width), BF16),
                pltpu.VMEM((chips, one[0], second, half, width), BF16),
                pltpu.VMEM((chips, one[1], half, width), BF16),
                pltpu.VMEM((chips, one[1], first, half, width), BF16),
                pltpu.VMEM((chips, one[0], half, width), BF16),
                pltpu.VMEM((chips + 1, 2, half, width), BF16),
                pltpu.VMEM((chips, 2, half, width), F32),
                sem((chips, owners)),
                sem((chips, owners)),
                sem((chips, one[0], second)),
                sem((chips, one[1])),
                sem((chips, one[1], first)),
                sem((chips, one[0])),
                sem((chips + 1,)),
                sem((sends,)),
            ],
            compiler_params=pltpu.CompilerParams(
                collective_id=collective_id + part, has_side_effects=True,
                vmem_limit_bytes=60 * 2**20,
            ),
        )(p)

    parts_out = [call(part) for part in range(parts)]
    return parts_out[0] if parts == 1 else jnp.concatenate(parts_out, axis=-1)


def exchange_kernel(devices, owners, same, x_ref, out_ref, own_sem, recv, sends):
    dp = lax.axis_index("dp")
    ex = lax.axis_index("expert")
    me = dp * owners + ex
    barrier = pltpu.get_barrier_semaphore()

    def target(i):
        other = (me + i) % devices
        return other, (other // owners, other % owners)

    def hello(i, _):
        pl.semaphore_signal(barrier, inc=1, device_id=target(i)[1], device_id_type=MESH)
        return 0

    lax.fori_loop(1, devices, hello, 0)
    stay = pltpu.make_async_copy(x_ref.at[0 if same else me], out_ref.at[me], own_sem)
    stay.start()
    pl.semaphore_wait(barrier, devices - 1)

    def copy(i):
        other, where = target(i)
        return pltpu.make_async_remote_copy(
            src_ref=x_ref.at[0 if same else other], dst_ref=out_ref.at[me],
            send_sem=sends.at[i], recv_sem=recv.at[me], device_id=where, device_id_type=MESH,
        )

    def send(i, _):
        copy(i).start()
        return 0

    def landed(i, _):
        other, where = target(i)
        pltpu.make_async_remote_copy(
            src_ref=out_ref.at[other], dst_ref=out_ref.at[other], send_sem=sends.at[i],
            recv_sem=recv.at[other], device_id=where, device_id_type=MESH,
        ).wait_recv()
        copy(i).wait_send()
        return 0

    lax.fori_loop(1, devices, send, 0)
    lax.fori_loop(1, devices, landed, 0)
    stay.wait()


def exchange(x, devices, owners, collective_id):
    same = x.shape[0] == 1
    return pl.pallas_call(
        functools.partial(exchange_kernel, devices, owners, same),
        out_shape=jax.ShapeDtypeStruct((devices,) + x.shape[1:], x.dtype),
        in_specs=[pl.BlockSpec(memory_space=pl.ANY)],
        out_specs=pl.BlockSpec(memory_space=pl.ANY),
        scratch_shapes=[
            pltpu.SemaphoreType.DMA,
            pltpu.SemaphoreType.DMA((devices,)),
            pltpu.SemaphoreType.DMA((devices,)),
        ],
        compiler_params=pltpu.CompilerParams(collective_id=collective_id, has_side_effects=True),
    )(x)


D = 2048
KVH = 16
HD = 128
FF = 5632
NEXP = 8
TOK_MB = 64
CAP = 24
LANES = 128
EPSILON = 1e-06


def product(pattern, operand, factor):
    return jnp.einsum(pattern, operand, factor, preferred_element_type=F32)


def turn(values, cosine, sine):
    shaped = values.reshape(values.shape[:-1] + (-1, 2, HD // 2))
    former, latter = shaped[..., 0, :], shaped[..., 1, :]
    cosine, sine = cosine[..., None, :], sine[..., None, :]
    turned = jnp.stack([former * cosine - latter * sine, latter * cosine + former * sine], axis=-2)
    return turned.reshape(values.shape)


def angles_of(places):
    frequency = 10000.0 ** (-(jnp.arange(HD // 2, dtype=F32) * (2.0 / HD)))
    angles = places.astype(F32)[..., None] * frequency
    return jnp.cos(angles), jnp.sin(angles)


def norm_forward(values, norm_gain):
    inverse = lax.rsqrt(jnp.mean(values * values, axis=-1, keepdims=True) + EPSILON)
    return (values * inverse * norm_gain, inverse)


def norm_backward(values, inverse, norm_gain, grad_normed):
    scaled = grad_normed * norm_gain
    grad_gain = jnp.sum(grad_normed * values * inverse, axis=(0, 1))
    grad_values = inverse * scaled - values * inverse**3 * jnp.mean(
        scaled * values, axis=-1, keepdims=True
    )
    return (grad_values, grad_gain)


def choices(routes):
    return (routes[..., None] == jnp.arange(NEXP, dtype=jnp.int32)).astype(F32)


def gate_values(logits, choose):
    picked = jnp.sum(choose * logits[..., None, :], axis=-1)
    highest = jnp.max(picked, axis=-1, keepdims=True)
    exponent = jnp.exp(picked - highest)
    return exponent / jnp.sum(exponent, axis=-1, keepdims=True)


def gate_grads(gate_probs, grad_gate_probs, choose):
    weighted = jnp.sum(gate_probs * grad_gate_probs, axis=-1, keepdims=True)
    grad_picked = gate_probs * (grad_gate_probs - weighted)
    return jnp.sum(grad_picked[..., None] * choose, axis=-2)


def seats(routes, first_expert, local_count, groups):
    experts = first_expert + jnp.arange(local_count, dtype=jnp.int32)
    hit = jnp.any(routes[:, :, :, None] == experts, axis=2).astype(jnp.int32)
    rank = jnp.cumsum(hit, axis=1) - hit
    blocks = routes.shape[0]
    per = blocks // groups
    hit = hit.reshape(groups, per, TOK_MB, local_count)
    seat = rank.reshape(hit.shape) + (jnp.arange(per, dtype=jnp.int32) * CAP)[:, None, None]
    seat = jnp.where(hit > 0, seat, -1).reshape(groups, per * TOK_MB, local_count)
    seat = jnp.swapaxes(seat, 1, 2)
    return seat[:, :, None, :] == jnp.arange(per * CAP, dtype=jnp.int32)[:, None]


def tile_starts(shards):
    share = FF // shards
    most = max(share * d % LANES for d in range(shards))
    tiles = -(-(share + most) // LANES)
    starts = [min(share * d // LANES, FF // LANES - tiles) for d in range(shards)]
    return tiles, starts, [share * d - LANES * starts[d] for d in range(shards)]


def shards(
    tokens, lengths, attention_routes, feedforward_routes, norm_gains, router_weight,
    key_value_weight, query_weight, output_weight, input_weight, down_weight, cotangent,
):
    n_dp = lax.axis_size("dp")
    owners = lax.axis_size("expert")
    chips = n_dp // 2
    devices = n_dp * owners
    dp = lax.axis_index("dp")
    ex = lax.axis_index("expert")
    me = dp * owners + ex
    mb = tokens.shape[0]
    local_count = NEXP // owners
    seqs = mb * n_dp
    row_length = owners * TOK_MB
    heads = KVH // n_dp
    hc = heads * HD
    att = KVH * HD
    depth = D // n_dp
    slice_rows = D // devices
    tiles, starts, offsets = tile_starts(n_dp)
    share, wide = FF // n_dp, tiles * LANES
    offset = jnp.array(offsets, jnp.int32)[dp]
    scaling = HD ** (-0.5)

    query_parts = jnp.transpose(
        query_weight.reshape(local_count, depth, n_dp, hc), (2, 0, 1, 3)
    )
    query_full = lax.all_to_all(query_parts, "dp", 0, 0, tiled=True)
    query_full = jnp.swapaxes(query_full, 0, 1).reshape(local_count, D, hc)
    key_value_parts = jnp.transpose(
        key_value_weight.reshape(slice_rows, 2, n_dp, hc), (2, 0, 1, 3)
    )
    key_value_full = lax.all_to_all(key_value_parts, "dp", 0, 0, tiled=True)
    key_value_full = lax.all_gather(
        key_value_full.reshape(n_dp, slice_rows, 2 * hc), "expert", axis=1
    ).reshape(D, 2 * hc)
    input_parts = jnp.stack(
        [
            jnp.stack(
                [
                    lax.slice_in_dim(input_weight, g * FF + LANES * s, g * FF + LANES * s + wide, axis=2)
                    for g in range(2)
                ]
            )
            for s in starts
        ]
    )
    input_full = lax.all_to_all(input_parts, "dp", 0, 0, tiled=True)
    input_full = jnp.transpose(input_full, (2, 1, 0, 3, 4)).reshape(local_count, 2, D, wide)
    gate_full, up_full = input_full[:, 0], input_full[:, 1]
    down_full = lax.dynamic_update_slice(
        jnp.zeros((local_count, wide, D), BF16), down_weight, (0, offset, 0)
    )

    shared = jnp.concatenate([norm_gains, router_weight], axis=1).astype(F32)
    small = jnp.concatenate(
        [
            attention_routes.reshape(-1).astype(F32),
            feedforward_routes.reshape(-1).astype(F32),
            shared.reshape(-1),
            lengths.reshape(-1).astype(F32),
        ]
    )
    count = small.shape[0]
    small = jnp.pad(small, (0, -count % (8 * LANES))).reshape(1, -1, LANES)
    small = exchange(small, devices, owners, 1).reshape(devices, -1)
    route_count = mb * TOK_MB * 2
    routes_all = small[:, : 2 * route_count].astype(jnp.int32)
    mixer_routes = routes_all[:, :route_count].reshape(n_dp, owners, mb, TOK_MB, 2)
    mixer_routes = jnp.transpose(mixer_routes, (2, 0, 1, 3, 4)).reshape(-1, TOK_MB, 2)
    feed_routes = routes_all[:, route_count:].reshape(-1, TOK_MB, 2)
    shared_all = small[:, 2 * route_count : 2 * route_count + slice_rows * 18].reshape(D, 18)
    gain_mixer, gain_feed = shared_all[:, 0], shared_all[:, 1]
    router_mixer = shared_all[:, 2 : 2 + NEXP]
    router_feed = shared_all[:, 2 + NEXP :]
    lengths_all = small[:, count - mb : count].astype(jnp.int32)
    row_lengths = lengths_all.reshape(n_dp, owners, mb)[:, 0].T.reshape(seqs)

    own_tokens = tokens[:, 0].astype(F32)
    home_places = ex * TOK_MB + jnp.arange(TOK_MB, dtype=jnp.int32)
    own_valid = (home_places[None, :] < lengths[:, :1]).astype(F32)
    own_cotangent = cotangent[:, 0].astype(F32) * own_valid[..., None]

    normed_mixer, inverse_mixer = norm_forward(own_tokens, gain_mixer)
    normed_mixer = normed_mixer.astype(BF16)
    mixer_all = gather_all(normed_mixer, chips, owners, True, 2).reshape(seqs, row_length, D)
    onehot_mixer = seats(mixer_routes, ex * local_count, local_count, seqs)
    seat_places = jnp.sum(
        jnp.where(onehot_mixer, jnp.arange(row_length, dtype=jnp.int32), 0), axis=-1
    )
    choose_mixer = choices(mixer_routes.reshape(seqs, row_length, 2))
    logits_mixer = product("std,de->ste", mixer_all, router_mixer.astype(BF16))
    gates_mixer = gate_values(logits_mixer, choose_mixer)
    experts_here = ex * local_count + jnp.arange(local_count, dtype=jnp.int32)
    here_mixer = mixer_routes.reshape(seqs, row_length, 2)[..., None] == experts_here
    slot_gates_mixer = jnp.sum(jnp.where(here_mixer, gates_mixer[..., None], 0.0), axis=2)
    seat_gates_mixer = jnp.sum(
        jnp.where(onehot_mixer, jnp.swapaxes(slot_gates_mixer, 1, 2)[:, :, None, :], 0.0), axis=-1
    )
    onehot_mixer_low = onehot_mixer.astype(BF16)

    key_places = jnp.arange(row_length, dtype=jnp.int32)
    key_cos, key_sin = angles_of(key_places)
    key_value = product("std,dc->stc", mixer_all, key_value_full)
    keys = turn(key_value[..., :hc], key_cos, key_sin).astype(BF16)
    values = key_value[..., hc:].astype(BF16)
    rows_mixer = product("slrt,std->lsrd", onehot_mixer_low, mixer_all).astype(BF16)
    seat_cos, seat_sin = angles_of(jnp.swapaxes(seat_places, 0, 1))
    queries = product("lsrd,ldc->lsrc", rows_mixer, query_full)
    queries = (turn(queries, seat_cos, seat_sin) * scaling).astype(BF16)
    query_heads = queries.reshape(local_count, seqs, -1, heads, HD)
    key_heads = keys.reshape(seqs, row_length, heads, HD)
    value_heads = values.reshape(seqs, row_length, heads, HD)
    allowed = (key_places <= seat_places[..., None]) & (
        key_places < row_lengths[:, None, None, None]
    )
    allowed = jnp.swapaxes(allowed, 0, 1)[:, :, None]
    scores = product("lsrhd,skhd->lshrk", query_heads, key_heads)
    scores = jnp.where(allowed, scores, -1e30)
    highest = jnp.max(scores, axis=-1, keepdims=True)
    exponent = jnp.exp(scores - highest)
    attn_probs = exponent / jnp.sum(exponent, axis=-1, keepdims=True)
    attn_low = attn_probs.astype(BF16)
    mixture = product("lshrk,skhd->lsrhd", attn_low, value_heads).reshape(queries.shape)
    seat_gates_mixer = jnp.swapaxes(seat_gates_mixer, 0, 1)[..., None]
    mixture_gated = (mixture * seat_gates_mixer).astype(BF16)
    mixer_rows = product("lsrc,lcd->lsrd", mixture_gated, output_weight).astype(BF16)
    mixer_part = product("slrt,lsrd->std", onehot_mixer_low, mixer_rows).astype(BF16)
    mixer_sum = scatter_sum(
        mixer_part.reshape(mb, devices, TOK_MB, D), chips, owners, True, 10
    )

    second = own_tokens + mixer_sum
    normed_feed, inverse_feed = norm_forward(second, gain_feed)
    normed_feed = normed_feed.astype(BF16)
    groups = seqs
    feed_all = gather_all(normed_feed, chips, owners, False, 3).reshape(groups, -1, D)
    cot_all = lax.all_gather(
        own_cotangent.astype(BF16), ("dp", "expert"), axis=0
    ).reshape(groups, -1, D)
    group_size = feed_all.shape[1]
    onehot_feed = seats(feed_routes, ex * local_count, local_count, groups)
    grouped_routes = feed_routes.reshape(groups, group_size, 2)
    choose_feed = choices(grouped_routes)
    logits_feed = product("std,de->ste", feed_all, router_feed.astype(BF16))
    gates_feed = gate_values(logits_feed, choose_feed)
    here_feed = grouped_routes[..., None] == experts_here
    slot_gates_feed = jnp.sum(jnp.where(here_feed, gates_feed[..., None], 0.0), axis=2)
    seat_gates_feed = jnp.sum(
        jnp.where(onehot_feed, jnp.swapaxes(slot_gates_feed, 1, 2)[:, :, None, :], 0.0), axis=-1
    )
    seat_gates_feed = jnp.swapaxes(seat_gates_feed, 0, 1)[..., None]
    onehot_feed_low = onehot_feed.astype(BF16)
    rows_feed = product("slrt,std->lsrd", onehot_feed_low, feed_all).astype(BF16)
    cot_rows = product("slrt,std->lsrd", onehot_feed_low, cot_all).astype(BF16)
    gate_part = product("lsrd,ldf->lsrf", rows_feed, gate_full)
    up_part = product("lsrd,ldf->lsrf", rows_feed, up_full)
    sigmoid = jax.nn.sigmoid(gate_part)
    silu = gate_part * sigmoid
    active = silu * up_part
    active_gated = (active * seat_gates_feed).astype(BF16)
    feed_rows = product("lsrf,lfd->lsrd", active_gated, down_full).astype(BF16)
    feed_part = product("slrt,lsrd->std", onehot_feed_low, feed_rows).astype(BF16)
    grad_plain = product("lsrd,lfd->lsrf", cot_rows, down_full)
    gate_terms_feed = jnp.sum(active * grad_plain, axis=-1)
    grad_active = grad_plain * seat_gates_feed
    grad_gate = (grad_active * up_part * sigmoid * (1.0 + gate_part * (1.0 - sigmoid))).astype(BF16)
    grad_up = (grad_active * silu).astype(BF16)
    grad_gate_w = product("lsrd,lsrf->ldf", rows_feed, grad_gate).astype(BF16)
    grad_up_w = product("lsrd,lsrf->ldf", rows_feed, grad_up).astype(BF16)
    grad_input_parts = jnp.stack([grad_gate_w, grad_up_w], axis=1).reshape(
        local_count, 2, n_dp, depth, wide
    )
    grad_input_parts = jnp.transpose(grad_input_parts, (2, 0, 1, 3, 4))
    grad_input_parts = lax.all_to_all(grad_input_parts, "dp", 0, 0, tiled=True)
    grad_rows_feed = (
        product("lsrf,ldf->lsrd", grad_gate, gate_full) + product("lsrf,ldf->lsrd", grad_up, up_full)
    ).astype(BF16)
    grad_feed_part = product("slrt,lsrd->std", onehot_feed_low, grad_rows_feed).astype(BF16)
    grad_down = product("lsrf,lsrd->lfd", active_gated, cot_rows)
    grad_down = lax.dynamic_slice_in_dim(grad_down, offset, share, axis=1)

    def gate_home(terms, onehot, here, by_row, collective_id):
        slot = jnp.sum(
            jnp.where(onehot, jnp.swapaxes(terms, 0, 1)[..., None], 0.0), axis=2
        )
        slot = jnp.sum(jnp.where(here, jnp.swapaxes(slot, 1, 2)[:, :, None, :], 0.0), axis=-1)
        if by_row:
            slot = jnp.swapaxes(slot.reshape(mb, devices, TOK_MB, 2), 0, 1)
        slot = slot.reshape(devices, -1, LANES)
        slot = jnp.pad(slot, ((0, 0), (0, -slot.shape[1] % 8), (0, 0)))
        slot = jnp.sum(exchange(slot, devices, owners, collective_id), axis=0)
        return slot.reshape(-1)[: mb * TOK_MB * 2].reshape(mb, TOK_MB, 2)

    def own_of(by_group, by_row):
        if by_row:
            return lax.dynamic_index_in_dim(
                by_group.reshape((mb, devices, TOK_MB) + by_group.shape[2:]), me, 1, keepdims=False
            )
        return lax.dynamic_index_in_dim(
            by_group.reshape((devices, mb, TOK_MB) + by_group.shape[2:]), me, 0, keepdims=False
        )

    grad_normed_feed = scatter_sum(
        grad_feed_part.reshape(devices, mb, TOK_MB, D), chips, owners, False, 20
    )
    grad_gates_feed = gate_home(gate_terms_feed, onehot_feed, here_feed, False, 4)
    grad_logits_feed = gate_grads(
        own_of(gates_feed, False), grad_gates_feed, own_of(choose_feed, False)
    )
    grad_normed_feed = grad_normed_feed + product(
        "mte,de->mtd", grad_logits_feed, router_feed
    )
    grad_second, grad_gain_feed = norm_backward(second, inverse_feed, gain_feed, grad_normed_feed)
    grad_second = grad_second + own_cotangent

    grad_all = gather_all(grad_second.astype(BF16), chips, owners, True, 5).reshape(
        seqs, row_length, D
    )
    feed_sum = scatter_sum(feed_part.reshape(devices, mb, TOK_MB, D), chips, owners, False, 30)
    result = (second + feed_sum).astype(BF16)[:, None]
    grad_rows = product("slrt,std->lsrd", onehot_mixer_low, grad_all).astype(BF16)
    grad_mixture = product("lsrd,lcd->lsrc", grad_rows, output_weight)
    gate_terms_mixer = jnp.sum(grad_mixture * mixture, axis=-1)
    grad_output = product("lsrc,lsrd->lcd", mixture_gated, grad_rows)
    grad_mixture_heads = (
        (grad_mixture * seat_gates_mixer).astype(BF16).reshape(query_heads.shape)
    )
    grad_probs = product("lsrhd,skhd->lshrk", grad_mixture_heads, value_heads)
    grad_values = product("lshrk,lsrhd->skhd", attn_low, grad_mixture_heads)
    row_dot = jnp.sum(attn_probs * grad_probs, axis=-1, keepdims=True)
    grad_scores = (attn_probs * (grad_probs - row_dot)).astype(BF16)
    grad_queries = product("lshrk,skhd->lsrhd", grad_scores, key_heads).reshape(queries.shape)
    grad_keys = product("lshrk,lsrhd->skhd", grad_scores, query_heads)
    grad_query_pre = (turn(grad_queries, seat_cos, -seat_sin) * scaling).astype(BF16)
    grad_key_value = jnp.concatenate(
        [
            turn(grad_keys.reshape(seqs, row_length, hc), key_cos, -key_sin),
            grad_values.reshape(seqs, row_length, hc),
        ],
        axis=-1,
    ).astype(BF16)
    grad_query = product("lsrd,lsrc->ldc", rows_mixer, grad_query_pre).astype(BF16)
    grad_query = jnp.swapaxes(grad_query.reshape(local_count, n_dp, depth, hc), 0, 1)
    grad_query = lax.all_to_all(grad_query, "dp", 0, 0, tiled=True)
    grad_rows_mixer = product("lsrc,ldc->lsrd", grad_query_pre, query_full).astype(BF16)
    grad_mixer_part = (
        product("slrt,lsrd->std", onehot_mixer_low, grad_rows_mixer)
        + product("stc,dc->std", grad_key_value, key_value_full)
    ).astype(BF16)
    grad_key_value_w = product("std,stc->dc", mixer_all, grad_key_value).astype(BF16)
    grad_normed_mixer = scatter_sum(
        grad_mixer_part.reshape(mb, devices, TOK_MB, D), chips, owners, True, 40
    )
    grad_key_value_w = exchange(
        grad_key_value_w.reshape(devices, slice_rows, 2 * hc), devices, owners, 6
    )
    grad_key_value_w = jnp.sum(
        grad_key_value_w.astype(F32).reshape(n_dp, owners, slice_rows, 2, hc), axis=1
    )
    grad_key_value_w = jnp.transpose(grad_key_value_w, (1, 2, 0, 3)).reshape(slice_rows, 2 * att)
    grad_gates_mixer = gate_home(gate_terms_mixer, onehot_mixer, here_mixer, True, 7)
    grad_logits_mixer = gate_grads(
        own_of(gates_mixer, True), grad_gates_mixer, own_of(choose_mixer, True)
    )
    grad_normed_mixer = grad_normed_mixer + product(
        "mte,de->mtd", grad_logits_mixer, router_mixer
    )
    grad_tokens, grad_gain_mixer = norm_backward(
        own_tokens, inverse_mixer, gain_mixer, grad_normed_mixer
    )
    grad_tokens = (grad_tokens + grad_second).astype(BF16)[:, None]

    gains = jnp.stack([grad_gain_mixer, grad_gain_feed], axis=1).reshape(devices, slice_rows * 2)
    logits = jnp.concatenate(
        [grad_logits_mixer.reshape(-1), grad_logits_feed.reshape(-1)]
    )
    last = jnp.concatenate(
        [gains, jnp.broadcast_to(logits, (devices,) + logits.shape)], axis=1
    )
    last = jnp.pad(last, ((0, 0), (0, -last.shape[1] % (8 * LANES)))).reshape(devices, -1, LANES)
    last = exchange(last, devices, owners, 8).reshape(devices, -1)
    grad_gains = jnp.sum(last[:, : slice_rows * 2], axis=0).reshape(slice_rows, 2)
    logits = last[:, slice_rows * 2 : slice_rows * 2 + 2 * mb * TOK_MB * NEXP].astype(BF16)
    logits = logits.reshape(devices, 2, mb * TOK_MB, NEXP)
    logits_m = jnp.swapaxes(
        logits[:, 0].reshape(devices, mb, TOK_MB, NEXP), 0, 1
    ).reshape(seqs, row_length, NEXP)
    router_m = product("std,ste->de", mixer_all, logits_m)
    router_f = product(
        "std,ste->de", feed_all, logits[:, 1].reshape(groups, group_size, NEXP)
    )
    grad_router = lax.dynamic_slice_in_dim(
        jnp.concatenate([router_m, router_f], axis=1), me * slice_rows, slice_rows, axis=0
    )

    grad_query = jnp.transpose(grad_query.astype(F32), (1, 2, 0, 3)).reshape(
        local_count, depth, att
    )
    pieces = []
    for g in range(2):
        edges = sorted(set(starts) | {s + tiles for s in starts})
        for low, high in zip(edges[:-1], edges[1:]):
            cover = [d for d in range(n_dp) if starts[d] <= low and high <= starts[d] + tiles]
            terms = [
                grad_input_parts[
                    d, :, g, :, (low - starts[d]) * LANES : (high - starts[d]) * LANES
                ].astype(F32)
                for d in cover
            ]
            pieces.append(functools.reduce(jnp.add, terms))
    grad_input = jnp.concatenate(pieces, axis=-1)
    return (
        result, grad_tokens, grad_gains, grad_router, grad_key_value_w, grad_query,
        grad_output, grad_input, grad_down,
    )


def solution(mesh):
    shared = P(("dp", "expert"), None)
    slots = P(None, "dp", "expert", None)
    owned = P("expert", "dp", None)
    return jax.shard_map(
        shards,
        mesh=mesh,
        in_specs=(slots, P(None, "dp"), slots, slots, shared, shared, shared) + (owned,) * 4 + (slots,),
        out_specs=(slots, slots, shared, shared, shared) + (owned,) * 4,
        check_vma=False,
    )
```

time: 6470 us -> 1980 us (0.31)
  waiting for transfers between devices: 5460 us -> 7.85 us
  Pallas kernels: 0 us -> 1180 us
  matrix products: 600 us -> 406 us
  blocking collectives: 145 us -> 20.5 us
  local copies, waits for them, and re-layouts: 82.4 us -> 187 us
    reduce_scatter x9 -> x0, waiting for transfers between devices: 3990 us -> none  [the longest x2 1740 us: shards(): lax.psum_scatter(expert_terms[2].astype(jnp.bfloat16), 'dp', scatter_dime...]
    all_gather x9 -> x2, waiting for transfers between devices: 1320 us -> 0.01 us  [the longest x1 0.01 us: shards(): lax.all_gather(key_value_full.reshape(n_dp, slice_rows, 2 * hc), 'expert'...]
    pallas_call x0 -> x12, Pallas kernels: none -> 1180 us  [the longest x4 531 us: call(): pl.pallas_call(functools.partial(scatter_kernel, chips, first, second, by...]
    dot_general x66 -> x36, matrix products: 595 us -> 406 us  [product(): return jnp.einsum(pattern, operand, factor, preferred_element_type=F32)]
    all_gather x2 -> x0, blocking collectives: 145 us -> none  [the longest x1 80 us: shards(): lax.all_gather(router_weight, ('dp', 'expert'), axis=0, tiled=True)]
    all_to_all x18 -> x4, waiting for transfers between devices: 100 us -> 7.81 us  [the longest x1 7.8 us: shards(): grad_query = lax.all_to_all(grad_query, 'dp', 0, 0, tiled=True)]
  transfers between devices with their start and end apart: 42 -> 6, of which waited for: 31 -> 1; matrix products, arithmetic and copies ran while one was open for 10% -> 25% of each run, Pallas kernels for 0% -> 51%
where the time goes in v1:
time: 1980 us; the launch traced here: 1970 us
  Pallas kernels  1180 us (60%)
  matrix products  406 us (21%)
  local copies, waits for them, and re-layouts  187 us (9%)
  other arithmetic  130 us (7%)
  starting transfers between devices  20.8 us (1%)
  blocking collectives  20.5 us (1%)
    pallas_call x4, Pallas kernels, call(): pl.pallas_call(functools.partial(scatter_kernel, chips, first, second, by...  531 us
    pallas_call x3, Pallas kernels, gather_all(): pl.pallas_call(functools.partial(gather_kernel, chips, first, second, by_...  505 us
    dot_general x36, matrix products, product(): return jnp.einsum(pattern, operand, factor, preferred_element_type=F32)  406 us
    pallas_call x5, Pallas kernels, exchange(): pl.pallas_call(functools.partial(exchange_kernel, devices, owners, same),...  139 us
  transfers between devices with their start and end apart: 6, of which 1 were waited for; matrix products, arithmetic and copies ran while one was open for 25% of the time, Pallas kernels for 51%

profile of v1, /device:TPU:1, one launch (start us, length us, event | category | flops | bytes accessed | tf_op | source)
XLA Modules:
  0.0 1966.5 jit_solution(2966132801464958246)
XLA Ops:
  9.0 20.5 %all_to_all.25 = bf16[8,64,2,256]{3,2,1,0:T(2,128)(2,1)S(1)} all-to-all(bf16[8,64,2,256]{3,2,1,0:T(2,128)(2,1)S(1)} %copy.897), channel_id=1, replica_groups=mesh['dp'=8,'expert'=4] {'dp'}, dimensions={0} | all-to-all | bytes 1048576 | tf_op jit(solution)/shard_map/all_to_all | solution.py:570
  47.0 65.1 %shard_map.196 = f32[32,16,128]{2,1,0:T(8,128)} custom-call(f32[1,16,128]{2,1,0:T(8,128)} %fusion.140.x_ref), custom_call_target="tpu_custom_call" | custom-call | tf_op jit(solution)/shard_map/pallas_call | solution.py:442
  197.7 332.8 %shard_map.197 = bf16[2,32,64,2048]{3,2,1,0:T(8,128)(2,1)} custom-call(bf16[2,64,2048]{2,1,0:T(8,128)(2,1)} %fusion.107.x_ref), custom_call_target="tpu_custom_call" | custom-call | tf_op jit(solution)/shard_map/pallas_call | solution.py:177
  648.6 87.3 %shard_map.198 = f32[2,64,2048]{2,1,0:T(8,128)} custom-call(bf16[2,32,64,2048]{3,2,1,0:T(8,128)(2,1)} %bitcast.540), custom_call_target="tpu_custom_call" | custom-call | tf_op jit(solution)/shard_map/pallas_call | solution.py:363
  739.3 87.3 %shard_map.199 = bf16[32,2,64,2048]{3,2,1,0:T(8,128)(2,1)} custom-call(bf16[2,64,2048]{2,1,0:T(8,128)(2,1)} %multiply_convert_fusion.5.x_ref), custom_call_target="tpu_custom_call" | custom-call | tf_op jit(solution)/shard_map/pallas_call | solution.py:177
  874.9 14.0 fusion.18
  899.2 20.4 %multiply_reduce_fusion = (f32[2,16,96]{2,1,0:T(8,128)S(1)}, f32[2,16,96,768]{3,2,1,0:T(8,128)}) fusion(f32[2,16,96,768]{3,2,1,0:T(8,128)} %fusion.16, f32[2,16,96,768]{3,2,1,0:T(8,128)} %fusion.18, bf16[2,768,2048]{2,1,0:T(8,128)(2,1)} %constant_dynamic-update-slice_fusion, bf16[2,16,96,2048]{3,2,0,1:T(8,128)(2,1)} %convert_bitcast_fusion.1), kind=kOutput, calls=%fused_computation.33 | convolution fusion | flops 9680188416 | bytes 47198208 | tf_op jit(solution)/shard_map/lsrd,lfd->lsrf/dot_general | solution.py:468
  936.5 16.8 multiply_convert_fusion
  953.3 18.6 fusion.31
  971.8 18.1 fusion.29
  990.0 23.4 %bitcast_convert_fusion = bf16[16,256,2048]{2,1,0:T(8,128)(2,1)} fusion(f32[2,16,96,2048]{3,2,0,1:T(8,128)} %fusion.31, f32[2,16,96,2048]{3,2,0,1:T(8,128)} %fusion.29, s32[16,2,256]{2,1,0:T(2,128)S(1)} %copy.924), kind=kOutput, calls=%fused_computation.3 | convolution fusion | flops 3242983424 | bytes 67141632 | tf_op jit(solution)/shard_map/slrt,lsrd->std/dot_general | solution.py:468
  1013.4 84.6 %shard_map.201 = f32[2,64,2048]{2,1,0:T(8,128)} custom-call(bf16[32,2,64,2048]{3,2,1,0:T(8,128)(2,1)} %bitcast.537), custom_call_target="tpu_custom_call" | custom-call | tf_op jit(solution)/shard_map/pallas_call | solution.py:363
  1103.3 85.0 %shard_map.203 = bf16[2,32,64,2048]{3,2,1,0:T(8,128)(2,1)} custom-call(bf16[2,64,2048]{2,1,0:T(8,128)(2,1)} %fusion.131.x_ref), custom_call_target="tpu_custom_call" | custom-call | tf_op jit(solution)/shard_map/pallas_call | solution.py:177
  1251.8 15.0 bitcast_convert_fusion.3
  1266.8 16.7 bitcast_convert_fusion.4
  1307.7 16.2 fusion.27
  1337.3 268.5 %shard_map.200 = f32[2,64,2048]{2,1,0:T(8,128)} custom-call(bf16[32,2,64,2048]{3,2,1,0:T(8,128)(2,1)} %bitcast.538), custom_call_target="tpu_custom_call" | custom-call | tf_op jit(solution)/shard_map/pallas_call | solution.py:363
  1635.4 14.6 bitcast_convert_fusion.6
  1650.0 38.4 %shard_map.207 = bf16[32,64,512]{2,1,0:T(8,128)(2,1)} custom-call(bf16[32,64,512]{2,1,0:T(8,128)(2,1)} %bitcast.574), custom_call_target="tpu_custom_call" | custom-call | tf_op jit(solution)/shard_map/pallas_call | solution.py:442
  1701.5 16.7 fusion.4
  1718.2 22.8 %fusion.1 = bf16[16,256,2048]{2,1,0:T(8,128)(2,1)} fusion(f32[16,256,2048,1]{2,1,3,0:T(8,128)} %fusion.4, bf16[2048,512,1]{1,0,2:T(8,128)(2,1)} %bitcast.608, bf16[16,256,256]{2,1,0:T(8,128)(2,1)} %copy.960, bf16[16,256,256]{2,1,0:T(8,128)(2,1)} %copy.959), kind=kOutput, calls=%fused_computation.2 | convolution fusion | flops 8615100416 | bytes 56623104 | tf_op jit(solution)/shard_map/stc,dc->std/dot_general | solution.py:468
  1741.0 91.0 %shard_map.204 = f32[2,64,2048]{2,1,0:T(8,128)} custom-call(bf16[2,32,64,2048]{3,2,1,0:T(8,128)(2,1)} %bitcast.550), custom_call_target="tpu_custom_call" | custom-call | tf_op jit(solution)/shard_map/pallas_call | solution.py:363
  1835.8 17.4 shard_map.206
  1871.6 17.3 fusion.38
  (459 shorter events, 539.7 us)
Async XLA Ops:
  7.2 628.5 %copy-start = (bf16[2,256,2048]{2,1,0:T(8,128)(2,1)S(1)}, bf16[2,256,2048]{2,1,0:T(8,128)(2,1)}, u32[]{:S(2)}) copy-start(bf16[2,256,2048]{2,1,0:T(8,128)(2,1)} %param.21) | copy-start | bytes 6291460
  7.2 577.9 %all-gather.3.cloned.1.call-start = ((), (), s32[]{:S(2)}) async-start(), calls=%async_computation.5 | async-start | bytes 2621440 | tf_op jit(solution)/shard_map/all_gather | solution.py:571
  30.6 858.3 %all-gather.5.cloned.1.call-start = ((), (), s32[]{:S(2)}) async-start(), calls=%async_computation.6 | async-start | bytes 17301504 | tf_op jit(solution)/shard_map/all_gather | solution.py:675
  40.3 108.0 %all-to-all-start.1 = ((bf16[8,2,256,256]{3,2,1,0:T(8,128)(2,1)}), bf16[8,2,256,256]{3,2,1,0:T(8,128)(2,1)}, u32[]{:S(2)}, u32[]{:S(2)}) async-start(bf16[8,2,256,256]{3,2,1,0:T(8,128)(2,1)} %copy.904), calls=%async_computation.1 | async-start | bytes 4194304 | tf_op jit(solution)/shard_map/all_to_all | solution.py:565
  148.3 699.7 %all-to-all-start.2 = ((bf16[8,2,2,256,768]{4,3,2,1,0:T(8,128)(2,1)}), bf16[8,2,2,256,768]{4,3,2,1,0:T(8,128)(2,1)}, u32[]{:S(2)}, u32[]{:S(2)}) async-start(bf16[8,2,2,256,768]{4,3,2,1,0:T(8,128)(2,1)} %fusion.86), calls=%async_computation.2 | async-start | bytes 25165824 | tf_op jit(solution)/shard_map/all_to_all | solution.py:585
  159.0 382.1 %copy-start.44 = (s32[16,256,2]{1,0,2:T(8,128)}, s32[16,256,2]{1,0,2:T(8,128)S(1)}, u32[]{:S(2)}) copy-start(s32[16,256,2]{1,0,2:T(8,128)S(1)} %eq.133) | copy-start | bytes 98308
  165.0 376.1 %copy-start.79 = (s32[2]{0:T(128)}, s32[2]{0:T(128)S(1)}, u32[]{:S(2)}) copy-start(s32[2]{0:T(128)S(1)} %iota_add_fusion.1) | copy-start | bytes 28
  191.2 798.7 %copy-start.37 = (s32[16,2,256]{2,1,0:T(2,128)}, s32[16,2,256]{2,1,0:T(2,128)S(1)}, u32[]{:S(2)}) copy-start(s32[16,2,256]{2,1,0:T(2,128)S(1)} %copy.924) | copy-start | bytes 98308
  191.3 444.4 %copy-start.34 = (s32[16,2,256]{2,1,0:T(2,128)}, s32[16,2,256]{2,1,0:T(2,128)S(1)}, u32[]{:S(2)}) copy-start(s32[16,2,256]{2,1,0:T(2,128)S(1)} %copy.896) | copy-start | bytes 98308
  195.1 335.3 %copy-start.56 = (f32[2048]{0:T(1024)}, f32[2048]{0:T(1024)S(1)}, u32[]{:S(2)}) copy-start(f32[2048]{0:T(1024)S(1)} %get-tuple-element.113) | copy-start | bytes 24580
  195.1 543.0 %copy-start.50 = (f32[2048]{0:T(1024)}, f32[2048]{0:T(1024)S(1)}, u32[]{:S(2)}) copy-start(f32[2048]{0:T(1024)S(1)} %get-tuple-element.112) | copy-start | bytes 24580
  195.6 334.8 %copy-start.70 = (f32[2,64]{1,0:T(2,128)}, f32[2,64]{1,0:T(2,128)S(1)}, u32[]{:S(2)}) copy-start(f32[2,64]{1,0:T(2,128)S(1)} %get-tuple-element.166) | copy-start | bytes 1540
  541.9 93.8 %copy-start.46 = (f32[2,16,96]{2,1,0:T(8,128)}, f32[2,16,96]{2,1,0:T(8,128)S(1)}, u32[]{:S(2)}) copy-start(f32[2,16,96]{2,1,0:T(8,128)S(1)} %copy.917) | copy-start | bytes 36868
  1248.2 51.8 %all-to-all-start.3 = ((bf16[8,2,256,256]{3,2,1,0:T(8,128)(2,1)}), bf16[8,2,256,256]{3,2,1,0:T(8,128)(2,1)S(1)}, u32[]{:S(2)}, u32[]{:S(2)}) async-start(bf16[8,2,256,256]{3,2,1,0:T(8,128)(2,1)} %bitcast.561), calls=%async_computation.3 | async-start | bytes 4194304 | tf_op jit(solution)/shard_map/all_to_all | solution.py:782
  1301.4 621.5 %all-to-all-start.4 = ((bf16[8,2,2,256,768]{4,3,1,2,0:T(8,128)(2,1)}), bf16[8,2,2,256,768]{4,3,1,2,0:T(8,128)(2,1)}, u32[]{:S(2)}, u32[]{:S(2)}) async-start(bf16[8,2,2,256,768]{4,3,1,2,0:T(8,128)(2,1)} %copy_bitcast_fusion), calls=%async_computation.4 | async-start | bytes 25165824 | tf_op jit(solution)/shard_map/all_to_all | solution.py:712
  1337.2 268.5 %copy-start.69 = (f32[2,16,96]{2,1,0:T(8,128)S(1)}, f32[2,16,96]{2,1,0:T(8,128)}, u32[]{:S(2)}) copy-start(f32[2,16,96]{2,1,0:T(8,128)} %get-tuple-element.147) | copy-start | bytes 36868
  1337.2 268.6 %copy-start.36 = (s32[16,2,256]{2,1,0:T(2,128)S(1)}, s32[16,2,256]{2,1,0:T(2,128)}, u32[]{:S(2)}) copy-start(s32[16,2,256]{2,1,0:T(2,128)} %copy-done.34) | copy-start | bytes 98308
  1337.2 269.6 %copy-start.45 = (s32[16,256,2]{1,0,2:T(8,128)S(1)}, s32[16,256,2]{1,0,2:T(8,128)}, u32[]{:S(2)}) copy-start(s32[16,256,2]{1,0,2:T(8,128)} %copy-done.44) | copy-start | bytes 98308
  1337.3 269.6 %copy-start.81 = (s32[2]{0:T(128)S(1)}, s32[2]{0:T(128)}, u32[]{:S(2)}) copy-start(s32[2]{0:T(128)} %copy-done.79) | copy-start | bytes 28
  1337.3 282.0 %copy-start.68 = (f32[2,1,64,2]{2,1,0,3:T(1,128)S(1)}, f32[2,1,64,2]{2,1,0,3:T(1,128)}, u32[]{:S(2)}) copy-start(f32[2,1,64,2]{2,1,0,3:T(1,128)} %fusion.148) | copy-start | bytes 3076
  1337.3 282.0 %copy-start.82 = (s32[2,1,64,2]{2,3,0,1:T(2,128)S(1)}, s32[2,1,64,2]{2,3,0,1:T(2,128)}, u32[]{:S(2)}) copy-start(s32[2,1,64,2]{2,3,0,1:T(2,128)} %constant_dynamic-slice_fusion.5) | copy-start | bytes 3076
  1337.3 282.2 %copy-start.40 = (bf16[2,16,96,2,128]{4,3,2,1,0:T(2,128)(2,1)S(1)}, bf16[2,16,96,2,128]{4,3,2,1,0:T(2,128)(2,1)}, u32[]{:S(2)}) copy-start(bf16[2,16,96,2,128]{4,3,2,1,0:T(2,128)(2,1)} %copy-done.39) | copy-start | bytes 4718596
  1337.3 282.2 %copy-start.55 = (f32[2,16,2,96]{3,0,2,1:T(2,128)S(1)}, f32[2,16,2,96]{3,0,2,1:T(2,128)}, u32[]{:S(2)}) copy-start(f32[2,16,2,96]{3,0,2,1:T(2,128)} %copy-done.53) | copy-start | bytes 73732
  1741.0 93.0 %copy-start.64 = (f32[2048]{0:T(1024)S(1)}, f32[2048]{0:T(1024)}, u32[]{:S(2)}) copy-start(f32[2048]{0:T(1024)} %get-tuple-element.108) | copy-start | bytes 24580
  (73 other events, 1846.0 us)
Sparse Core Ops, SparseCore 0:
  30.7 35.3 all-gather.2
  69.1 155.2 all-gather.4

commit v2 on v1

v2 whole, which is shorter than its diff:
```python
import functools

import jax
import jax.numpy as jnp
from jax import lax
from jax.experimental import pallas as pl
from jax.experimental.pallas import tpu as pltpu
from jax.sharding import PartitionSpec as P

MESH = pl.DeviceIdType.MESH
BF16 = jnp.bfloat16
START = 1
F32 = jnp.float32
ANY = pl.BlockSpec(memory_space=pl.ANY)


def expert_factors(owners):
    return (2, owners // 2) if owners % 2 == 0 and owners > 2 else (1, owners)


class Place:
    def __init__(self, chips, first, second):
        dp = lax.axis_index("dp")
        ex = lax.axis_index("expert")
        self.chips, self.first, self.second = chips, first, second
        self.owners, self.n_dp = first * second, chips * 2
        self.dp, self.ex = dp, ex
        self.z, self.k = dp // 2, dp % 2
        self.a, self.b = ex // second, ex % second

    def at(self, z=None, k=None, a=None, b=None):
        z = self.z if z is None else z
        k = self.k if k is None else k
        a = self.a if a is None else a
        b = self.b if b is None else b
        return (z * 2 + k, a * self.second + b)

    def other(self, i):
        number = (self.dp * self.owners + self.ex + i) % (self.n_dp * self.owners)
        return number, (number // self.owners, number % self.owners)

    def greet(self, reach):
        barrier = pltpu.get_barrier_semaphore()

        def hello(target):
            pl.semaphore_signal(barrier, inc=1, device_id=target, device_id_type=MESH)

        if reach == "all":
            count = self.n_dp * self.owners - 1

            def one(i, carried):
                hello(self.other(i)[1])
                return carried

            lax.fori_loop(1, count + 1, one, 0)
            pl.semaphore_wait(barrier, count)
            return
        if reach in ("column", "dp"):
            for i in range(1, self.n_dp):
                hello(((self.dp + i) % self.n_dp, self.ex))
        if reach == "column":
            pl.semaphore_wait(barrier, self.n_dp - 1)
            return
        for i in range(1, self.first):
            hello(self.at(a=(self.a + i) % self.first))
        for i in range(1, self.second):
            hello(self.at(b=(self.b + i) % self.second))
        if reach == "dp":
            pl.semaphore_wait(barrier, self.first + self.second + self.n_dp - 3)
            return
        hello(self.at(k=1 - self.k))
        pl.when(self.z > 0)(lambda: hello(self.at(z=self.z - 1)))
        pl.when(self.z < self.chips - 1)(lambda: hello(self.at(z=self.z + 1)))
        along = (self.z > 0).astype(jnp.int32) + (self.z < self.chips - 1).astype(jnp.int32)
        pl.semaphore_wait(barrier, self.first + self.second - 1 + along)


def remote(src, dst, send, recv, target):
    return pltpu.make_async_remote_copy(
        src_ref=src, dst_ref=dst, send_sem=send, recv_sem=recv, device_id=target, device_id_type=MESH
    )


class Job:
    def __init__(self, src, out_shape, pick, put):
        self.src, self.out_shape, self.pick, self.put = src, out_shape, pick, put


class Load:
    def __init__(self, jobs, me, srcs, outs, sems):
        self.jobs, self.me, self.srcs, self.outs = jobs, me, srcs, outs
        self.own, self.send, self.recv = sems if jobs else (None,) * 3

    def peers(self):
        return [(i, (self.me.dp + i) % self.me.n_dp) for i in range(1, self.me.n_dp)]

    def copy(self, j, i, d):
        me, job = self.me, self.jobs[j]
        return remote(
            job.pick(self.srcs[j], d), job.put(self.outs[j], me.dp),
            self.send.at[j, i], self.recv.at[j, me.dp], (d, me.ex),
        )

    def stay(self, j):
        job, dp = self.jobs[j], self.me.dp
        return pltpu.make_async_copy(
            job.pick(self.srcs[j], dp), job.put(self.outs[j], dp), self.own.at[j]
        )

    def start(self):
        for j in range(len(self.jobs)):
            for i, d in self.peers():
                self.copy(j, i, d).start()
            self.stay(j).start()

    def landed(self, j):
        self.stay(j).wait()
        for i, d in self.peers():
            dst = self.jobs[j].put(self.outs[j], d)
            remote(dst, dst, self.send.at[j, i], self.recv.at[j, d], (d, self.me.ex)).wait_recv()

    def finish(self, skip=()):
        for j in range(len(self.jobs)):
            if j not in skip:
                self.landed(j)
            for i, d in self.peers():
                self.copy(j, i, d).wait_send()

    @staticmethod
    def scratch(jobs, n_dp):
        if not jobs:
            return []
        sem = pltpu.SemaphoreType.DMA
        return [sem((len(jobs),)), sem((len(jobs), n_dp)), sem((len(jobs), n_dp))]


class Carried:
    def __init__(self, jobs, chips, owners, refs, ins, outs):
        first, second = expert_factors(owners)
        n = len(jobs)
        refs = list(refs)
        srcs = refs[ins : ins + n]
        results = refs[ins + n + outs : ins + 2 * n + outs]
        sems = refs[len(refs) - 3 :] if n else []
        kept = refs[:ins] + refs[ins + n : ins + n + outs] + refs[ins + 2 * n + outs :]
        self.refs = kept[: len(kept) - 3] if n else kept
        self.jobs = jobs
        if n:
            self.me = Place(chips, first, second)
            self.load = Load(jobs, self.me, srcs, results, sems)

    def start(self):
        if self.jobs:

            @pl.when(pl.program_id(0) == 0)
            def _():
                self.me.greet("column")
                self.load.start()

    def finish(self):
        if self.jobs:
            pl.when(pl.program_id(0) == pl.num_programs(0) - 1)(self.load.finish)


class Mail:
    def __init__(self, arrays, me, srcs, outs, sems):
        self.arrays, self.me, self.srcs, self.outs = arrays, me, srcs, outs
        self.devices = me.n_dp * me.owners
        self.number = me.dp * me.owners + me.ex
        self.own, self.send, self.recv = sems if arrays else (None,) * 3

    def part(self, j, n):
        return self.srcs[j].at[0 if self.arrays[j].shape[0] == 1 else n]

    def copy(self, j, i):
        n, where = self.me.other(i)
        return remote(
            self.part(j, n), self.outs[j].at[self.number], self.send.at[j, i],
            self.recv.at[j, self.number], where,
        )

    def stay(self, j):
        return pltpu.make_async_copy(
            self.part(j, self.number), self.outs[j].at[self.number], self.own.at[j]
        )

    def start(self):
        for j in range(len(self.arrays)):

            def one(i, carried, j=j):
                self.copy(j, i).start()
                return carried

            self.stay(j).start()
            lax.fori_loop(1, self.devices, one, 0)

    def finish(self):
        for j in range(len(self.arrays)):

            def one(i, carried, j=j):
                n, where = self.me.other(i)
                there = self.outs[j].at[n]
                remote(there, there, self.send.at[j, i], self.recv.at[j, n], where).wait_recv()
                self.copy(j, i).wait_send()
                return carried

            self.stay(j).wait()
            lax.fori_loop(1, self.devices, one, 0)

    @staticmethod
    def scratch(arrays, devices):
        if not arrays:
            return []
        sem = pltpu.SemaphoreType.DMA
        return [sem((len(arrays),)), sem((len(arrays), devices)), sem((len(arrays), devices))]

    @staticmethod
    def shapes(arrays, devices):
        return [jax.ShapeDtypeStruct((devices,) + a.shape[1:], a.dtype) for a in arrays]


class Gather:
    def __init__(self, me, by_row, x_ref, out_ref, sems):
        self.me, self.by_row, self.x_ref, self.out_ref = me, by_row, x_ref, out_ref
        self.own_sem, self.recv, self.sends = sems
        self.pending = []
        self.own = self.index(me.z, me.a, me.b)

    @staticmethod
    def scratch(chips, first, second):
        sem = pltpu.SemaphoreType.DMA
        sends = 4 + (2 * chips - 1) * (
            2 + 2 * (first + second - 1) + 2 * (second - 1) * first + 2 * (first - 1) * second
        )
        return [sem((2,)), sem((chips * 2 * first * second, 2)), sem((sends,))]

    def index(self, z, a, b):
        return (z * 2 + self.me.k) * self.me.owners + a * self.me.second + b

    def piece(self, blk, h):
        return self.out_ref.at[h, blk] if self.by_row else self.out_ref.at[blk, h]

    def push(self, src, blk, h, target, when=None):
        copy = remote(
            src, self.piece(blk, h), self.sends.at[len(self.pending)], self.recv.at[blk, h], target
        )
        self.pending.append((copy, when))
        copy.start() if when is None else pl.when(when)(copy.start)

    def landed(self, blk, h, when=None):
        there = self.piece(blk, h)
        copy = remote(there, there, self.sends.at[0], self.recv.at[blk, h], self.me.at())
        copy.wait_recv() if when is None else pl.when(when)(copy.wait_recv)

    def spread(self, blk, source, when=None):
        me = self.me
        for h in range(2):
            for i in range(1, me.second):
                self.push(source(h), blk, h, me.at(b=(me.b + i) % me.second), when)
            for i in range(1, me.first):
                self.push(source(h), blk, h, me.at(a=(me.a + i) % me.first), when)
        for h in range(2):
            self.push(source(h), blk, h, me.at(k=1 - me.k), when)

    def relay(self, z, when):
        me = self.me
        for h in range(2):
            if h == 0:
                froms = [(me.a, (me.b + i) % me.second) for i in range(1, me.second)]
                onward = [dict(a=(me.a + i) % me.first) for i in range(1, me.first)]
            else:
                froms = [((me.a + i) % me.first, me.b) for i in range(1, me.first)]
                onward = [dict(b=(me.b + i) % me.second) for i in range(1, me.second)]
            for a, b in froms:
                blk = self.index(z, a, b)
                self.landed(blk, h, when)
                for target in onward:
                    self.push(self.piece(blk, h), blk, h, me.at(**target), when)
                self.push(self.piece(blk, h), blk, h, me.at(k=1 - me.k), when)

    def settle(self, z, when):
        me = self.me
        for h in range(2):
            for i in range(1, me.second if h else me.first):
                for j in range(me.first if h else me.second):
                    if h == 0:
                        a, b = (me.a + i) % me.first, (me.b + j) % me.second
                    else:
                        a, b = (me.a + j) % me.first, (me.b + i) % me.second
                    blk = self.index(z, a, b)
                    self.landed(blk, h, when)
                    self.push(self.piece(blk, h), blk, h, me.at(k=1 - me.k), when)

    def begin(self):
        me, x_ref, own = self.me, self.x_ref, self.own
        self.stays = [
            pltpu.make_async_copy(x_ref.at[h], self.piece(own, h), self.own_sem.at[h])
            for h in range(2)
        ]
        for stay in self.stays:
            stay.start()
        for h in range(2):
            self.push(x_ref.at[h], own, h, me.at(z=me.z + 1), me.z < me.chips - 1)
            self.push(x_ref.at[h], own, h, me.at(z=me.z - 1), me.z > 0)
        self.spread(own, lambda h: x_ref.at[h])
        self.queue = [(me.z, None)]

    def stage(self, t):
        me, fresh = self.me, []
        for sign in (-1, 1):
            z = me.z + sign * t
            there = (z >= 0) if sign < 0 else (z < me.chips)
            blk = self.index(z, me.a, me.b)
            further = (me.z < me.chips - 1) if sign < 0 else (me.z > 0)
            for h in range(2):
                self.landed(blk, h, there)
                self.push(self.piece(blk, h), blk, h, me.at(z=me.z - sign), there & further)
            self.spread(blk, lambda h, blk=blk: self.piece(blk, h), there)
            fresh.append((z, there))
        self.drain()
        self.queue = fresh

    def drain(self):
        for z, there in self.queue:
            self.relay(z, there)
        for z, there in self.queue:
            self.settle(z, there)

    def finish(self):
        me = self.me
        for stay in self.stays:
            stay.wait()
        for z in range(me.chips):
            for e in range(me.owners):
                for h in range(2):
                    self.landed((z * 2 + 1 - me.k) * me.owners + e, h)
        for copy, when in self.pending:
            copy.wait_send() if when is None else pl.when(when)(copy.wait_send)


def taken(refs, number):
    return [refs.pop(0) for _ in range(number)]


def gather_kernel(chips, first, second, orders, jobs, mails, *refs):
    me = Place(chips, first, second)
    refs = list(refs)
    x_refs = taken(refs, len(orders))
    mail_srcs = taken(refs, len(mails))
    srcs = taken(refs, len(jobs))
    out_refs = taken(refs, len(orders))
    mail_outs = taken(refs, len(mails))
    outs = taken(refs, len(jobs))
    gathers = [
        Gather(me, by_row, x_ref, out_ref, taken(refs, 3))
        for by_row, x_ref, out_ref in zip(orders, x_refs, out_refs)
    ]
    if mails:
        spread_send, spread_recv = taken(refs, 2)
        mail = Mail(mails, me, mail_srcs, mail_outs, taken(refs, 3))
    load = Load(jobs, me, srcs, outs, refs)
    me.greet("all" if mails else "dp" if jobs else "near")
    for gather in gathers:
        gather.begin()
    if mails:
        mail.start()
    for t in range(1, chips):
        for gather in gathers:
            gather.stage(t)
        if t == min(START, chips - 1):
            load.start()
    for gather in gathers:
        gather.drain()
    if mails:
        j = len(jobs) - 1
        load.landed(j)
        column = outs[j].at[:, me.ex]
        spreads = [
            remote(
                column, column, spread_send.at[i], spread_recv.at[me.ex],
                (me.dp, (me.ex + i) % me.owners),
            )
            for i in range(1, me.owners)
        ]
        for copy in spreads:
            copy.start()
        mail.finish()
        for i in range(1, me.owners):
            e = (me.ex + i) % me.owners
            there = outs[j].at[:, e]
            remote(there, there, spread_send.at[i], spread_recv.at[e], (me.dp, e)).wait_recv()
        for copy in spreads:
            copy.wait_send()
    for gather in gathers:
        gather.finish()
    load.finish(skip=(len(jobs) - 1,) if mails else ())


def gather_all(xs, orders, chips, owners, collective_id, jobs=(), mails=()):
    first, second = expert_factors(owners)
    blocks = chips * 2 * owners
    sem = pltpu.SemaphoreType.DMA
    shapes = []
    for x, by_row in zip(xs, orders):
        rest = x.shape[1:]
        shape = (2, blocks) + rest if by_row else (blocks, 2) + rest
        shapes.append(jax.ShapeDtypeStruct(shape, x.dtype))
    shapes += Mail.shapes(mails, blocks) + [job.out_shape for job in jobs]
    ins = list(xs) + list(mails) + [job.src for job in jobs]
    scratch = Gather.scratch(chips, first, second) * len(xs)
    if mails:
        scratch += [sem((owners,)), sem((owners,))] + Mail.scratch(mails, blocks)
    return pl.pallas_call(
        functools.partial(
            gather_kernel, chips, first, second, orders, jobs,
            [jax.ShapeDtypeStruct(a.shape, a.dtype) for a in mails],
        ),
        out_shape=shapes,
        in_specs=[ANY] * len(ins),
        out_specs=[ANY] * len(shapes),
        scratch_shapes=scratch + Load.scratch(jobs, chips * 2),
        compiler_params=pltpu.CompilerParams(collective_id=collective_id, has_side_effects=True),
    )(*ins)


def scatter_kernel(
    chips, first, second, by_row, column, width, jobs, mails, *refs
):
    me = Place(chips, first, second)
    owners = first * second
    n, m = len(jobs), len(mails)
    p_ref, srcs, mail_srcs = refs[0], refs[1 : n + 1], refs[n + 1 : n + m + 1]
    refs = refs[n + m + 1 :]
    out_ref, outs, mail_outs = refs[0], refs[1 : n + 1], refs[n + 1 : n + m + 1]
    refs = refs[n + m + 1 :]
    mine, fromk, a0, b0, b1, a1, fromz, total = refs[:8]
    load_sem, ks, a0s, b0s, b1s, a1s, zs, sends = refs[8:16]
    refs = refs[16:]
    mail = Mail(mails, me, mail_srcs, mail_outs, refs[:3])
    carried = Load(jobs, me, srcs, outs, refs[3:] if mails else refs)
    me.greet("all" if mails else "dp" if jobs else "near")
    pending = []

    def push(src, dst, sem, target, when=None):
        copy = remote(src, dst, sends.at[len(pending)], sem, target)
        pending.append((copy, when))
        copy.start() if when is None else pl.when(when)(copy.start)

    def landed(dst, sem):
        remote(dst, dst, sends.at[0], sem, me.at()).wait_recv()

    low = me.z < chips // 2

    def line(t):
        return jnp.where(
            low,
            jnp.where(t < chips - 1 - me.z, chips - 1 - t, t - (chips - 1 - me.z)),
            jnp.where(t < me.z, t, chips - 1 - (t - me.z)),
        )

    cut = pl.ds(column, width)

    def block(z, k, e):
        blk = (z * 2 + k) * owners + e
        return p_ref.at[:, blk, :, cut] if by_row else p_ref.at[blk, :, :, cut]

    loads = {}
    for t in range(chips):
        z = line(t)
        for e in range(owners):
            load = pltpu.make_async_copy(
                block(z, me.k, e), mine.at[t, e], load_sem.at[t, e]
            )
            load.start()
            loads[t, e] = load
            push(
                block(z, 1 - me.k, e),
                fromk.at[t, e], ks.at[t, e], me.at(k=1 - me.k),
            )

    mail.start()
    carried.start()

    def add(*terms):
        value = terms[0].astype(F32)
        for term in terms[1:]:
            value = value + term.astype(F32)
        return value

    def step_one(t):
        for i in range(first):
            for j in range(second):
                a, b = (me.a + 1 + i) % first, (me.b + 1 + j) % second
                e = a * second + b
                loads_sem = load_sem.at[t, e]
                pltpu.make_async_copy(mine.at[t, e], mine.at[t, e], loads_sem).wait()
                landed(fromk.at[t, e], ks.at[t, e])
                mine[t, e] = add(mine[t, e], fromk[t, e]).astype(BF16)
                if i < first - 1:
                    push(
                        mine.at[t, e, 0], a0.at[t, first - 2 - i, b],
                        a0s.at[t, first - 2 - i, b], me.at(a=a),
                    )
                if j < second - 1:
                    push(
                        mine.at[t, e, 1], b1.at[t, second - 2 - j, a],
                        b1s.at[t, second - 2 - j, a], me.at(b=b),
                    )

    def step_two(t):
        for j in range(second - 1):
            b = (me.b + 1 + j) % second
            e = me.a * second + b
            for i in range(first - 1):
                landed(a0.at[t, i, b], a0s.at[t, i, b])
            mine[t, e, 0] = add(
                mine[t, e, 0], *[a0[t, i, b] for i in range(first - 1)]
            ).astype(BF16)
            push(
                mine.at[t, e, 0], b0.at[t, second - 2 - j],
                b0s.at[t, second - 2 - j], me.at(b=b),
            )
        for i in range(first - 1):
            a = (me.a + 1 + i) % first
            e = a * second + me.b
            for j in range(second - 1):
                landed(b1.at[t, j, a], b1s.at[t, j, a])
            mine[t, e, 1] = add(
                mine[t, e, 1], *[b1[t, j, a] for j in range(second - 1)]
            ).astype(BF16)
            push(
                mine.at[t, e, 1], a1.at[t, first - 2 - i],
                a1s.at[t, first - 2 - i], me.at(a=a),
            )

    def step_three(t):
        z = line(t)
        e = me.ex
        for i in range(first - 1):
            landed(a0.at[t, i, me.b], a0s.at[t, i, me.b])
            landed(a1.at[t, i], a1s.at[t, i])
        for j in range(second - 1):
            landed(b1.at[t, j, me.a], b1s.at[t, j, me.a])
            landed(b0.at[t, j], b0s.at[t, j])
        total[t, 0] = add(
            mine[t, e, 0], *[a0[t, i, me.b] for i in range(first - 1)],
            *[b0[t, j] for j in range(second - 1)],
        )
        total[t, 1] = add(
            mine[t, e, 1], *[b1[t, j, me.a] for j in range(second - 1)],
            *[a1[t, i] for i in range(first - 1)],
        )
        if t < chips - 1:
            up = z > me.z
            from_beyond = jnp.where(up, me.z > 0, me.z < chips - 1)

            @pl.when(from_beyond)
            def _():
                landed(fromz.at[z], zs.at[z])
                total[t] = total[t] + fromz[z].astype(F32)

            mine[t, e] = total[t].astype(BF16)
            push(mine.at[t, e], fromz.at[z], zs.at[z], me.at(z=me.z + 1), up)
            slot = jnp.where(z == me.z - 1, chips, z)
            push(mine.at[t, e], fromz.at[slot], zs.at[slot], me.at(z=me.z - 1), jnp.logical_not(up))
        else:

            @pl.when(me.z > 0)
            def _():
                landed(fromz.at[me.z], zs.at[me.z])
                total[t] = total[t] + fromz[me.z].astype(F32)

            @pl.when(me.z < chips - 1)
            def _():
                landed(fromz.at[chips], zs.at[chips])
                total[t] = total[t] + fromz[chips].astype(F32)

            out_ref[...] = total[t]

    for t in range(chips + 2):
        if t < chips:
            step_one(t)
        if 0 <= t - 1 < chips:
            step_two(t - 1)
        if 0 <= t - 2 < chips:
            step_three(t - 2)
    mail.finish()
    carried.finish()
    for copy, when in pending:
        copy.wait_send() if when is None else pl.when(when)(copy.wait_send)


def scatter_sum(p, chips, owners, by_row, collective_id, jobs=(), mails=()):
    first, second = expert_factors(owners)
    half, full = p.shape[2:]
    parts = 1
    while chips * owners * half * (full // parts) * 8 > 20 * 2**20:
        parts *= 2
    width = full // parts
    one = max(first - 1, 1), max(second - 1, 1)
    sends = chips * (owners + 2 + 2 * (first - 1) * second + 2 * (second - 1) * first)
    sends += chips * (first + second)

    def call(part, jobs, mails):
        sem = pltpu.SemaphoreType.DMA
        return pl.pallas_call(
            functools.partial(scatter_kernel, chips, first, second, by_row, part * width, width, jobs, mails),
            out_shape=[jax.ShapeDtypeStruct((2, half, width), F32)]
            + [job.out_shape for job in jobs]
            + Mail.shapes(mails, chips * 2 * owners),
            in_specs=[ANY] * (1 + len(jobs) + len(mails)),
            out_specs=[pl.BlockSpec(memory_space=pltpu.VMEM)] + [ANY] * (len(jobs) + len(mails)),
            scratch_shapes=[
                pltpu.VMEM((chips, owners, 2, half, width), BF16),
                pltpu.VMEM((chips, owners, 2, half, width), BF16),
                pltpu.VMEM((chips, one[0], second, half, width), BF16),
                pltpu.VMEM((chips, one[1], half, width), BF16),
                pltpu.VMEM((chips, one[1], first, half, width), BF16),
                pltpu.VMEM((chips, one[0], half, width), BF16),
                pltpu.VMEM((chips + 1, 2, half, width), BF16),
                pltpu.VMEM((chips, 2, half, width), F32),
                sem((chips, owners)),
                sem((chips, owners)),
                sem((chips, one[0], second)),
                sem((chips, one[1])),
                sem((chips, one[1], first)),
                sem((chips, one[0])),
                sem((chips + 1,)),
                sem((sends,)),
            ]
            + Mail.scratch(mails, chips * 2 * owners)
            + Load.scratch(jobs, chips * 2),
            compiler_params=pltpu.CompilerParams(
                collective_id=collective_id + part, has_side_effects=True,
                vmem_limit_bytes=60 * 2**20,
            ),
        )(p, *[job.src for job in jobs], *mails)

    calls = [
        call(part, () if part else jobs, () if part else mails) for part in range(parts)
    ]
    whole = calls[0][0] if parts == 1 else jnp.concatenate([c[0] for c in calls], axis=-1)
    return [whole] + list(calls[0][1:])


def exchange_kernel(chips, first, second, array, x_ref, out_ref, *sems):
    me = Place(chips, first, second)
    mail = Mail([array], me, [x_ref], [out_ref], sems)
    me.greet("all")
    mail.start()
    mail.finish()


def exchange(x, chips, owners, collective_id):
    first, second = expert_factors(owners)
    devices = chips * 2 * owners
    shape = jax.ShapeDtypeStruct(x.shape, x.dtype)
    return pl.pallas_call(
        functools.partial(exchange_kernel, chips, first, second, shape),
        out_shape=shape,
        in_specs=[ANY],
        out_specs=ANY,
        scratch_shapes=Mail.scratch([shape], devices),
        compiler_params=pltpu.CompilerParams(collective_id=collective_id, has_side_effects=True),
    )(x)


D = 2048
KVH = 16
HD = 128
FF = 5632
NEXP = 8
TOK_MB = 64
CAP = 24
LANES = 128
EPSILON = 1e-06


def dot(a, b):
    return jnp.dot(a, b, preferred_element_type=F32)


def dot_nt(a, b):
    return lax.dot_general(a, b, (((1,), (1,)), ((), ())), preferred_element_type=F32)


def dot_tn(a, b):
    return lax.dot_general(a, b, (((0,), (0,)), ((), ())), preferred_element_type=F32)


def counted(shape, axis):
    return lax.broadcasted_iota(jnp.int32, shape, axis).astype(F32)


def two_parts(value):
    upper = value.astype(BF16)
    return upper, (value - upper.astype(F32)).astype(BF16)


class Seats:
    def __init__(self, meta, first_expert, count, tri, eye):
        slots = meta.shape[1]
        per = slots // TOK_MB * CAP
        self.count, self.per, self.slots, self.first = count, per, slots, first_expert
        line = counted(meta.shape, 0)
        expert = first_expert + line
        hit = (meta[0:1] == expert) | (meta[1:2] == expert)
        hit = hit & (line < count)
        rank = dot(jnp.where(hit, 1.0, 0.0).astype(BF16), tri)
        block = lax.broadcasted_iota(jnp.int32, meta.shape, 1) // TOK_MB
        seat = jnp.where(hit, block.astype(F32) * CAP + rank + line * per, -1.0)
        self.routes = dot_nt(eye, meta.astype(BF16))
        column = dot_nt(eye, seat.astype(BF16))
        total = count * per
        row = counted((total, slots), 0)
        lane = counted((slots, total), 1)
        here, there = row == seat[0:1], lane == column[:, 0:1]
        for l in range(1, count):
            here = here | (row == seat[l : l + 1])
            there = there | (lane == column[:, l : l + 1])
        self.take = jnp.where(here, 1.0, 0.0).astype(BF16)
        self.put = jnp.where(there, 1.0, 0.0).astype(BF16)

    def gates(self, logits):
        lane = counted(logits.shape, 1)
        one = jnp.sum(jnp.where(lane == self.routes[:, 0:1], logits, 0.0), axis=1, keepdims=True)
        two = jnp.sum(jnp.where(lane == self.routes[:, 1:2], logits, 0.0), axis=1, keepdims=True)
        highest = jnp.maximum(one, two)
        one, two = jnp.exp(one - highest), jnp.exp(two - highest)
        total = one + two
        return one / total, two / total

    def seat_values(self, pairs, plain):
        lane = counted((self.slots, LANES), 1)
        per_expert = []
        for l in range(self.count):
            expert = self.first + l
            values = [
                jnp.where(self.routes[:, 0:1] == expert, a, 0.0)
                + jnp.where(self.routes[:, 1:2] == expert, b, 0.0)
                for a, b in pairs
            ] + list(plain)
            packed = jnp.zeros((self.slots, LANES), F32)
            for i, value in enumerate(values):
                upper, lower = two_parts(value)
                packed = jnp.where(lane == 2 * i, upper.astype(F32), packed)
                packed = jnp.where(lane == 2 * i + 1, lower.astype(F32), packed)
            part = dot(self.take[l * self.per : (l + 1) * self.per], packed.astype(BF16))
            per_expert.append(
                [part[:, 2 * i : 2 * i + 1] + part[:, 2 * i + 1 : 2 * i + 2] for i in range(len(values))]
            )
        return [
            jnp.concatenate(parts, axis=0) if self.count > 1 else parts[0]
            for parts in zip(*per_expert)
        ]

    def slot_values(self, value):
        total = self.count * self.per
        lane = counted((total, LANES), 1)
        row = counted((total, LANES), 0)
        upper, lower = two_parts(value)
        packed = jnp.zeros((total, LANES), F32)
        for l in range(self.count):
            mine = (row >= l * self.per) & (row < (l + 1) * self.per)
            packed = jnp.where(mine & (lane == 2 * l), upper.astype(F32), packed)
            packed = jnp.where(mine & (lane == 2 * l + 1), lower.astype(F32), packed)
        back = dot(self.put, packed.astype(BF16))
        out = jnp.zeros((self.slots, 8), F32)
        lane = counted((self.slots, 8), 1)
        for l in range(self.count):
            value = back[:, 2 * l : 2 * l + 1] + back[:, 2 * l + 1 : 2 * l + 2]
            for k in range(2):
                chosen = (self.routes[:, k : k + 1] == self.first + l) & (lane == k)
                out = jnp.where(chosen, value, out)
        return out


def first_expert(count):
    return (lax.axis_index("expert") * count).astype(F32)


def turned(values, cosine, sine):
    heads = []
    for h in range(values.shape[1] // HD):
        head = values[:, h * HD : (h + 1) * HD]
        heads.append(head * cosine + pltpu.roll(head, HD // 2, 1) * sine)
    return heads[0] if len(heads) == 1 else jnp.concatenate(heads, axis=1)


def mixer_forward_kernel(count, jobs, chips, owners, *refs):
    carried = Carried(jobs, chips, owners, refs, 12, 10)
    (
        length_ref, x_ref, meta_ref, gain_ref, router_ref, wq_ref, wkv_ref, wo_ref,
        tri_ref, eye_ref, upper_ref, lower_ref,
        normed_ref, part_ref, rows_ref, key_ref, value_ref, query_ref, mix_ref, gated_ref, info_ref, gates_ref,
    ) = carried.refs
    carried.start()
    hc = key_ref.shape[2]
    x = x_ref[0].astype(F32)
    inverse = lax.rsqrt(jnp.mean(x * x, axis=1, keepdims=True) + EPSILON)
    normed = (x * inverse * gain_ref[...]).astype(BF16)
    normed_ref[0] = normed
    seats = Seats(meta_ref[0], first_expert(count), count, tri_ref[...], eye_ref[...])
    one, two = seats.gates(dot(normed, router_ref[...]))
    lane = counted((seats.slots, 8), 1)
    gates_ref[0] = jnp.where(lane == 0, one, jnp.where(lane == 1, two, 0.0))
    gate, place = seats.seat_values([(one, two)], [counted((seats.slots, 1), 0)])
    lane = counted((gate.shape[0], 8), 1)
    info_ref[0] = jnp.where(lane == 0, gate, jnp.where(lane == 1, place, 0.0))

    key_value = dot(normed, wkv_ref[...])
    upper, lower = upper_ref[...], lower_ref[...]
    table = upper.astype(F32) + lower.astype(F32)
    key = turned(key_value[:, :hc], table[:, :HD], table[:, HD:]).astype(BF16)
    value = key_value[:, hc:].astype(BF16)
    key_ref[0], value_ref[0] = key, value

    rows = dot(seats.take, normed).astype(BF16)
    per = seats.per
    for l in range(count):
        rows_ref[l] = rows[l * per : (l + 1) * per]
    table = dot(seats.take, upper) + dot(seats.take, lower)
    query = [dot(rows[l * per : (l + 1) * per], wq_ref[l]) for l in range(count)]
    query = query[0] if count == 1 else jnp.concatenate(query, axis=0)
    query = (turned(query, table[:, :HD], table[:, HD:]) * HD ** (-0.5)).astype(BF16)
    query_ref[0] = query

    at = counted((seats.take.shape), 1)
    length = length_ref[pl.program_id(0)].astype(F32)
    allowed = (at <= place) & (at < length)
    mix = []
    for h in range(hc // HD):
        cut = slice(h * HD, (h + 1) * HD)
        scores = jnp.where(allowed, dot_nt(query[:, cut], key[:, cut]), -1e30)
        exponent = jnp.exp(scores - jnp.max(scores, axis=1, keepdims=True))
        probs = (exponent / jnp.sum(exponent, axis=1, keepdims=True)).astype(BF16)
        mix.append(dot(probs, value[:, cut]))
    mix = mix[0] if len(mix) == 1 else jnp.concatenate(mix, axis=1)
    mix_ref[0] = mix
    gated = (mix * gate).astype(BF16)
    for l in range(count):
        gated_ref[l] = gated[l * per : (l + 1) * per]
    out = [dot(gated[l * per : (l + 1) * per], wo_ref[l]).astype(BF16) for l in range(count)]
    out = out[0] if count == 1 else jnp.concatenate(out, axis=0)
    part_ref[0] = dot(seats.put, out).astype(BF16)
    carried.finish()


def mixer_backward_kernel(count, jobs, chips, owners, *refs):
    carried = Carried(jobs, chips, owners, refs, 15, 5)
    (
        length_ref, grad_ref, meta_ref, wq_ref, wkv_ref, wo_ref, tri_ref, eye_ref,
        upper_ref, lower_ref, key_ref, value_ref, query_ref, mix_ref, info_ref,
        part_ref, rows_ref, terms_ref, grad_query_ref, grad_key_value_ref,
    ) = carried.refs
    carried.start()
    hc = key_ref.shape[2]
    seats = Seats(meta_ref[0], first_expert(count), count, tri_ref[...], eye_ref[...])
    per = seats.per
    rows = dot(seats.take, grad_ref[0]).astype(BF16)
    for l in range(count):
        rows_ref[l] = rows[l * per : (l + 1) * per]
    grad_mix = [dot_nt(rows[l * per : (l + 1) * per], wo_ref[l]) for l in range(count)]
    grad_mix = grad_mix[0] if count == 1 else jnp.concatenate(grad_mix, axis=0)
    gate, place = info_ref[0, :, 0:1], info_ref[0, :, 1:2]
    terms_ref[0] = seats.slot_values(jnp.sum(grad_mix * mix_ref[0], axis=1, keepdims=True))
    grad_mix = (grad_mix * gate).astype(BF16)

    at = counted(seats.take.shape, 1)
    length = length_ref[pl.program_id(0)].astype(F32)
    allowed = (at <= place) & (at < length)
    key, value, query = key_ref[0], value_ref[0], query_ref[0]
    grad_query, grad_key, grad_value = [], [], []
    for h in range(hc // HD):
        cut = slice(h * HD, (h + 1) * HD)
        scores = jnp.where(allowed, dot_nt(query[:, cut], key[:, cut]), -1e30)
        exponent = jnp.exp(scores - jnp.max(scores, axis=1, keepdims=True))
        probs = exponent / jnp.sum(exponent, axis=1, keepdims=True)
        grad_probs = dot_nt(grad_mix[:, cut], value[:, cut])
        grad_value.append(dot_tn(probs.astype(BF16), grad_mix[:, cut]))
        row_dot = jnp.sum(probs * grad_probs, axis=1, keepdims=True)
        grad_scores = (probs * (grad_probs - row_dot)).astype(BF16)
        grad_query.append(dot(grad_scores, key[:, cut]))
        grad_key.append(dot_tn(grad_scores, query[:, cut]))

    def joined(parts):
        return parts[0] if len(parts) == 1 else jnp.concatenate(parts, axis=1)

    upper, lower = upper_ref[...], lower_ref[...]
    table = dot(seats.take, upper) + dot(seats.take, lower)
    grad_query = turned(joined(grad_query), table[:, :HD], -table[:, HD:]) * HD ** (-0.5)
    grad_query = grad_query.astype(BF16)
    for l in range(count):
        grad_query_ref[l] = grad_query[l * per : (l + 1) * per]
    table = upper.astype(F32) + lower.astype(F32)
    grad_key = turned(joined(grad_key), table[:, :HD], -table[:, HD:])
    grad_key_value = jnp.concatenate([grad_key, joined(grad_value)], axis=1).astype(BF16)
    grad_key_value_ref[0] = grad_key_value
    back = [
        dot_nt(grad_query[l * per : (l + 1) * per], wq_ref[l]).astype(BF16) for l in range(count)
    ]
    back = back[0] if count == 1 else jnp.concatenate(back, axis=0)
    part_ref[0] = (dot(seats.put, back) + dot_nt(grad_key_value, wkv_ref[...])).astype(BF16)
    carried.finish()


def feed_kernel(count, groups, offsets, offset_ref, x_ref, cot_ref, meta_ref, router_ref, wd_ref, tri_ref, eye_ref, *refs):
    wg_ref, wu_ref = refs[0 : 2 * count : 2], refs[1 : 2 * count : 2]
    (
        part_ref, back_ref, rows_ref, cot_rows_ref, active_ref, grad_gate_ref, grad_up_ref, terms_ref,
        gates_ref, out_ref, dx_ref, gate_ref, term_ref,
    ) = refs[2 * count :]
    kept = []
    for g in range(groups):
        seats = Seats(meta_ref[g], first_expert(count), count, tri_ref[...], eye_ref[...])
        kept.append(seats)
        per = seats.per
        one, two = seats.gates(dot(x_ref[g], router_ref[...]))
        lane = counted((seats.slots, 8), 1)
        gates_ref[g] = jnp.where(lane == 0, one, jnp.where(lane == 1, two, 0.0))
        (gate,) = seats.seat_values([(one, two)], [])
        rows = dot(seats.take, x_ref[g]).astype(BF16)
        valid = meta_ref[g][2:3] > 0.0
        cot_rows = dot(jnp.where(valid, seats.take, 0.0).astype(BF16), cot_ref[g]).astype(BF16)
        for l in range(count):
            rows_ref[l, g * per : (g + 1) * per] = rows[l * per : (l + 1) * per]
            cot_rows_ref[l, g * per : (g + 1) * per] = cot_rows[l * per : (l + 1) * per]
            gate_ref[l, g * per : (g + 1) * per] = jnp.broadcast_to(
                gate[l * per : (l + 1) * per], (per, LANES)
            )
    wide = wd_ref.shape[1]
    for l in range(count):
        rows, cot_rows, gate = rows_ref[l], cot_rows_ref[l], gate_ref[l][:, 0:1]
        gate_part = dot(rows, wg_ref[l][...])
        up_part = dot(rows, wu_ref[l][...])
        grad_plain = dot_nt(cot_rows, wd_ref[l])
        sigmoid = 1.0 / (1.0 + jnp.exp(-gate_part))
        silu = gate_part * sigmoid
        active = silu * up_part
        gated = active * gate
        front = gated
        for off in offsets:
            front = jnp.where(offset_ref[0] == off, pltpu.roll(gated, wide - off, 1), front)
        active_ref[l] = front.astype(BF16)
        gated = gated.astype(BF16)
        term = jnp.sum(active * grad_plain, axis=1, keepdims=True)
        grad_active = grad_plain * gate
        grad_up = (grad_active * silu).astype(BF16)
        grad_gate = (
            grad_active * up_part * sigmoid * (1.0 + gate_part * (1.0 - sigmoid))
        ).astype(BF16)
        grad_gate_ref[l], grad_up_ref[l] = grad_gate, grad_up
        out = dot(gated, wd_ref[l]).astype(BF16)
        back = (dot_nt(grad_gate, wg_ref[l][...]) + dot_nt(grad_up, wu_ref[l][...])).astype(BF16)
        for g in range(groups):
            out_ref[g, l * per : (l + 1) * per] = out[g * per : (g + 1) * per]
            dx_ref[g, l * per : (l + 1) * per] = back[g * per : (g + 1) * per]
            term_ref[g, l * per : (l + 1) * per] = jnp.broadcast_to(
                term[g * per : (g + 1) * per], (per, LANES)
            )
    for g in range(groups):
        part_ref[g] = dot(kept[g].put, out_ref[g]).astype(BF16)
        back_ref[g] = dot(kept[g].put, dx_ref[g]).astype(BF16)
        terms_ref[g] = kept[g].slot_values(term_ref[g][:, 0:1])


def whole_block(array):
    return pl.BlockSpec(array.shape, lambda i: (0,) * array.ndim)


def step_block(shape, first=1):
    return pl.BlockSpec((first,) + tuple(shape[1:]), lambda i: (i,) + (0,) * (len(shape) - 1))


SMEM = pl.BlockSpec(memory_space=pltpu.SMEM)


def constants(slots):
    at = jnp.arange(slots)
    earlier = (at[:, None] < at[None, :]) & (at[:, None] // TOK_MB == at[None, :] // TOK_MB)
    return earlier.astype(BF16), (at[:, None] == at[None, :]).astype(BF16)


def mixer_tables(slots):
    frequency = 10000.0 ** (-(jnp.arange(HD // 2, dtype=F32) * (2.0 / HD)))
    angles = jnp.arange(slots, dtype=F32)[:, None] * frequency
    cosine, sine = jnp.cos(angles), jnp.sin(angles)
    table = jnp.concatenate([cosine, cosine, -sine, sine], axis=1)
    upper = lax.reduce_precision(table, 8, 7)
    return upper.astype(BF16), (table - upper).astype(BF16)


def mixer_forward(x, meta, lengths, gain, router, wq, wkv, wo, fixed, jobs, chips, owners, collective_id):
    seqs, slots, _ = x.shape
    count, _, hc = wq.shape
    seats = slots // TOK_MB * CAP * count
    per = seats // count

    def by_expert(width):
        shape = (count, seqs * per, width)
        return shape, BF16, pl.BlockSpec((count, per, width), lambda i: (0, i, 0))

    def by_row(rows, width, dtype=BF16):
        shape = (seqs, rows, width)
        return shape, dtype, step_block(shape)

    outs = [
        by_row(slots, D), by_row(slots, D), by_expert(D), by_row(slots, hc), by_row(slots, hc),
        by_row(seats, hc), by_row(seats, hc, F32), by_expert(hc), by_row(seats, 8, F32), by_row(slots, 8, F32),
    ]
    fixed_in = [gain, router, wq, wkv, wo, *fixed]
    return pl.pallas_call(
        functools.partial(mixer_forward_kernel, count, jobs, chips, owners),
        grid=(seqs,),
        out_shape=[jax.ShapeDtypeStruct(shape, dtype) for shape, dtype, _ in outs]
        + [job.out_shape for job in jobs],
        in_specs=[SMEM, step_block(x.shape), step_block(meta.shape)]
        + [whole_block(a) for a in fixed_in]
        + [ANY] * len(jobs),
        out_specs=[spec for _, _, spec in outs] + [ANY] * len(jobs),
        scratch_shapes=Load.scratch(jobs, chips * 2),
        compiler_params=pltpu.CompilerParams(
            vmem_limit_bytes=60 * 2**20,
            collective_id=collective_id if jobs else None,
            has_side_effects=bool(jobs),
        ),
    )(lengths, x, meta, *fixed_in, *[job.src for job in jobs])


def mixer_backward(
    grad, meta, lengths, wq, wkv, wo, fixed, saved, jobs, chips, owners, collective_id
):
    seqs, slots, _ = grad.shape
    count, _, hc = wq.shape
    seats = slots // TOK_MB * CAP * count
    per = seats // count

    def by_expert(width):
        shape = (count, seqs * per, width)
        return shape, BF16, pl.BlockSpec((count, per, width), lambda i: (0, i, 0))

    def by_row(rows, width, dtype=BF16):
        shape = (seqs, rows, width)
        return shape, dtype, step_block(shape)

    outs = [
        by_row(slots, D), by_expert(D), by_row(slots, 8, F32), by_expert(hc), by_row(slots, 2 * hc)
    ]
    fixed_in = [wq, wkv, wo, *fixed]
    return pl.pallas_call(
        functools.partial(mixer_backward_kernel, count, jobs, chips, owners),
        grid=(seqs,),
        out_shape=[jax.ShapeDtypeStruct(shape, dtype) for shape, dtype, _ in outs]
        + [job.out_shape for job in jobs],
        in_specs=[SMEM, step_block(grad.shape), step_block(meta.shape)]
        + [whole_block(a) for a in fixed_in]
        + [step_block(a.shape) for a in saved]
        + [ANY] * len(jobs),
        out_specs=[spec for _, _, spec in outs] + [ANY] * len(jobs),
        scratch_shapes=Load.scratch(jobs, chips * 2),
        compiler_params=pltpu.CompilerParams(
            vmem_limit_bytes=60 * 2**20,
            collective_id=collective_id if jobs else None,
            has_side_effects=bool(jobs),
        ),
    )(lengths, grad, meta, *fixed_in, *saved, *[job.src for job in jobs])


def feed(x, cot, meta, router, wgu, wd, fixed, offset, offsets):
    groups, slots, _ = x.shape
    count, wide, _ = wd.shape
    per = slots // TOK_MB * CAP
    at_once = 2
    seats = groups * per
    shapes = [((groups, slots, D), BF16), ((groups, slots, D), BF16)]
    specs = [step_block(s, at_once) for s, _ in shapes]
    for width in (D, D, wide, wide, wide):
        shapes.append(((count, seats, width), BF16))
        specs.append(pl.BlockSpec((count, at_once * per, width), lambda i: (0, i, 0)))
    for _ in range(2):
        shapes.append(((groups, slots, 8), F32))
        specs.append(step_block(shapes[-1][0], at_once))
    fixed_in = [router, wd, *fixed, *wgu]
    turns = sorted({o for o in offsets if o})
    return pl.pallas_call(
        functools.partial(feed_kernel, count, at_once, turns),
        grid=(groups // at_once,),
        out_shape=[jax.ShapeDtypeStruct(*s) for s in shapes],
        in_specs=[SMEM]
        + [step_block(a.shape, at_once) for a in (x, cot, meta)]
        + [whole_block(a) for a in fixed_in],
        out_specs=specs,
        scratch_shapes=[
            pltpu.VMEM((at_once, count * per, D), BF16),
            pltpu.VMEM((at_once, count * per, D), BF16),
            pltpu.VMEM((count, at_once * per, LANES), F32),
            pltpu.VMEM((at_once, count * per, LANES), F32),
        ],
        compiler_params=pltpu.CompilerParams(vmem_limit_bytes=60 * 2**20),
    )(offset.reshape(1), x, cot, meta, *fixed_in)


def norm_forward(values, norm_gain):
    inverse = lax.rsqrt(jnp.mean(values * values, axis=-1, keepdims=True) + EPSILON)
    return (values * inverse * norm_gain, inverse)


def norm_backward(values, inverse, norm_gain, grad_normed):
    scaled = grad_normed * norm_gain
    grad_gain = jnp.sum(grad_normed * values * inverse, axis=(0, 1))
    grad_values = inverse * scaled - values * inverse**3 * jnp.mean(
        scaled * values, axis=-1, keepdims=True
    )
    return (grad_values, grad_gain)


def gate_grads(gate_probs, grad_gate_probs, routes):
    weighted = jnp.sum(gate_probs * grad_gate_probs, axis=-1, keepdims=True)
    grad_picked = gate_probs * (grad_gate_probs - weighted)
    choose = (routes[..., None] == jnp.arange(NEXP, dtype=jnp.int32)).astype(F32)
    return jnp.sum(grad_picked[..., None] * choose, axis=-2)


def tile_starts(shards):
    share = FF // shards
    most = max(share * d % LANES for d in range(shards))
    tiles = -(-(share + most) // LANES)
    starts = [min(share * d // LANES, FF // LANES - tiles) for d in range(shards)]
    return tiles, starts, [share * d - LANES * starts[d] for d in range(shards)]


def put_together_kernel(count, starts, tiles, *refs):
    out_ref = refs[-1]
    edges = sorted(set(starts) | {s + tiles for s in starts})
    for l in range(count):
        for g in range(2):
            part = refs[l * 2 + g]
            for low, high in zip(edges[:-1], edges[1:]):
                cover = [d for d in range(len(starts)) if starts[d] <= low and high <= starts[d] + tiles]
                value = None
                for d in cover:
                    cut = slice((low - starts[d]) * LANES, (high - starts[d]) * LANES)
                    term = part[d, :, cut].astype(F32)
                    value = term if value is None else value + term
                out_ref[l, :, g * FF + low * LANES : g * FF + high * LANES] = value


def put_together(parts, count, starts, tiles):
    n_dp, depth, wide = parts[0].shape
    rows = 32
    return pl.pallas_call(
        functools.partial(put_together_kernel, count, starts, tiles),
        grid=(depth // rows,),
        out_shape=jax.ShapeDtypeStruct((count, depth, 2 * FF), F32),
        in_specs=[pl.BlockSpec((n_dp, rows, wide), lambda i: (0, i, 0))] * len(parts),
        out_specs=pl.BlockSpec((count, rows, 2 * FF), lambda i: (0, i, 0)),
        compiler_params=pltpu.CompilerParams(vmem_limit_bytes=48 * 2**20),
    )(*parts)


def product(pattern, operand, factor):
    return jnp.einsum(pattern, operand, factor, preferred_element_type=F32)


def shards(
    tokens, lengths, attention_routes, feedforward_routes, norm_gains, router_weight,
    key_value_weight, query_weight, output_weight, input_weight, down_weight, cotangent,
):
    n_dp = lax.axis_size("dp")
    owners = lax.axis_size("expert")
    chips = n_dp // 2
    devices = n_dp * owners
    dp = lax.axis_index("dp")
    ex = lax.axis_index("expert")
    me = dp * owners + ex
    mb = tokens.shape[0]
    count = NEXP // owners
    seqs = mb * n_dp
    slots = owners * TOK_MB
    hc = KVH // n_dp * HD
    att = KVH * HD
    depth = D // n_dp
    slice_rows = D // devices
    tiles, starts, offsets = tile_starts(n_dp)
    share, wide = FF // n_dp, tiles * LANES
    offset = jnp.array(offsets, jnp.int32)[dp]

    def query_job(l):
        return Job(
            query_weight,
            jax.ShapeDtypeStruct((D, hc), BF16),
            lambda src, d: src.at[l, :, pl.ds(pl.multiple_of(d * hc, LANES), hc)],
            lambda out, d: out.at[pl.ds(pl.multiple_of(d * depth, depth), depth)],
        )

    key_value_job = Job(
        jnp.swapaxes(key_value_weight.reshape(slice_rows, 2, att), 0, 1),
        jax.ShapeDtypeStruct((n_dp, owners, 2, slice_rows, hc), BF16),
        lambda src, d: src.at[:, :, pl.ds(pl.multiple_of(d * hc, LANES), hc)],
        lambda out, d: out.at[d, lax.axis_index("expert")],
    )

    def start_of(d):
        start = (share * d) // LANES
        if max(share * i // LANES - starts[i] for i in range(n_dp)):
            start = jnp.minimum(start, FF // LANES - tiles)
        return start

    def input_job(l, g):
        return Job(
            input_weight,
            jax.ShapeDtypeStruct((D, wide), BF16),
            lambda src, d: src.at[
                l, :, pl.ds(pl.multiple_of(g * FF + start_of(d) * LANES, LANES), wide)
            ],
            lambda out, d: out.at[pl.ds(pl.multiple_of(d * depth, depth), depth)],
        )

    def back_job(grad):
        return Job(
            grad,
            jax.ShapeDtypeStruct((n_dp, depth, grad.shape[1]), BF16),
            lambda src, d: src.at[pl.ds(pl.multiple_of(d * depth, depth), depth)],
            lambda out, d: out.at[d],
        )

    def spread_jobs(jobs, places):
        lists = [[] for _ in range(places)]
        for i, job in enumerate(jobs):
            lists[i * places // len(jobs)].append(job)
        return lists

    input_lists = spread_jobs([input_job(l, g) for l in range(count) for g in range(2)], 4)
    input_lists[2] += input_lists.pop()
    down_full = lax.dynamic_update_slice(
        jnp.zeros((count, wide, D), BF16), down_weight, (0, offset, 0)
    )

    def route_lines(routes):
        return jnp.swapaxes(routes[:, 0], 1, 2).reshape(-1, LANES).astype(F32)

    shared = jnp.concatenate([norm_gains, router_weight], axis=1).astype(F32)
    tail = jnp.concatenate([shared.reshape(-1), lengths.reshape(-1).astype(F32)])
    tail = jnp.pad(tail, (0, -tail.shape[0] % LANES)).reshape(-1, LANES)
    small = jnp.concatenate(
        [route_lines(attention_routes), route_lines(feedforward_routes), tail]
    )
    small = jnp.pad(small, ((0, -small.shape[0] % 8), (0, 0)))[None]
    tokens_all, cot_all, small, *resharded = gather_all(
        [tokens[:, 0], cotangent[:, 0]], [True, False], chips, owners, 1,
        [query_job(l) for l in range(count)] + [key_value_job], [small],
    )
    tokens_all = tokens_all.reshape(seqs, slots, D)
    query_full = jnp.stack(resharded[:-1])
    key_value_full = jnp.transpose(resharded[-1], (0, 1, 3, 2, 4)).reshape(D, 2 * hc)
    group_slots = mb * TOK_MB * 2
    groups = devices // 2
    cot_all = cot_all.reshape(groups, group_slots, D)
    lines = mb * 2 * TOK_MB // LANES
    mixer_routes = small[:, :lines].reshape(n_dp, owners, mb, 2, TOK_MB)
    mixer_meta = jnp.transpose(mixer_routes, (2, 0, 3, 1, 4)).reshape(seqs, 2, slots)
    mixer_meta = jnp.pad(mixer_meta, ((0, 0), (0, 6), (0, 0)))
    feed_routes = small[:, lines : 2 * lines].reshape(groups, 2, mb, 2, TOK_MB)
    feed_meta = jnp.transpose(feed_routes, (0, 3, 1, 2, 4)).reshape(groups, 2, group_slots)
    tail = small[:, 2 * lines :].reshape(devices, -1)
    shared_all = tail[:, : slice_rows * 18].reshape(D, 18)
    all_lengths = tail[:, slice_rows * 18 : slice_rows * 18 + mb].reshape(n_dp, owners, mb)
    row_lengths = all_lengths[:, 0].T.reshape(seqs).astype(jnp.int32)
    places = (jnp.arange(owners)[:, None, None] * TOK_MB + jnp.arange(TOK_MB)).astype(F32)
    valid = (places[None] < all_lengths[..., None]).astype(F32).reshape(groups, 1, group_slots)
    feed_meta = jnp.concatenate([feed_meta, valid], axis=1)
    feed_meta = jnp.pad(feed_meta, ((0, 0), (0, 5), (0, 0)))
    gain_mixer, gain_feed = shared_all[:, 0], shared_all[:, 1]
    router_mixer, router_feed = shared_all[:, 2 : 2 + NEXP], shared_all[:, 2 + NEXP :]

    def routers(part):
        return jnp.pad(part.astype(BF16), ((0, 0), (0, LANES - NEXP)))

    own_tokens = tokens[:, 0].astype(F32)
    home_places = ex * TOK_MB + jnp.arange(TOK_MB, dtype=jnp.int32)
    own_valid = (home_places[None, :] < lengths[:, :1]).astype(F32)
    own_cotangent = cotangent[:, 0].astype(F32) * own_valid[..., None]

    normed_mixer, inverse_mixer = norm_forward(own_tokens, gain_mixer)
    fixed = constants(slots)
    tables = mixer_tables(slots)
    (
        mixer_all, mixer_part, rows_mixer, keys, values, queries, mixture, mixture_gated, info,
        gates_mixer, *input_parts,
    ) = mixer_forward(
        tokens_all, mixer_meta, row_lengths, gain_mixer[None], routers(router_mixer), query_full,
        key_value_full, output_weight, (*fixed, *tables), input_lists[0], chips, owners, 2,
    )
    mixer_sum, *more_parts = scatter_sum(
        mixer_part.reshape(mb, devices, TOK_MB, D), chips, owners, True, 10, input_lists[1]
    )
    input_parts += more_parts

    second = own_tokens + mixer_sum
    normed_feed, inverse_feed = norm_forward(second, gain_feed)
    feed_all, *more_parts = gather_all(
        [normed_feed.astype(BF16)], [False], chips, owners, 3, input_lists[2]
    )
    input_parts += more_parts
    feed_all = feed_all.reshape(groups, group_slots, D)
    (
        feed_part, grad_feed_part, rows_feed, cot_rows, active_gated, grad_gate, grad_up,
        gate_terms_feed, gates_feed,
    ) = feed(
        feed_all, cot_all, feed_meta, routers(router_feed), input_parts, down_full,
        constants(group_slots), offset, offsets,
    )
    back_lists = []
    for l in range(count):
        for grad in (grad_gate, grad_up):
            back_lists.append(product("rd,rf->df", rows_feed[l], grad[l]).astype(BF16))
    back_lists = spread_jobs([back_job(grad) for grad in back_lists], 4)
    grad_down = product("lrf,lrd->lfd", active_gated[..., :share], cot_rows)

    def home_parts(terms, by_row):
        terms = terms[..., :2]
        if by_row:
            terms = jnp.swapaxes(terms.reshape(mb, devices, TOK_MB * 2), 0, 1)
        terms = terms.reshape(devices, -1, LANES)
        return jnp.pad(terms, ((0, 0), (0, -terms.shape[1] % 8), (0, 0)))

    def at_home(parts):
        return jnp.sum(parts, axis=0).reshape(-1)[: mb * TOK_MB * 2].reshape(mb, TOK_MB, 2)

    def own_of(gates, by_row):
        gates = gates[..., :2]
        if by_row:
            return lax.dynamic_index_in_dim(
                gates.reshape(mb, devices, TOK_MB, 2), me, 1, keepdims=False
            )
        return lax.dynamic_index_in_dim(
            gates.reshape(devices, mb, TOK_MB, 2), me, 0, keepdims=False
        )

    grad_normed_feed, *grad_input_parts, terms = scatter_sum(
        grad_feed_part.reshape(devices, mb, TOK_MB, D), chips, owners, False, 20, back_lists[0],
        [home_parts(gate_terms_feed, False)],
    )
    grad_logits_feed = gate_grads(
        own_of(gates_feed, False), at_home(terms), feedforward_routes[:, 0]
    )
    grad_normed_feed = grad_normed_feed + product("mte,de->mtd", grad_logits_feed, router_feed)
    grad_second, grad_gain_feed = norm_backward(second, inverse_feed, gain_feed, grad_normed_feed)
    grad_second = grad_second + own_cotangent

    grad_all, *more_parts = gather_all(
        [grad_second.astype(BF16)], [True], chips, owners, 5, back_lists[1]
    )
    grad_input_parts += more_parts
    grad_all = grad_all.reshape(seqs, slots, D)
    feed_sum, *more_parts = scatter_sum(
        feed_part.reshape(devices, mb, TOK_MB, D), chips, owners, False, 30, back_lists[2]
    )
    grad_input_parts += more_parts
    result = (second + feed_sum).astype(BF16)[:, None]
    (
        grad_mixer_part, grad_rows, gate_terms_mixer, grad_query_pre, grad_key_value, *more_parts
    ) = mixer_backward(
        grad_all, mixer_meta, row_lengths, query_full, key_value_full, output_weight,
        (*fixed, *tables), (keys, values, queries, mixture, info), back_lists[3], chips, owners, 6,
    )
    grad_input_parts += more_parts
    grad_output = product("lrc,lrd->lcd", mixture_gated, grad_rows)
    grad_query = [
        product("rd,rc->dc", rows_mixer[l], grad_query_pre[l]).astype(BF16) for l in range(count)
    ]
    grad_key_value_w = product("std,stc->dc", mixer_all, grad_key_value).astype(BF16)
    grad_normed_mixer, *more_parts = scatter_sum(
        grad_mixer_part.reshape(mb, devices, TOK_MB, D), chips, owners, True, 40,
        [back_job(grad) for grad in grad_query],
        [
            home_parts(gate_terms_mixer, True),
            grad_key_value_w.reshape(devices, slice_rows, 2 * hc),
        ],
    )
    *more_parts, terms, grad_key_value_w = more_parts
    grad_query = jnp.stack(more_parts, axis=1)
    grad_key_value_w = jnp.sum(
        grad_key_value_w.astype(F32).reshape(n_dp, owners, slice_rows, 2, hc), axis=1
    )
    grad_key_value_w = jnp.transpose(grad_key_value_w, (1, 2, 0, 3)).reshape(slice_rows, 2 * att)
    grad_logits_mixer = gate_grads(
        own_of(gates_mixer, True), at_home(terms), attention_routes[:, 0]
    )
    grad_normed_mixer = grad_normed_mixer + product("mte,de->mtd", grad_logits_mixer, router_mixer)
    grad_tokens, grad_gain_mixer = norm_backward(
        own_tokens, inverse_mixer, gain_mixer, grad_normed_mixer
    )
    grad_tokens = (grad_tokens + grad_second).astype(BF16)[:, None]

    router_terms = [
        product("mtd,mte->de", normed.astype(BF16), logits.astype(BF16))
        for normed, logits in ((normed_mixer, grad_logits_mixer), (normed_feed, grad_logits_feed))
    ]
    last = jnp.concatenate([grad_gain_mixer[:, None], grad_gain_feed[:, None], *router_terms], axis=1)
    last = last.reshape(devices, slice_rows * 18)
    last = jnp.pad(last, ((0, 0), (0, -last.shape[1] % (8 * LANES)))).reshape(devices, -1, LANES)
    last = jnp.sum(exchange(last, chips, owners, 8), axis=0).reshape(-1)
    last = last[: slice_rows * 18].reshape(slice_rows, 18)
    grad_gains, grad_router = last[:, :2], last[:, 2:]

    grad_query = jnp.transpose(grad_query.astype(F32), (1, 2, 0, 3)).reshape(count, depth, att)
    grad_input = put_together(grad_input_parts, count, starts, tiles)
    return (
        result, grad_tokens, grad_gains, grad_router, grad_key_value_w, grad_query,
        grad_output, grad_input, grad_down,
    )


def solution(mesh):
    shared = P(("dp", "expert"), None)
    slots = P(None, "dp", "expert", None)
    owned = P("expert", "dp", None)
    return jax.shard_map(
        shards,
        mesh=mesh,
        in_specs=(slots, P(None, "dp"), slots, slots, shared, shared, shared) + (owned,) * 4 + (slots,),
        out_specs=(slots, slots, shared, shared, shared) + (owned,) * 4,
        check_vma=False,
    )
```

time: 1980 us -> 1440 us (0.73)
  matrix products: 406 us -> 86.1 us
  local copies, waits for them, and re-layouts: 187 us -> 53.8 us
  other arithmetic: 130 us -> 31.7 us
  Pallas kernels: 1180 us -> 1260 us
  starting transfers between devices: 20.8 us -> 0 us
  blocking collectives: 20.5 us -> 0 us
    dot_general x36 -> x13, matrix products: 406 us -> 86.1 us  [product(): return jnp.einsum(pattern, operand, factor, preferred_element_type=F32)]
    pallas_call x8, Pallas kernels: 644 us -> 803 us  [the longest x3 506 us: gather_all(): pl.pallas_call(functools.partial(gather_kernel, chips, first, second, ord...]
    pallas_call x4, Pallas kernels: 531 us -> 458 us  [call(): pl.pallas_call(functools.partial(scatter_kernel, chips, first, second, by...]
    unnamed x31 -> x6, other arithmetic: 37.3 us -> 3.38 us
    transpose x19 -> x1, local copies, waits for them, and re-layouts: 29.1 us -> 2.19 us  [shards(): jnp.transpose(resharded[-1], (0, 1, 3, 2, 4)).reshape(D, 2 * hc)]
    unnamed x194 -> x77, local copies, waits for them, and re-layouts: 36.4 us -> 11.4 us
    convert_element_type x12 -> x8, other arithmetic: 28.1 us -> 4.42 us  [the longest x2 1.37 us: route_lines(): return jnp.swapaxes(routes[:, 0], 1, 2).reshape(-1, LANES).astype(F32)]
    all_to_all x4 -> x0, starting transfers between devices: 20.7 us -> none  [the longest x1 6.33 us: shards(): grad_input_parts = lax.all_to_all(grad_input_parts, 'dp', 0, 0, tiled=True)]
  transfers between devices with their start and end apart: 6 -> 0, of which waited for: 1 -> 0; matrix products, arithmetic and copies ran while one was open for 25% -> 0% of each run, Pallas kernels for 51% -> 0%
where the time goes in v2:
time: 1440 us
  Pallas kernels  1260 us (88%)
  matrix products  86.1 us (6%)
  local copies, waits for them, and re-layouts  53.8 us (4%)
  other arithmetic  31.7 us (2%)
    pallas_call x3, Pallas kernels, gather_all(): pl.pallas_call(functools.partial(gather_kernel, chips, first, second, ord...  506 us
    pallas_call x4, Pallas kernels, call(): pl.pallas_call(functools.partial(scatter_kernel, chips, first, second, by...  458 us
    pallas_call x1, Pallas kernels, feed(): pl.pallas_call(functools.partial(feed_kernel, count, at_once, turns), gri...  123 us
    dot_general x13, matrix products, product(): return jnp.einsum(pattern, operand, factor, preferred_element_type=F32)  86.1 us
    pallas_call x1, Pallas kernels, mixer_forward(): pl.pallas_call(functools.partial(mixer_forward_kernel, count, jobs, chips...  75 us
    pallas_call x1, Pallas kernels, mixer_backward(): pl.pallas_call(functools.partial(mixer_backward_kernel, count, jobs, chip...  71.4 us

profile of v2, /device:TPU:1, one launch (start us, length us, event | category | flops | bytes accessed | tf_op | source)
XLA Modules:
  0.0 1436.3 jit_solution(11033540414566220849)
XLA Ops:
  6.3 209.0 %shard_map.196 = (bf16[2,32,64,2048]{3,2,1,0:T(8,128)(2,1)}, bf16[32,2,64,2048]{3,2,1,0:T(8,128)(2,1)}, f32[32,16,128]{2,1,0:T(8,128)}, bf16[2048,256]{1,0:T(8,1...) custom-call(bf16[2,64,2048]{2,1,0:T(8,128)(2,1)} %bitcast.195, bf16[2,64,2048]{2,1,0:T(8,128)(2,1)} %bitcast.196, ...), custom_call_target="tpu_custom_call" | custom-call | tf_op jit(solution)/shard_map/pallas_call | solution.py:413
  233.3 75.0 %shard_map.197 = (bf16[16,256,2048]{2,1,0:T(8,128)(2,1)}, bf16[16,256,2048]{2,1,0:T(8,128)(2,1)}, bf16[2,1536,2048]{2,1,0:T(8,128)(2,1)}, bf16[16,256,256]{2,1,0...) custom-call(s32[16]{0:T(128)} %convert_element_type.176.refs_0_, ...), custom_call_target="tpu_custom_call" | custom-call | tf_op jit(solution)/shard_map/pallas_call | solution.py:1012
  308.3 108.0 %shard_map.198 = (f32[2,64,2048]{2,1,0:T(8,128)}, bf16[2048,768]{1,0:T(8,128)(2,1)}) custom-call(bf16[2,32,64,2048]{3,2,1,0:T(8,128)(2,1)} %bitcast.187, bf16[2,256,11264]{2,1,0:T(8,128)(2,1)} %refs_2_.1), custom_call_target="tpu_custom_call" | custom-call | tf_op jit(solution)/shard_map/pallas_call | solution.py:606
  419.5 164.9 %shard_map.199 = (bf16[32,2,64,2048]{3,2,1,0:T(8,128)(2,1)}, bf16[2048,768]{1,0:T(8,128)(2,1)}, bf16[2048,768]{1,0:T(8,128)(2,1)}) custom-call(bf16[2,64,2048]{2,1,0:T(8,128)(2,1)} %multiply_convert_fusion.refs_0_, bf16[2,256,11264]{2,1,0:T(8,128)(2,1)} %refs_2_.1, bf16[2,256,11264]{2,1,0:T(8,128)(2,1)} %refs_2_.1), custom_call_target="tpu_custom_call" | custom-call | tf_op jit(solution)/shard_map/pallas_call | solution.py:413
  590.4 6.2 constant_dynamic-update-slice_fusion.wd_ref
  598.8 122.6 %shard_map.200 = (bf16[16,256,2048]{2,1,0:T(8,128)(2,1)}, bf16[16,256,2048]{2,1,0:T(8,128)(2,1)}, bf16[2,1536,2048]{2,1,0:T(8,128)(2,1)}, bf16[2,1536,2048]{2,1,...) custom-call(s32[1]{0:T(128)} %dynamic_slice.11.offset_ref, ...), custom_call_target="tpu_custom_call" | custom-call | tf_op jit(solution)/shard_map/pallas_call | solution.py:1085
  721.4 16.3 %fusion.18 = f32[2,704,2048]{2,1,0:T(8,128)} fusion(bf16[2,1536,2048]{2,1,0:T(8,128)(2,1)} %get-tuple-element.106, bf16[2,1536,768]{2,1,0:T(8,128)(2,1)} %get-tuple-element.105), kind=kOutput, calls=%fused_computation.18 | convolution fusion | flops 8858370048 | bytes 28835840 | tf_op jit(solution)/shard_map/lrf,lrd->lfd/dot_general | solution.py:1162
  737.7 9.5 fusion.20.refs_1_
  747.2 117.9 %shard_map.201 = (f32[2,64,2048]{2,1,0:T(8,128)}, bf16[8,256,768]{2,1,0:T(8,128)(2,1)}) custom-call(bf16[32,2,64,2048]{3,2,1,0:T(8,128)(2,1)} %bitcast.189, bf16[2048,768]{1,0:T(8,128)(2,1)} %fusion.20.refs_1_), custom_call_target="tpu_custom_call" | custom-call | tf_op jit(solution)/shard_map/pallas_call | solution.py:606
  865.2 9.8 fusion.23.refs_15_
  875.0 9.7 fusion.29.refs_1_
  884.7 6.7 fusion.26.refs_1_
  894.9 102.8 %shard_map.202 = (f32[2,64,2048]{2,1,0:T(8,128)}, bf16[8,256,768]{2,1,0:T(8,128)(2,1)}, f32[32,8,128]{2,1,0:T(8,128)}) custom-call(bf16[32,2,64,2048]{3,2,1,0:T(8,128)(2,1)} %bitcast.188, bf16[2048,768]{1,0:T(8,128)(2,1)} %fusion.26.refs_1_, f32[32,8,128]{2,1,0:T(8,128)} %pad.40.refs_2_), custom_call_target="tpu_custom_call" | custom-call | tf_op jit(solution)/shard_map/pallas_call | solution.py:606
  1004.6 132.3 %shard_map.203 = (bf16[2,32,64,2048]{3,2,1,0:T(8,128)(2,1)}, bf16[8,256,768]{2,1,0:T(8,128)(2,1)}) custom-call(bf16[2,64,2048]{2,1,0:T(8,128)(2,1)} %fusion.86.refs_0_, bf16[2048,768]{1,0:T(8,128)(2,1)} %fusion.29.refs_1_), custom_call_target="tpu_custom_call" | custom-call | tf_op jit(solution)/shard_map/pallas_call | solution.py:413
  1136.9 71.4 %shard_map.204 = (bf16[16,256,2048]{2,1,0:T(8,128)(2,1)}, bf16[2,1536,2048]{2,1,0:T(8,128)(2,1)}, f32[16,256,8]{2,1,0:T(8,128)}, bf16[2,1536,256]{2,1,0:T(8,128)...) custom-call(s32[16]{0:T(128)} %convert_element_type.176.refs_0_, bf16[16,256,2048]{2,1,0:T(8,128)(2,1)} %bitcast.186, ...), custom_call_target="tpu_custom_call" | custom-call | tf_op jit(solution)/shard_map/pallas_call | solution.py:1050
  1208.4 15.8 %shard_map.207 = f32[2,256,11264]{2,1,0:T(8,128)} custom-call(bf16[8,256,768]{2,1,0:T(8,128)(2,1)S(1)} %copy-done, bf16[8,256,768]{2,1,0:T(8,128)(2,1)} %get-tuple-element.102.refs_1_, bf16[8,256,768]{2,1,0:T(8,128)(2,1)} %get-tuple-element.103.refs_2_, bf16[8,256,768]{2,1,0:T(8,128)(2,1)} %get-tuple-element.104.refs_3_), custom_call_target="tpu_custom_call" | custom-call | tf_op jit(solution)/shard_map/pallas_call | solution.py:1151
  1224.2 6.6 fusion.102
  1230.8 15.0 %bitcast_convert_fusion = bf16[2048,512]{1,0:T(8,128)(2,1)} fusion(bf16[16,256,2048]{2,1,0:T(8,128)(2,1)} %get-tuple-element.91, bf16[16,256,512]{2,1,0:T(8,128)(2,1)} %get-tuple-element.92), kind=kOutput, calls=%fused_computation.20 | convolution fusion | flops 8590983168 | bytes 23068672 | tf_op jit(solution)/shard_map/std,stc->dc/dot_general | solution.py:1162
  1253.7 129.1 %shard_map.205 = (f32[2,64,2048]{2,1,0:T(8,128)}, bf16[8,256,256]{2,1,0:T(8,128)(2,1)}, bf16[8,256,256]{2,1,0:T(8,128)(2,1)}, f32[32,8,128]{2,1,0:T(8,128)}, bf16[32,64,512]{2,1,0:T(8,128)(2,1)}) custom-call(bf16[2,32,64,2048]{3,2,1,0:T(8,128)(2,1)} %bitcast.185, bf16[2048,256]{1,0:T(8,128)(2,1)} %fusion.32.refs_1_, bf16[2048,256]{1,0:T(8,128)(2,1)} %fusion.35.refs_2_, ...), custom_call_target="tpu_custom_call" | custom-call | tf_op jit(solution)/shard_map/pallas_call | solution.py:606
  1386.6 5.4 copy.118
  1392.0 5.5 copy.125
  1405.3 12.2 shard_map.206
  1423.4 5.4 reshape.409
  1428.8 4.8 reduce_sum.139
  (166 shorter events, 70.7 us)
Async XLA Ops:
  217.5 782.5 %copy-start.1 = (f32[2048,18]{1,0:T(8,128)}, f32[2048,18]{1,0:T(8,128)S(1)}, u32[]{:S(2)}) copy-start(f32[2048,18]{1,0:T(8,128)S(1)} %reshape.380) | copy-start | bytes 442372
  308.3 108.0 %copy-start.7 = (bf16[2,1,64,2048]{3,2,1,0:T(8,128)(2,1)S(1)}, bf16[2,1,64,2048]{3,2,1,0:T(8,128)(2,1)}, u32[]{:S(2)}) copy-start(bf16[2,1,64,2048]{3,2,1,0:T(8,128)(2,1)} %param.13) | copy-start | bytes 1572868
  418.4 583.6 %copy-start.3 = (f32[2,64,2048]{2,1,0:T(8,128)}, f32[2,64,2048]{2,1,0:T(8,128)S(1)}, u32[]{:S(2)}) copy-start(f32[2,64,2048]{2,1,0:T(8,128)S(1)} %get-tuple-element.159) | copy-start | bytes 3145732
  419.5 164.9 %copy-start.20 = (s32[8]{0:T(128)S(1)}, s32[8]{0:T(128)}, u32[]{:S(2)}) copy-start(s32[8]{0:T(128)} %constant.82.clone) | copy-start | bytes 100
  721.4 16.3 %copy-start.18 = (bf16[2,1536,768]{2,1,0:T(8,128)(2,1)S(1)}, bf16[2,1536,768]{2,1,0:T(8,128)(2,1)}, u32[]{:S(2)}) copy-start(bf16[2,1536,768]{2,1,0:T(8,128)(2,1)} %get-tuple-element.73) | copy-start | bytes 14155780
  747.2 127.8 %slice-start.11 = ((s8[4718592]{0:T(1024)(128)(4,1)}), s8[524288]{0:T(1024)(128)(4,1)S(1)}, s32[]{:S(2)}) async-start(s8[4718592]{0:T(1024)(128)(4,1)} %bitcast.236), calls=%async_computation.11 | async-start | bytes 1048576
  865.1 9.8 slice-start.12
  865.1 19.6 %slice-start.6 = ((s8[12582912]{0:T(1024)(128)(4,1)}), s8[4194304]{0:T(1024)(128)(4,1)S(1)}, s32[]{:S(2)}) async-start(s8[12582912]{0:T(1024)(128)(4,1)} %bitcast.232), calls=%async_computation.6 | async-start | bytes 8388608
  865.1 19.5 %slice-start.7 = ((s8[12582912]{0:T(1024)(128)(4,1)}), s8[4194304]{0:T(1024)(128)(4,1)S(1)}, s32[]{:S(2)}) async-start(s8[12582912]{0:T(1024)(128)(4,1)} %bitcast.232), calls=%async_computation.7 | async-start | bytes 8388608
  865.1 19.5 %slice-start.9 = ((s8[4718592]{0:T(1024)(128)(4,1)}), s8[4194304]{0:T(1024)(128)(4,1)S(1)}, s32[]{:S(2)}) async-start(s8[4718592]{0:T(1024)(128)(4,1)} %bitcast.234), calls=%async_computation.9 | async-start | bytes 8388608
  875.0 9.7 slice-start.8
  875.0 9.7 slice-start.10
  894.9 105.0 %copy-start.14 = (s32[2,1,64,2]{2,3,1,0:T(2,128)S(1)}, s32[2,1,64,2]{2,3,1,0:T(2,128)}, u32[]{:S(2)}) copy-start(s32[2,1,64,2]{2,3,1,0:T(2,128)} %param.16) | copy-start | bytes 3076
  1001.9 135.0 %copy-start.5 = (f32[2,64,2048]{2,1,0:T(8,128)}, f32[2,64,2048]{2,1,0:T(8,128)S(1)}, u32[]{:S(2)}) copy-start(f32[2,64,2048]{2,1,0:T(8,128)S(1)} %get-tuple-element.176) | copy-start | bytes 3145732
  1136.9 71.4 %copy-start = (bf16[8,256,768]{2,1,0:T(8,128)(2,1)S(1)}, bf16[8,256,768]{2,1,0:T(8,128)(2,1)}, u32[]{:S(2)}) copy-start(bf16[8,256,768]{2,1,0:T(8,128)(2,1)} %get-tuple-element.101.refs_0_) | copy-start | bytes 9437188
  1208.3 15.9 %slice-start = ((s8[12582912]{0:T(1024)(128)(4,1)}), s8[4194304]{0:T(1024)(128)(4,1)S(1)}, s32[]{:S(2)}) async-start(s8[12582912]{0:T(1024)(128)(4,1)} %bitcast.183), calls=%async_computation | async-start | bytes 8388608
  1208.3 15.9 %slice-start.1 = ((s8[12582912]{0:T(1024)(128)(4,1)}), s8[4194304]{0:T(1024)(128)(4,1)S(1)}, s32[]{:S(2)}) async-start(s8[12582912]{0:T(1024)(128)(4,1)} %bitcast.183), calls=%async_computation.1 | async-start | bytes 8388608
  1208.4 15.8 %slice-start.2 = ((s8[12582912]{0:T(1024)(128)(4,1)}), s8[4194304]{0:T(1024)(128)(4,1)S(1)}, s32[]{:S(2)}) async-start(s8[12582912]{0:T(1024)(128)(4,1)} %bitcast.183), calls=%async_computation.2 | async-start | bytes 8388608
  1224.2 21.6 %slice-start.3 = ((s8[12582912]{0:T(1024)(128)(4,1)}), s8[4194304]{0:T(1024)(128)(4,1)S(1)}, s32[]{:S(2)}) async-start(s8[12582912]{0:T(1024)(128)(4,1)} %bitcast.230), calls=%async_computation.3 | async-start | bytes 8388608
  1224.2 21.6 %slice-start.4 = ((s8[12582912]{0:T(1024)(128)(4,1)}), s8[4194304]{0:T(1024)(128)(4,1)S(1)}, s32[]{:S(2)}) async-start(s8[12582912]{0:T(1024)(128)(4,1)} %bitcast.230), calls=%async_computation.4 | async-start | bytes 8388608
  1230.8 15.0 %slice-start.5 = ((s8[12582912]{0:T(1024)(128)(4,1)}), s8[4194304]{0:T(1024)(128)(4,1)S(1)}, s32[]{:S(2)}) async-start(s8[12582912]{0:T(1024)(128)(4,1)} %bitcast.230), calls=%async_computation.5 | async-start | bytes 8388608
  1230.8 15.0 %copy-start.19 = (bf16[2,1536,256]{2,1,0:T(8,128)(2,1)S(1)}, bf16[2,1536,256]{2,1,0:T(8,128)(2,1)}, u32[]{:S(2)}) copy-start(bf16[2,1536,256]{2,1,0:T(8,128)(2,1)} %get-tuple-element.89) | copy-start | bytes 4718596
  1399.2 20.9 %copy-start.4 = (f32[2,64,2048]{2,1,0:T(8,128)S(1)}, f32[2,64,2048]{2,1,0:T(8,128)}, u32[]{:S(2)}) copy-start(f32[2,64,2048]{2,1,0:T(8,128)} %copy-done.3) | copy-start | bytes 3145732
  1399.2 20.9 %copy-start.6 = (f32[2,64,2048]{2,1,0:T(8,128)S(1)}, f32[2,64,2048]{2,1,0:T(8,128)}, u32[]{:S(2)}) copy-start(f32[2,64,2048]{2,1,0:T(8,128)} %copy-done.5) | copy-start | bytes 3145732
  (10 other events, 65.5 us)

commit v3 on v2

--- a/solution.py
+++ b/solution.py
@@ -9,7 +9,6 @@
 
 MESH = pl.DeviceIdType.MESH
 BF16 = jnp.bfloat16
-START = 1
 F32 = jnp.float32
 ANY = pl.BlockSpec(memory_space=pl.ANY)
 
@@ -134,34 +133,6 @@
         return [sem((len(jobs),)), sem((len(jobs), n_dp)), sem((len(jobs), n_dp))]
 
 
-class Carried:
-    def __init__(self, jobs, chips, owners, refs, ins, outs):
-        first, second = expert_factors(owners)
-        n = len(jobs)
-        refs = list(refs)
-        srcs = refs[ins : ins + n]
-        results = refs[ins + n + outs : ins + 2 * n + outs]
-        sems = refs[len(refs) - 3 :] if n else []
-        kept = refs[:ins] + refs[ins + n : ins + n + outs] + refs[ins + 2 * n + outs :]
-        self.refs = kept[: len(kept) - 3] if n else kept
-        self.jobs = jobs
-        if n:
-            self.me = Place(chips, first, second)
-            self.load = Load(jobs, self.me, srcs, results, sems)
-
-    def start(self):
-        if self.jobs:
-
-            @pl.when(pl.program_id(0) == 0)
-            def _():
-                self.me.greet("column")
-                self.load.start()
-
-    def finish(self):
-        if self.jobs:
-            pl.when(pl.program_id(0) == pl.num_programs(0) - 1)(self.load.finish)
-
-
 class Mail:
     def __init__(self, arrays, me, srcs, outs, sems):
         self.arrays, self.me, self.srcs, self.outs = arrays, me, srcs, outs
@@ -244,13 +215,19 @@
         copy = remote(
             src, self.piece(blk, h), self.sends.at[len(self.pending)], self.recv.at[blk, h], target
         )
-        self.pending.append((copy, when))
-        copy.start() if when is None else pl.when(when)(copy.start)
+        self.pending.append(when)
+        copy.start() if when is None else pl.when(when())(copy.start)
 
     def landed(self, blk, h, when=None):
         there = self.piece(blk, h)
         copy = remote(there, there, self.sends.at[0], self.recv.at[blk, h], self.me.at())
-        copy.wait_recv() if when is None else pl.when(when)(copy.wait_recv)
+        copy.wait_recv() if when is None else pl.when(when())(copy.wait_recv)
+
+    def there(self, shift):
+        if shift == 0:
+            return None
+        me = self.me
+        return lambda: (me.z + shift >= 0) if shift < 0 else (me.z + shift < me.chips)
 
     def spread(self, blk, source, when=None):
         me = self.me
@@ -262,8 +239,9 @@
         for h in range(2):
             self.push(source(h), blk, h, me.at(k=1 - me.k), when)
 
-    def relay(self, z, when):
-        me = self.me
+    def relay(self, shift):
+        me, when = self.me, self.there(shift)
+        z = me.z + shift
         for h in range(2):
             if h == 0:
                 froms = [(me.a, (me.b + i) % me.second) for i in range(1, me.second)]
@@ -278,8 +256,9 @@
                     self.push(self.piece(blk, h), blk, h, me.at(**target), when)
                 self.push(self.piece(blk, h), blk, h, me.at(k=1 - me.k), when)
 
-    def settle(self, z, when):
-        me = self.me
+    def settle(self, shift):
+        me, when = self.me, self.there(shift)
+        z = me.z + shift
         for h in range(2):
             for i in range(1, me.second if h else me.first):
                 for j in range(me.first if h else me.second):
@@ -291,51 +270,59 @@
                     self.landed(blk, h, when)
                     self.push(self.piece(blk, h), blk, h, me.at(k=1 - me.k), when)
 
+    def stay(self, h):
+        return pltpu.make_async_copy(
+            self.x_ref.at[h], self.piece(self.own, h), self.own_sem.at[h]
+        )
+
     def begin(self):
         me, x_ref, own = self.me, self.x_ref, self.own
-        self.stays = [
-            pltpu.make_async_copy(x_ref.at[h], self.piece(own, h), self.own_sem.at[h])
-            for h in range(2)
-        ]
-        for stay in self.stays:
-            stay.start()
         for h in range(2):
-            self.push(x_ref.at[h], own, h, me.at(z=me.z + 1), me.z < me.chips - 1)
-            self.push(x_ref.at[h], own, h, me.at(z=me.z - 1), me.z > 0)
+            self.stay(h).start()
+        for h in range(2):
+            self.push(x_ref.at[h], own, h, me.at(z=me.z + 1), self.there(1))
+            self.push(x_ref.at[h], own, h, me.at(z=me.z - 1), self.there(-1))
         self.spread(own, lambda h: x_ref.at[h])
-        self.queue = [(me.z, None)]
 
     def stage(self, t):
-        me, fresh = self.me, []
-        for sign in (-1, 1):
-            z = me.z + sign * t
-            there = (z >= 0) if sign < 0 else (z < me.chips)
-            blk = self.index(z, me.a, me.b)
-            further = (me.z < me.chips - 1) if sign < 0 else (me.z > 0)
+        me = self.me
+        for shift in (-t, t):
+            there, onward = self.there(shift), self.there(1 if shift < 0 else -1)
+            blk = self.index(me.z + shift, me.a, me.b)
             for h in range(2):
                 self.landed(blk, h, there)
-                self.push(self.piece(blk, h), blk, h, me.at(z=me.z - sign), there & further)
+                self.push(
+                    self.piece(blk, h), blk, h, me.at(z=me.z + (1 if shift < 0 else -1)),
+                    lambda there=there, onward=onward: there() & onward(),
+                )
             self.spread(blk, lambda h, blk=blk: self.piece(blk, h), there)
-            fresh.append((z, there))
-        self.drain()
-        self.queue = fresh
-
-    def drain(self):
-        for z, there in self.queue:
-            self.relay(z, there)
-        for z, there in self.queue:
-            self.settle(z, there)
+
+    def drain(self, t):
+        shifts = (-t, t) if t else (0,)
+        for shift in shifts:
+            self.relay(shift)
+        for shift in shifts:
+            self.settle(shift)
+
+    def along(self):
+        return [functools.partial(self.stage, t) for t in range(1, self.me.chips)]
+
+    def across(self):
+        return [functools.partial(self.drain, t) for t in range(self.me.chips)]
 
     def finish(self):
         me = self.me
-        for stay in self.stays:
-            stay.wait()
+        for h in range(2):
+            self.stay(h).wait()
         for z in range(me.chips):
             for e in range(me.owners):
                 for h in range(2):
                     self.landed((z * 2 + 1 - me.k) * me.owners + e, h)
-        for copy, when in self.pending:
-            copy.wait_send() if when is None else pl.when(when)(copy.wait_send)
+        for i, when in enumerate(self.pending):
+            copy = remote(
+                self.x_ref.at[0], self.x_ref.at[0], self.sends.at[i], self.recv.at[0, 0], me.at()
+            )
+            copy.wait_send() if when is None else pl.when(when())(copy.wait_send)
 
 
 def taken(refs, number):
@@ -364,15 +351,16 @@
         gather.begin()
     if mails:
         mail.start()
-    for t in range(1, chips):
-        for gather in gathers:
-            gather.stage(t)
-        if t == min(START, chips - 1):
+    along = [stage for stages in zip(*[gather.along() for gather in gathers]) for stage in stages]
+    for i, stage in enumerate(along):
+        if i == len(along) - 1:
             load.start()
-    for gather in gathers:
-        gather.drain()
+        stage()
+    rest = [stage for stages in zip(*[gather.across() for gather in gathers]) for stage in stages]
+    for stage in rest[:2]:
+        stage()
     if mails:
-        j = len(jobs) - 1
+        j = 0
         load.landed(j)
         column = outs[j].at[:, me.ex]
         spreads = [
@@ -384,6 +372,9 @@
         ]
         for copy in spreads:
             copy.start()
+    for stage in rest[2:]:
+        stage()
+    if mails:
         mail.finish()
         for i in range(1, me.owners):
             e = (me.ex + i) % me.owners
@@ -393,7 +384,7 @@
             copy.wait_send()
     for gather in gathers:
         gather.finish()
-    load.finish(skip=(len(jobs) - 1,) if mails else ())
+    load.finish(skip=(0,) if mails else ())
 
 
 def gather_all(xs, orders, chips, owners, collective_id, jobs=(), mails=()):
@@ -423,211 +414,236 @@
     )(*ins)
 
 
-def scatter_kernel(
-    chips, first, second, by_row, column, width, jobs, mails, *refs
-):
-    me = Place(chips, first, second)
-    owners = first * second
-    n, m = len(jobs), len(mails)
-    p_ref, srcs, mail_srcs = refs[0], refs[1 : n + 1], refs[n + 1 : n + m + 1]
-    refs = refs[n + m + 1 :]
-    out_ref, outs, mail_outs = refs[0], refs[1 : n + 1], refs[n + 1 : n + m + 1]
-    refs = refs[n + m + 1 :]
-    mine, fromk, a0, b0, b1, a1, fromz, total = refs[:8]
-    load_sem, ks, a0s, b0s, b1s, a1s, zs, sends = refs[8:16]
-    refs = refs[16:]
-    mail = Mail(mails, me, mail_srcs, mail_outs, refs[:3])
-    carried = Load(jobs, me, srcs, outs, refs[3:] if mails else refs)
-    me.greet("all" if mails else "dp" if jobs else "near")
-    pending = []
-
-    def push(src, dst, sem, target, when=None):
-        copy = remote(src, dst, sends.at[len(pending)], sem, target)
-        pending.append((copy, when))
-        copy.start() if when is None else pl.when(when)(copy.start)
-
-    def landed(dst, sem):
-        remote(dst, dst, sends.at[0], sem, me.at()).wait_recv()
-
-    low = me.z < chips // 2
-
-    def line(t):
+class Scatter:
+    def __init__(self, me, by_row, column, width, p_ref, out_ref, refs):
+        self.me, self.by_row, self.cut = me, by_row, pl.ds(column, width)
+        self.p_ref, self.out_ref = p_ref, out_ref
+        self.mine, self.fromk, self.a0, self.b0, self.b1, self.a1, self.fromz = refs[:7]
+        self.load_sem, self.ks, self.a0s, self.b0s, self.b1s, self.a1s, self.zs, self.sends = refs[7:]
+        self.pending = []
+
+    @staticmethod
+    def scratch(chips, first, second, half, width):
+        sem, owners = pltpu.SemaphoreType.DMA, first * second
+        one = max(first - 1, 1), max(second - 1, 1)
+        sends = chips * (owners + 2 + 2 * (first - 1) * second + 2 * (second - 1) * first)
+        return [
+            pltpu.VMEM((chips, owners, 2, half, width), BF16),
+            pltpu.VMEM((chips, owners, 2, half, width), BF16),
+            pltpu.VMEM((chips, one[0], second, half, width), BF16),
+            pltpu.VMEM((chips, one[1], half, width), BF16),
+            pltpu.VMEM((chips, one[1], first, half, width), BF16),
+            pltpu.VMEM((chips, one[0], half, width), BF16),
+            pltpu.VMEM((chips + 1, 2, half, width), BF16),
+            sem((chips, owners)),
+            sem((chips, owners)),
+            sem((chips, one[0], second)),
+            sem((chips, one[1])),
+            sem((chips, one[1], first)),
+            sem((chips, one[0])),
+            sem((chips + 1,)),
+            sem((sends + chips * (first + second),)),
+        ]
+
+    def push(self, src, dst, sem, target, part, when=None):
+        copy = remote(src, dst, self.sends.at[len(self.pending)], sem, target)
+        self.pending.append((part, when))
+        copy.start() if when is None else pl.when(when())(copy.start)
+
+    def landed(self, dst, sem):
+        remote(dst, dst, self.sends.at[0], sem, self.me.at()).wait_recv()
+
+    def line(self, t):
+        z, chips = self.me.z, self.me.chips
         return jnp.where(
-            low,
-            jnp.where(t < chips - 1 - me.z, chips - 1 - t, t - (chips - 1 - me.z)),
-            jnp.where(t < me.z, t, chips - 1 - (t - me.z)),
+            z < chips // 2,
+            jnp.where(t < chips - 1 - z, chips - 1 - t, t - (chips - 1 - z)),
+            jnp.where(t < z, t, chips - 1 - (t - z)),
         )
 
-    cut = pl.ds(column, width)
-
-    def block(z, k, e):
-        blk = (z * 2 + k) * owners + e
-        return p_ref.at[:, blk, :, cut] if by_row else p_ref.at[blk, :, :, cut]
-
-    loads = {}
-    for t in range(chips):
-        z = line(t)
-        for e in range(owners):
-            load = pltpu.make_async_copy(
-                block(z, me.k, e), mine.at[t, e], load_sem.at[t, e]
-            )
-            load.start()
-            loads[t, e] = load
-            push(
-                block(z, 1 - me.k, e),
-                fromk.at[t, e], ks.at[t, e], me.at(k=1 - me.k),
-            )
-
-    mail.start()
-    carried.start()
-
+    def block(self, z, k, e):
+        blk = (z * 2 + k) * self.me.owners + e
+        if self.by_row:
+            return self.p_ref.at[:, blk, :, self.cut]
+        return self.p_ref.at[blk, :, :, self.cut]
+
+    def begin(self):
+        me = self.me
+        for t in range(me.chips):
+            z = self.line(t)
+            for e in range(me.owners):
+                pltpu.make_async_copy(
+                    self.block(z, me.k, e), self.mine.at[t, e], self.load_sem.at[t, e]
+                ).start()
+                self.push(
+                    self.block(z, 1 - me.k, e), self.fromk.at[t, e], self.ks.at[t, e],
+                    me.at(k=1 - me.k), "block",
+                )
+
+    @staticmethod
     def add(*terms):
         value = terms[0].astype(F32)
         for term in terms[1:]:
             value = value + term.astype(F32)
         return value
 
-    def step_one(t):
+    def step_one(self, t):
+        me, mine = self.me, self.mine
+        first, second = me.first, me.second
         for i in range(first):
             for j in range(second):
                 a, b = (me.a + 1 + i) % first, (me.b + 1 + j) % second
                 e = a * second + b
-                loads_sem = load_sem.at[t, e]
-                pltpu.make_async_copy(mine.at[t, e], mine.at[t, e], loads_sem).wait()
-                landed(fromk.at[t, e], ks.at[t, e])
-                mine[t, e] = add(mine[t, e], fromk[t, e]).astype(BF16)
+                pltpu.make_async_copy(mine.at[t, e], mine.at[t, e], self.load_sem.at[t, e]).wait()
+                self.landed(self.fromk.at[t, e], self.ks.at[t, e])
+                mine[t, e] = self.add(mine[t, e], self.fromk[t, e]).astype(BF16)
                 if i < first - 1:
-                    push(
-                        mine.at[t, e, 0], a0.at[t, first - 2 - i, b],
-                        a0s.at[t, first - 2 - i, b], me.at(a=a),
+                    slot = first - 2 - i
+                    self.push(
+                        mine.at[t, e, 0], self.a0.at[t, slot, b], self.a0s.at[t, slot, b],
+                        me.at(a=a), "half",
                     )
                 if j < second - 1:
-                    push(
-                        mine.at[t, e, 1], b1.at[t, second - 2 - j, a],
-                        b1s.at[t, second - 2 - j, a], me.at(b=b),
+                    slot = second - 2 - j
+                    self.push(
+                        mine.at[t, e, 1], self.b1.at[t, slot, a], self.b1s.at[t, slot, a],
+                        me.at(b=b), "half",
                     )
 
-    def step_two(t):
+    def step_two(self, t):
+        me, mine = self.me, self.mine
+        first, second = me.first, me.second
         for j in range(second - 1):
             b = (me.b + 1 + j) % second
             e = me.a * second + b
             for i in range(first - 1):
-                landed(a0.at[t, i, b], a0s.at[t, i, b])
-            mine[t, e, 0] = add(
-                mine[t, e, 0], *[a0[t, i, b] for i in range(first - 1)]
+                self.landed(self.a0.at[t, i, b], self.a0s.at[t, i, b])
+            mine[t, e, 0] = self.add(
+                mine[t, e, 0], *[self.a0[t, i, b] for i in range(first - 1)]
             ).astype(BF16)
-            push(
-                mine.at[t, e, 0], b0.at[t, second - 2 - j],
-                b0s.at[t, second - 2 - j], me.at(b=b),
+            slot = second - 2 - j
+            self.push(
+                mine.at[t, e, 0], self.b0.at[t, slot], self.b0s.at[t, slot], me.at(b=b), "half"
             )
         for i in range(first - 1):
             a = (me.a + 1 + i) % first
             e = a * second + me.b
             for j in range(second - 1):
-                landed(b1.at[t, j, a], b1s.at[t, j, a])
-            mine[t, e, 1] = add(
-                mine[t, e, 1], *[b1[t, j, a] for j in range(second - 1)]
+                self.landed(self.b1.at[t, j, a], self.b1s.at[t, j, a])
+            mine[t, e, 1] = self.add(
+                mine[t, e, 1], *[self.b1[t, j, a] for j in range(second - 1)]
             ).astype(BF16)
-            push(
-                mine.at[t, e, 1], a1.at[t, first - 2 - i],
-                a1s.at[t, first - 2 - i], me.at(a=a),
+            slot = first - 2 - i
+            self.push(
+                mine.at[t, e, 1], self.a1.at[t, slot], self.a1s.at[t, slot], me.at(a=a), "half"
             )
 
-    def step_three(t):
-        z = line(t)
-        e = me.ex
+    def step_three(self, t):
+        me, mine, total, fromz, zs = self.me, self.mine, self.out_ref, self.fromz, self.zs
+        first, second, chips = me.first, me.second, me.chips
+        z, e = self.line(t), me.ex
         for i in range(first - 1):
-            landed(a0.at[t, i, me.b], a0s.at[t, i, me.b])
-            landed(a1.at[t, i], a1s.at[t, i])
+            self.landed(self.a0.at[t, i, me.b], self.a0s.at[t, i, me.b])
+            self.landed(self.a1.at[t, i], self.a1s.at[t, i])
         for j in range(second - 1):
-            landed(b1.at[t, j, me.a], b1s.at[t, j, me.a])
-            landed(b0.at[t, j], b0s.at[t, j])
-        total[t, 0] = add(
-            mine[t, e, 0], *[a0[t, i, me.b] for i in range(first - 1)],
-            *[b0[t, j] for j in range(second - 1)],
+            self.landed(self.b1.at[t, j, me.a], self.b1s.at[t, j, me.a])
+            self.landed(self.b0.at[t, j], self.b0s.at[t, j])
+        total[0] = self.add(
+            mine[t, e, 0], *[self.a0[t, i, me.b] for i in range(first - 1)],
+            *[self.b0[t, j] for j in range(second - 1)],
         )
-        total[t, 1] = add(
-            mine[t, e, 1], *[b1[t, j, me.a] for j in range(second - 1)],
-            *[a1[t, i] for i in range(first - 1)],
+        total[1] = self.add(
+            mine[t, e, 1], *[self.b1[t, j, me.a] for j in range(second - 1)],
+            *[self.a1[t, i] for i in range(first - 1)],
         )
+
+        def also(when, slot):
+            @pl.when(when)
+            def _():
+                self.landed(fromz.at[slot], zs.at[slot])
+                total[...] = total[...] + fromz[slot].astype(F32)
+
         if t < chips - 1:
             up = z > me.z
-            from_beyond = jnp.where(up, me.z > 0, me.z < chips - 1)
-
-            @pl.when(from_beyond)
-            def _():
-                landed(fromz.at[z], zs.at[z])
-                total[t] = total[t] + fromz[z].astype(F32)
-
-            mine[t, e] = total[t].astype(BF16)
-            push(mine.at[t, e], fromz.at[z], zs.at[z], me.at(z=me.z + 1), up)
+            also(jnp.where(up, me.z > 0, me.z < chips - 1), z)
+            mine[t, e] = total[...].astype(BF16)
+            self.push(
+                mine.at[t, e], fromz.at[z], zs.at[z], me.at(z=me.z + 1), "block",
+                lambda: self.line(t) > me.z,
+            )
             slot = jnp.where(z == me.z - 1, chips, z)
-            push(mine.at[t, e], fromz.at[slot], zs.at[slot], me.at(z=me.z - 1), jnp.logical_not(up))
+            self.push(
+                mine.at[t, e], fromz.at[slot], zs.at[slot], me.at(z=me.z - 1), "block",
+                lambda: self.line(t) < me.z,
+            )
         else:
-
-            @pl.when(me.z > 0)
-            def _():
-                landed(fromz.at[me.z], zs.at[me.z])
-                total[t] = total[t] + fromz[me.z].astype(F32)
-
-            @pl.when(me.z < chips - 1)
-            def _():
-                landed(fromz.at[chips], zs.at[chips])
-                total[t] = total[t] + fromz[chips].astype(F32)
-
-            out_ref[...] = total[t]
-
-    for t in range(chips + 2):
-        if t < chips:
-            step_one(t)
-        if 0 <= t - 1 < chips:
-            step_two(t - 1)
-        if 0 <= t - 2 < chips:
-            step_three(t - 2)
+            also(me.z > 0, me.z)
+            also(me.z < chips - 1, chips)
+
+    def stage(self, t):
+        if t < self.me.chips:
+            self.step_one(t)
+        if 0 <= t - 1 < self.me.chips:
+            self.step_two(t - 1)
+        if 0 <= t - 2 < self.me.chips:
+            self.step_three(t - 2)
+
+    def stages(self):
+        return [functools.partial(self.stage, t) for t in range(self.me.chips + 2)]
+
+    def finish(self):
+        for i, (part, when) in enumerate(self.pending):
+            ref = self.mine.at[0, 0] if part == "block" else self.mine.at[0, 0, 0]
+            copy = remote(ref, ref, self.sends.at[i], self.zs.at[0], self.me.at())
+            copy.wait_send() if when is None else pl.when(when())(copy.wait_send)
+
+
+def scatter_parts(chips, owners, half, full):
+    parts = 1
+    while chips * owners * half * (full // parts) * 8 > 20 * 2**20:
+        parts *= 2
+    return parts
+
+
+def scatter_kernel(chips, first, second, by_row, column, width, jobs, mails, *refs):
+    me = Place(chips, first, second)
+    refs = list(refs)
+    (p_ref,) = taken(refs, 1)
+    srcs, mail_srcs = taken(refs, len(jobs)), taken(refs, len(mails))
+    (out_ref,) = taken(refs, 1)
+    outs, mail_outs = taken(refs, len(jobs)), taken(refs, len(mails))
+    scatter = Scatter(me, by_row, column, width, p_ref, out_ref, taken(refs, 15))
+    mail = Mail(mails, me, mail_srcs, mail_outs, taken(refs, 3) if mails else ())
+    load = Load(jobs, me, srcs, outs, refs)
+    me.greet("all" if mails else "dp" if jobs else "near")
+    scatter.begin()
+    mail.start()
+    load.start()
+    for stage in scatter.stages():
+        stage()
     mail.finish()
-    carried.finish()
-    for copy, when in pending:
-        copy.wait_send() if when is None else pl.when(when)(copy.wait_send)
+    load.finish()
+    scatter.finish()
 
 
 def scatter_sum(p, chips, owners, by_row, collective_id, jobs=(), mails=()):
     first, second = expert_factors(owners)
     half, full = p.shape[2:]
-    parts = 1
-    while chips * owners * half * (full // parts) * 8 > 20 * 2**20:
-        parts *= 2
+    parts = scatter_parts(chips, owners, half, full)
     width = full // parts
-    one = max(first - 1, 1), max(second - 1, 1)
-    sends = chips * (owners + 2 + 2 * (first - 1) * second + 2 * (second - 1) * first)
-    sends += chips * (first + second)
 
     def call(part, jobs, mails):
-        sem = pltpu.SemaphoreType.DMA
         return pl.pallas_call(
-            functools.partial(scatter_kernel, chips, first, second, by_row, part * width, width, jobs, mails),
+            functools.partial(
+                scatter_kernel, chips, first, second, by_row, part * width, width, jobs,
+                [jax.ShapeDtypeStruct(a.shape, a.dtype) for a in mails],
+            ),
             out_shape=[jax.ShapeDtypeStruct((2, half, width), F32)]
             + [job.out_shape for job in jobs]
             + Mail.shapes(mails, chips * 2 * owners),
             in_specs=[ANY] * (1 + len(jobs) + len(mails)),
             out_specs=[pl.BlockSpec(memory_space=pltpu.VMEM)] + [ANY] * (len(jobs) + len(mails)),
-            scratch_shapes=[
-                pltpu.VMEM((chips, owners, 2, half, width), BF16),
-                pltpu.VMEM((chips, owners, 2, half, width), BF16),
-                pltpu.VMEM((chips, one[0], second, half, width), BF16),
-                pltpu.VMEM((chips, one[1], half, width), BF16),
-                pltpu.VMEM((chips, one[1], first, half, width), BF16),
-                pltpu.VMEM((chips, one[0], half, width), BF16),
-                pltpu.VMEM((chips + 1, 2, half, width), BF16),
-                pltpu.VMEM((chips, 2, half, width), F32),
-                sem((chips, owners)),
-                sem((chips, owners)),
-                sem((chips, one[0], second)),
-                sem((chips, one[1])),
-                sem((chips, one[1], first)),
-                sem((chips, one[0])),
-                sem((chips + 1,)),
-                sem((sends,)),
-            ]
+            scratch_shapes=Scatter.scratch(chips, first, second, half, width)
             + Mail.scratch(mails, chips * 2 * owners)
             + Load.scratch(jobs, chips * 2),
             compiler_params=pltpu.CompilerParams(
@@ -641,6 +657,106 @@
     ]
     whole = calls[0][0] if parts == 1 else jnp.concatenate([c[0] for c in calls], axis=-1)
     return [whole] + list(calls[0][1:])
+
+
+class Riders:
+    def __init__(self, chips, owners, jobs=(), gather=None, scatter=None):
+        self.chips, self.owners, self.jobs = chips, owners, jobs
+        self.factors = expert_factors(owners)
+        self.orders = [order for pair in (gather, scatter) if pair for order in pair[1:]]
+        self.has = gather is not None, scatter is not None
+        self.ins = [pair[0] for pair in (gather, scatter) if pair] + [job.src for job in jobs]
+        self.out_shapes, self.out_specs, self.scratch = [], [], []
+        blocks = chips * 2 * owners
+        if gather:
+            x, by_row = gather
+            rest = x.shape[1:]
+            shape = (2, blocks) + rest if by_row else (blocks, 2) + rest
+            self.out_shapes.append(jax.ShapeDtypeStruct(shape, x.dtype))
+            self.out_specs.append(ANY)
+            self.scratch += Gather.scratch(chips, *self.factors)
+        if scatter:
+            half, full = scatter[0].shape[2:]
+            shape = jax.ShapeDtypeStruct((2, half, full), F32)
+            self.out_shapes.append(shape)
+            self.out_specs.append(pl.BlockSpec(shape.shape, lambda i: (0, 0, 0)))
+            self.scratch += Scatter.scratch(chips, *self.factors, half, full)
+            self.full = full
+        self.out_shapes += [job.out_shape for job in jobs]
+        self.out_specs += [ANY] * len(jobs)
+        self.scratch += Load.scratch(jobs, chips * 2)
+        self.ins_specs = [ANY] * len(self.ins)
+        self.count = len(self.ins)
+
+    def params(self, collective_id):
+        if not self.count:
+            return dict(vmem_limit_bytes=60 * 2**20)
+        return dict(
+            vmem_limit_bytes=60 * 2**20, collective_id=collective_id, has_side_effects=True
+        )
+
+    def board(self, refs, ins, outs, scratch=0):
+        refs = list(refs)
+        own = taken(refs, ins)
+        given = taken(refs, self.count)
+        own += taken(refs, outs)
+        results = taken(refs, self.count)
+        own += taken(refs, scratch)
+        if not self.count:
+            return own
+        self.me = me = Place(self.chips, *self.factors)
+        orders, staged, self.stages = list(self.orders), [], []
+        if self.has[0]:
+            rider = Gather(me, orders.pop(0), given.pop(0), results.pop(0), taken(refs, 3))
+            staged.append(rider)
+        if self.has[1]:
+            rider = Scatter(
+                me, orders.pop(0), 0, self.full, given.pop(0), results.pop(0), taken(refs, 15)
+            )
+            staged.append(rider)
+        load = Load(self.jobs, me, given, results, refs)
+        step, steps = pl.program_id(0), pl.num_programs(0)
+
+        @pl.when(step == 0)
+        def _():
+            me.greet("column" if not staged else "dp" if self.jobs else "near")
+            for rider in staged:
+                rider.begin()
+            if not self.has[0]:
+                load.start()
+
+        plan = []
+        for rider in staged:
+            if isinstance(rider, Gather):
+                along, across = rider.along(), rider.across()
+                along.insert(len(along) - 1, load.start)
+                plan += [(1 + i // 2, stage) for i, stage in enumerate(along)]
+                begin = 2 + len(along) // 2
+                plan += [
+                    (begin + i * (self.steps - 1 - begin) // len(across), stage)
+                    for i, stage in enumerate(across)
+                ]
+            else:
+                stages = rider.stages()
+                plan += [
+                    (1 + i * (self.steps - 2) // (len(stages) - 1), stage)
+                    for i, stage in enumerate(stages)
+                ]
+        for at, stage in plan:
+            pl.when(step == at)(stage)
+
+        def finish():
+            @pl.when(step == steps - 1)
+            def _():
+                for rider in staged:
+                    rider.finish()
+                load.finish()
+
+        self.alight = finish
+        return own
+
+    def alight(self):
+        pass
 
 
 def exchange_kernel(chips, first, second, array, x_ref, out_ref, *sems):
@@ -787,14 +903,12 @@
     return heads[0] if len(heads) == 1 else jnp.concatenate(heads, axis=1)
 
 
-def mixer_forward_kernel(count, jobs, chips, owners, *refs):
-    carried = Carried(jobs, chips, owners, refs, 12, 10)
+def mixer_forward_kernel(count, riders, *refs):
     (
         length_ref, x_ref, meta_ref, gain_ref, router_ref, wq_ref, wkv_ref, wo_ref,
         tri_ref, eye_ref, upper_ref, lower_ref,
         normed_ref, part_ref, rows_ref, key_ref, value_ref, query_ref, mix_ref, gated_ref, info_ref, gates_ref,
-    ) = carried.refs
-    carried.start()
+    ) = riders.board(refs, 12, 10)
     hc = key_ref.shape[2]
     x = x_ref[0].astype(F32)
     inverse = lax.rsqrt(jnp.mean(x * x, axis=1, keepdims=True) + EPSILON)
@@ -843,17 +957,15 @@
     out = [dot(gated[l * per : (l + 1) * per], wo_ref[l]).astype(BF16) for l in range(count)]
     out = out[0] if count == 1 else jnp.concatenate(out, axis=0)
     part_ref[0] = dot(seats.put, out).astype(BF16)
-    carried.finish()
-
-
-def mixer_backward_kernel(count, jobs, chips, owners, *refs):
-    carried = Carried(jobs, chips, owners, refs, 15, 5)
+    riders.alight()
+
+
+def mixer_backward_kernel(count, riders, *refs):
     (
         length_ref, grad_ref, meta_ref, wq_ref, wkv_ref, wo_ref, tri_ref, eye_ref,
         upper_ref, lower_ref, key_ref, value_ref, query_ref, mix_ref, info_ref,
         part_ref, rows_ref, terms_ref, grad_query_ref, grad_key_value_ref,
-    ) = carried.refs
-    carried.start()
+    ) = riders.board(refs, 15, 5)
     hc = key_ref.shape[2]
     seats = Seats(meta_ref[0], first_expert(count), count, tri_ref[...], eye_ref[...])
     per = seats.per
@@ -901,67 +1013,78 @@
     ]
     back = back[0] if count == 1 else jnp.concatenate(back, axis=0)
     part_ref[0] = (dot(seats.put, back) + dot_nt(grad_key_value, wkv_ref[...])).astype(BF16)
-    carried.finish()
-
-
-def feed_kernel(count, groups, offsets, offset_ref, x_ref, cot_ref, meta_ref, router_ref, wd_ref, tri_ref, eye_ref, *refs):
-    wg_ref, wu_ref = refs[0 : 2 * count : 2], refs[1 : 2 * count : 2]
+    riders.alight()
+
+
+def feed_kernel(count, l, last, groups, turns, riders, *refs):
+    prior = 2 * l if last else 0
+    refs = riders.board(refs, 10 + prior, 9 if last else 9, 4 if last else 2)
     (
-        part_ref, back_ref, rows_ref, cot_rows_ref, active_ref, grad_gate_ref, grad_up_ref, terms_ref,
-        gates_ref, out_ref, dx_ref, gate_ref, term_ref,
-    ) = refs[2 * count :]
+        offset_ref, x_ref, cot_ref, meta_ref, router_ref, wg_ref, wu_ref, wd_ref, tri_ref, eye_ref,
+    ) = refs[:10]
+    before, refs = refs[10 : 10 + prior], refs[10 + prior :]
+    part_ref, back_ref, rows_ref, cot_rows_ref, active_ref, grad_gate_ref, grad_up_ref, terms_ref, gates_ref = refs[:9]
+    gate_ref, term_ref = refs[9:11]
     kept = []
     for g in range(groups):
         seats = Seats(meta_ref[g], first_expert(count), count, tri_ref[...], eye_ref[...])
         kept.append(seats)
         per = seats.per
+        mine = slice(l * per, (l + 1) * per)
         one, two = seats.gates(dot(x_ref[g], router_ref[...]))
         lane = counted((seats.slots, 8), 1)
         gates_ref[g] = jnp.where(lane == 0, one, jnp.where(lane == 1, two, 0.0))
         (gate,) = seats.seat_values([(one, two)], [])
-        rows = dot(seats.take, x_ref[g]).astype(BF16)
+        take = seats.take[mine]
         valid = meta_ref[g][2:3] > 0.0
-        cot_rows = dot(jnp.where(valid, seats.take, 0.0).astype(BF16), cot_ref[g]).astype(BF16)
-        for l in range(count):
-            rows_ref[l, g * per : (g + 1) * per] = rows[l * per : (l + 1) * per]
-            cot_rows_ref[l, g * per : (g + 1) * per] = cot_rows[l * per : (l + 1) * per]
-            gate_ref[l, g * per : (g + 1) * per] = jnp.broadcast_to(
-                gate[l * per : (l + 1) * per], (per, LANES)
-            )
-    wide = wd_ref.shape[1]
-    for l in range(count):
-        rows, cot_rows, gate = rows_ref[l], cot_rows_ref[l], gate_ref[l][:, 0:1]
-        gate_part = dot(rows, wg_ref[l][...])
-        up_part = dot(rows, wu_ref[l][...])
-        grad_plain = dot_nt(cot_rows, wd_ref[l])
-        sigmoid = 1.0 / (1.0 + jnp.exp(-gate_part))
-        silu = gate_part * sigmoid
-        active = silu * up_part
-        gated = active * gate
-        front = gated
-        for off in offsets:
-            front = jnp.where(offset_ref[0] == off, pltpu.roll(gated, wide - off, 1), front)
-        active_ref[l] = front.astype(BF16)
-        gated = gated.astype(BF16)
-        term = jnp.sum(active * grad_plain, axis=1, keepdims=True)
-        grad_active = grad_plain * gate
-        grad_up = (grad_active * silu).astype(BF16)
-        grad_gate = (
-            grad_active * up_part * sigmoid * (1.0 + gate_part * (1.0 - sigmoid))
-        ).astype(BF16)
-        grad_gate_ref[l], grad_up_ref[l] = grad_gate, grad_up
-        out = dot(gated, wd_ref[l]).astype(BF16)
-        back = (dot_nt(grad_gate, wg_ref[l][...]) + dot_nt(grad_up, wu_ref[l][...])).astype(BF16)
+        here = slice(g * per, (g + 1) * per)
+        rows_ref[here] = dot(take, x_ref[g]).astype(BF16)
+        cot_rows_ref[here] = dot(jnp.where(valid, take, 0.0).astype(BF16), cot_ref[g]).astype(BF16)
+        gate_ref[here] = jnp.broadcast_to(gate[mine], (per, LANES))
+    wide = wd_ref.shape[0]
+    rows, cot_rows, gate = rows_ref[...], cot_rows_ref[...], gate_ref[...][:, 0:1]
+    gate_part = dot(rows, wg_ref[...])
+    up_part = dot(rows, wu_ref[...])
+    grad_plain = dot_nt(cot_rows, wd_ref[...])
+    sigmoid = 1.0 / (1.0 + jnp.exp(-gate_part))
+    silu = gate_part * sigmoid
+    active = silu * up_part
+    gated = active * gate
+    front = gated
+    for off in turns:
+        front = jnp.where(offset_ref[0] == off, pltpu.roll(gated, wide - off, 1), front)
+    active_ref[...] = front.astype(BF16)
+    gated = gated.astype(BF16)
+    term = jnp.sum(active * grad_plain, axis=1, keepdims=True)
+    term_ref[...] = jnp.broadcast_to(term, term_ref.shape)
+    grad_active = grad_plain * gate
+    grad_up = (grad_active * silu).astype(BF16)
+    grad_gate = (
+        grad_active * up_part * sigmoid * (1.0 + gate_part * (1.0 - sigmoid))
+    ).astype(BF16)
+    grad_gate_ref[...], grad_up_ref[...] = grad_gate, grad_up
+    out = dot(gated, wd_ref[...]).astype(BF16)
+    back = (dot_nt(grad_gate, wg_ref[...]) + dot_nt(grad_up, wu_ref[...])).astype(BF16)
+    if last:
+        out_ref, dx_ref = refs[11:]
         for g in range(groups):
-            out_ref[g, l * per : (l + 1) * per] = out[g * per : (g + 1) * per]
-            dx_ref[g, l * per : (l + 1) * per] = back[g * per : (g + 1) * per]
-            term_ref[g, l * per : (l + 1) * per] = jnp.broadcast_to(
-                term[g * per : (g + 1) * per], (per, LANES)
-            )
+            here = slice(g * per, (g + 1) * per)
+            for e in range(l):
+                out_ref[g, e * per : (e + 1) * per] = before[2 * e][here]
+                dx_ref[g, e * per : (e + 1) * per] = before[2 * e + 1][here]
+            out_ref[g, mine] = out[here]
+            dx_ref[g, mine] = back[here]
+        for g in range(groups):
+            part_ref[g] = dot(kept[g].put, out_ref[g]).astype(BF16)
+            back_ref[g] = dot(kept[g].put, dx_ref[g]).astype(BF16)
+    else:
+        part_ref[...], back_ref[...] = out, back
     for g in range(groups):
-        part_ref[g] = dot(kept[g].put, out_ref[g]).astype(BF16)
-        back_ref[g] = dot(kept[g].put, dx_ref[g]).astype(BF16)
-        terms_ref[g] = kept[g].slot_values(term_ref[g][:, 0:1])
+        value = term_ref[g * per : (g + 1) * per][:, 0:1]
+        parts = [value if e == l else jnp.zeros_like(value) for e in range(count)]
+        value = parts[0] if count == 1 else jnp.concatenate(parts, axis=0)
+        terms_ref[g] = kept[g].slot_values(value)
+    riders.alight()
 
 
 def whole_block(array):
@@ -990,8 +1113,9 @@
     return upper.astype(BF16), (table - upper).astype(BF16)
 
 
-def mixer_forward(x, meta, lengths, gain, router, wq, wkv, wo, fixed, jobs, chips, owners, collective_id):
+def mixer_forward(x, meta, lengths, gain, router, wq, wkv, wo, fixed, riders, collective_id):
     seqs, slots, _ = x.shape
+    riders.steps = seqs
     count, _, hc = wq.shape
     seats = slots // TOK_MB * CAP * count
     per = seats // count
@@ -1010,27 +1134,24 @@
     ]
     fixed_in = [gain, router, wq, wkv, wo, *fixed]
     return pl.pallas_call(
-        functools.partial(mixer_forward_kernel, count, jobs, chips, owners),
+        functools.partial(mixer_forward_kernel, count, riders),
         grid=(seqs,),
         out_shape=[jax.ShapeDtypeStruct(shape, dtype) for shape, dtype, _ in outs]
-        + [job.out_shape for job in jobs],
+        + riders.out_shapes,
         in_specs=[SMEM, step_block(x.shape), step_block(meta.shape)]
         + [whole_block(a) for a in fixed_in]
-        + [ANY] * len(jobs),
-        out_specs=[spec for _, _, spec in outs] + [ANY] * len(jobs),
-        scratch_shapes=Load.scratch(jobs, chips * 2),
-        compiler_params=pltpu.CompilerParams(
-            vmem_limit_bytes=60 * 2**20,
-            collective_id=collective_id if jobs else None,
-            has_side_effects=bool(jobs),
-        ),
-    )(lengths, x, meta, *fixed_in, *[job.src for job in jobs])
+        + riders.ins_specs,
+        out_specs=[spec for _, _, spec in outs] + riders.out_specs,
+        scratch_shapes=riders.scratch,
+        compiler_params=pltpu.CompilerParams(**riders.params(collective_id)),
+    )(lengths, x, meta, *fixed_in, *riders.ins)
 
 
 def mixer_backward(
-    grad, meta, lengths, wq, wkv, wo, fixed, saved, jobs, chips, owners, collective_id
+    grad, meta, lengths, wq, wkv, wo, fixed, saved, riders, collective_id
 ):
     seqs, slots, _ = grad.shape
+    riders.steps = seqs
     count, _, hc = wq.shape
     seats = slots // TOK_MB * CAP * count
     per = seats // count
@@ -1048,56 +1169,86 @@
     ]
     fixed_in = [wq, wkv, wo, *fixed]
     return pl.pallas_call(
-        functools.partial(mixer_backward_kernel, count, jobs, chips, owners),
+        functools.partial(mixer_backward_kernel, count, riders),
         grid=(seqs,),
         out_shape=[jax.ShapeDtypeStruct(shape, dtype) for shape, dtype, _ in outs]
-        + [job.out_shape for job in jobs],
+        + riders.out_shapes,
         in_specs=[SMEM, step_block(grad.shape), step_block(meta.shape)]
         + [whole_block(a) for a in fixed_in]
         + [step_block(a.shape) for a in saved]
-        + [ANY] * len(jobs),
-        out_specs=[spec for _, _, spec in outs] + [ANY] * len(jobs),
-        scratch_shapes=Load.scratch(jobs, chips * 2),
-        compiler_params=pltpu.CompilerParams(
-            vmem_limit_bytes=60 * 2**20,
-            collective_id=collective_id if jobs else None,
-            has_side_effects=bool(jobs),
-        ),
-    )(lengths, grad, meta, *fixed_in, *saved, *[job.src for job in jobs])
-
-
-def feed(x, cot, meta, router, wgu, wd, fixed, offset, offsets):
+        + riders.ins_specs,
+        out_specs=[spec for _, _, spec in outs] + riders.out_specs,
+        scratch_shapes=riders.scratch,
+        compiler_params=pltpu.CompilerParams(**riders.params(collective_id)),
+    )(lengths, grad, meta, *fixed_in, *saved, *riders.ins)
+
+
+def feed(x, cot, meta, router, wg, wu, wd, fixed, offset, offsets, l, count, before, riders, collective_id):
     groups, slots, _ = x.shape
-    count, wide, _ = wd.shape
+    wide, _ = wd.shape
     per = slots // TOK_MB * CAP
-    at_once = 2
+    last = l == count - 1
+    at_once = 2 if last else 4
+    riders.steps = groups // at_once
     seats = groups * per
-    shapes = [((groups, slots, D), BF16), ((groups, slots, D), BF16)]
-    specs = [step_block(s, at_once) for s, _ in shapes]
-    for width in (D, D, wide, wide, wide):
-        shapes.append(((count, seats, width), BF16))
-        specs.append(pl.BlockSpec((count, at_once * per, width), lambda i: (0, i, 0)))
-    for _ in range(2):
-        shapes.append(((groups, slots, 8), F32))
-        specs.append(step_block(shapes[-1][0], at_once))
-    fixed_in = [router, wd, *fixed, *wgu]
+
+    def of_rows(width):
+        return ((seats, width), BF16), pl.BlockSpec((at_once * per, width), lambda i: (i, 0))
+
+    def of_slots(width, dtype):
+        return ((groups, slots, width), dtype), step_block((groups, slots, width), at_once)
+
+    outs = [of_slots(D, BF16) if last else of_rows(D)] * 2
+    outs += [of_rows(width) for width in (D, D, wide, wide, wide)] + [of_slots(8, F32)] * 2
+    fixed_in = [router, wg, wu, wd, *fixed]
     turns = sorted({o for o in offsets if o})
+    scratch = [pltpu.VMEM((at_once * per, LANES), F32)] * 2
+    if last:
+        scratch += [pltpu.VMEM((at_once, count * per, D), BF16)] * 2
     return pl.pallas_call(
-        functools.partial(feed_kernel, count, at_once, turns),
+        functools.partial(feed_kernel, count, l, last, at_once, turns, riders),
         grid=(groups // at_once,),
-        out_shape=[jax.ShapeDtypeStruct(*s) for s in shapes],
+        out_shape=[jax.ShapeDtypeStruct(*shape) for shape, _ in outs] + riders.out_shapes,
         in_specs=[SMEM]
         + [step_block(a.shape, at_once) for a in (x, cot, meta)]
-        + [whole_block(a) for a in fixed_in],
-        out_specs=specs,
-        scratch_shapes=[
-            pltpu.VMEM((at_once, count * per, D), BF16),
-            pltpu.VMEM((at_once, count * per, D), BF16),
-            pltpu.VMEM((count, at_once * per, LANES), F32),
-            pltpu.VMEM((at_once, count * per, LANES), F32),
+        + [
+            pl.BlockSpec(a.shape, lambda i, n=a.ndim: (0,) * n, pipeline_mode=pl.Buffered(1))
+            for a in fixed_in
+        ]
+        + [of_rows(D)[1]] * len(before)
+        + riders.ins_specs,
+        out_specs=[spec for _, spec in outs] + riders.out_specs,
+        scratch_shapes=scratch + riders.scratch,
+        compiler_params=pltpu.CompilerParams(**riders.params(collective_id)),
+    )(offset.reshape(1), x, cot, meta, *fixed_in, *before, *riders.ins)
+
+
+def rejoin_kernel(owners, *refs):
+    *parts, key_value, query_out, key_value_out = refs
+    for l, part in enumerate(parts):
+        n_dp, _, hc = part.shape
+        for d in range(n_dp):
+            query_out[l, :, d * hc : (d + 1) * hc] = part[d].astype(F32)
+    for d in range(n_dp):
+        total = key_value[d * owners].astype(F32)
+        for e in range(1, owners):
+            total = total + key_value[d * owners + e].astype(F32)
+        for half in range(2):
+            at = (half * n_dp + d) * hc
+            key_value_out[:, at : at + hc] = total[:, half * hc : (half + 1) * hc]
+
+
+def rejoin(parts, key_value, owners):
+    n_dp, depth, hc = parts[0].shape
+    rows = key_value.shape[1]
+    return pl.pallas_call(
+        functools.partial(rejoin_kernel, owners),
+        out_shape=[
+            jax.ShapeDtypeStruct((len(parts), depth, n_dp * hc), F32),
+            jax.ShapeDtypeStruct((rows, 2 * n_dp * hc), F32),
         ],
-        compiler_params=pltpu.CompilerParams(vmem_limit_bytes=60 * 2**20),
-    )(offset.reshape(1), x, cot, meta, *fixed_in)
+        compiler_params=pltpu.CompilerParams(vmem_limit_bytes=48 * 2**20),
+    )(*parts, key_value)
 
 
 def norm_forward(values, norm_gain):
@@ -1224,14 +1375,7 @@
             lambda out, d: out.at[d],
         )
 
-    def spread_jobs(jobs, places):
-        lists = [[] for _ in range(places)]
-        for i, job in enumerate(jobs):
-            lists[i * places // len(jobs)].append(job)
-        return lists
-
-    input_lists = spread_jobs([input_job(l, g) for l in range(count) for g in range(2)], 4)
-    input_lists[2] += input_lists.pop()
+    input_jobs = [[input_job(l, g) for g in range(2)] for l in range(count)]
     down_full = lax.dynamic_update_slice(
         jnp.zeros((count, wide, D), BF16), down_weight, (0, offset, 0)
     )
@@ -1246,16 +1390,15 @@
         [route_lines(attention_routes), route_lines(feedforward_routes), tail]
     )
     small = jnp.pad(small, ((0, -small.shape[0] % 8), (0, 0)))[None]
-    tokens_all, cot_all, small, *resharded = gather_all(
-        [tokens[:, 0], cotangent[:, 0]], [True, False], chips, owners, 1,
-        [query_job(l) for l in range(count)] + [key_value_job], [small],
+    tokens_all, small, *resharded = gather_all(
+        [tokens[:, 0]], [True], chips, owners, 1,
+        [key_value_job] + [query_job(l) for l in range(count)], [small],
     )
     tokens_all = tokens_all.reshape(seqs, slots, D)
-    query_full = jnp.stack(resharded[:-1])
-    key_value_full = jnp.transpose(resharded[-1], (0, 1, 3, 2, 4)).reshape(D, 2 * hc)
+    query_full = jnp.stack(resharded[1:])
+    key_value_full = jnp.transpose(resharded[0], (0, 1, 3, 2, 4)).reshape(D, 2 * hc)
     group_slots = mb * TOK_MB * 2
     groups = devices // 2
-    cot_all = cot_all.reshape(groups, group_slots, D)
     lines = mb * 2 * TOK_MB // LANES
     mixer_routes = small[:, :lines].reshape(n_dp, owners, mb, 2, TOK_MB)
     mixer_meta = jnp.transpose(mixer_routes, (2, 0, 3, 1, 4)).reshape(seqs, 2, slots)
@@ -1286,36 +1429,50 @@
     tables = mixer_tables(slots)
     (
         mixer_all, mixer_part, rows_mixer, keys, values, queries, mixture, mixture_gated, info,
-        gates_mixer, *input_parts,
+        gates_mixer, cot_all, *input_parts,
     ) = mixer_forward(
         tokens_all, mixer_meta, row_lengths, gain_mixer[None], routers(router_mixer), query_full,
-        key_value_full, output_weight, (*fixed, *tables), input_lists[0], chips, owners, 2,
-    )
+        key_value_full, output_weight, (*fixed, *tables),
+        Riders(chips, owners, input_jobs[0][:1], gather=(cotangent[:, 0], False)), 2,
+    )
+    cot_all = cot_all.reshape(groups, group_slots, D)
     mixer_sum, *more_parts = scatter_sum(
-        mixer_part.reshape(mb, devices, TOK_MB, D), chips, owners, True, 10, input_lists[1]
+        mixer_part.reshape(mb, devices, TOK_MB, D), chips, owners, True, 10, input_jobs[0][1:]
     )
     input_parts += more_parts
 
     second = own_tokens + mixer_sum
     normed_feed, inverse_feed = norm_forward(second, gain_feed)
     feed_all, *more_parts = gather_all(
-        [normed_feed.astype(BF16)], [False], chips, owners, 3, input_lists[2]
+        [normed_feed.astype(BF16)], [False], chips, owners, 3,
+        input_jobs[1][:1] if count > 1 else [],
     )
     input_parts += more_parts
     feed_all = feed_all.reshape(groups, group_slots, D)
-    (
-        feed_part, grad_feed_part, rows_feed, cot_rows, active_gated, grad_gate, grad_up,
-        gate_terms_feed, gates_feed,
-    ) = feed(
-        feed_all, cot_all, feed_meta, routers(router_feed), input_parts, down_full,
-        constants(group_slots), offset, offsets,
-    )
-    back_lists = []
+    feed_fixed = constants(group_slots)
+    before, back_jobs, actives, cots, gate_terms_feed = [], [], [], [], 0.0
     for l in range(count):
+        carried = [job for jobs in input_jobs[l + 1 : l + 2] for job in jobs[l == 0 :]]
+        carried += back_jobs[:1]
+        (
+            feed_part, grad_feed_part, rows_feed, cot_rows, active_gated, grad_gate, grad_up,
+            terms, gates_feed, *more_parts,
+        ) = feed(
+            feed_all, cot_all, feed_meta, routers(router_feed), input_parts[2 * l], input_parts[2 * l + 1],
+            down_full[l], feed_fixed, offset, offsets, l, count, before, Riders(chips, owners, carried),
+            60 + l,
+        )
+        before += [feed_part, grad_feed_part]
+        grad_input_parts = more_parts[len(carried) - len(back_jobs[:1]) :]
+        input_parts += more_parts[: len(carried) - len(back_jobs[:1])]
         for grad in (grad_gate, grad_up):
-            back_lists.append(product("rd,rf->df", rows_feed[l], grad[l]).astype(BF16))
-    back_lists = spread_jobs([back_job(grad) for grad in back_lists], 4)
-    grad_down = product("lrf,lrd->lfd", active_gated[..., :share], cot_rows)
+            back_jobs.append(back_job(product("rd,rf->df", rows_feed, grad).astype(BF16)))
+        actives.append(active_gated[:, :share])
+        cots.append(cot_rows)
+        gate_terms_feed = gate_terms_feed + terms
+    if count > 1:
+        back_jobs = back_jobs[1:]
+    grad_down = product("lrf,lrd->lfd", jnp.stack(actives), jnp.stack(cots))
 
     def home_parts(terms, by_row):
         terms = terms[..., :2]
@@ -1337,10 +1494,11 @@
             gates.reshape(devices, mb, TOK_MB, 2), me, 0, keepdims=False
         )
 
-    grad_normed_feed, *grad_input_parts, terms = scatter_sum(
-        grad_feed_part.reshape(devices, mb, TOK_MB, D), chips, owners, False, 20, back_lists[0],
+    grad_normed_feed, *more_parts, terms = scatter_sum(
+        grad_feed_part.reshape(devices, mb, TOK_MB, D), chips, owners, False, 20, back_jobs[:1],
         [home_parts(gate_terms_feed, False)],
     )
+    grad_input_parts += more_parts
     grad_logits_feed = gate_grads(
         own_of(gates_feed, False), at_home(terms), feedforward_routes[:, 0]
     )
@@ -1349,22 +1507,24 @@
     grad_second = grad_second + own_cotangent
 
     grad_all, *more_parts = gather_all(
-        [grad_second.astype(BF16)], [True], chips, owners, 5, back_lists[1]
+        [grad_second.astype(BF16)], [True], chips, owners, 5, back_jobs[1:2]
     )
     grad_input_parts += more_parts
     grad_all = grad_all.reshape(seqs, slots, D)
-    feed_sum, *more_parts = scatter_sum(
-        feed_part.reshape(devices, mb, TOK_MB, D), chips, owners, False, 30, back_lists[2]
-    )
-    grad_input_parts += more_parts
-    result = (second + feed_sum).astype(BF16)[:, None]
+    feed_part = feed_part.reshape(devices, mb, TOK_MB, D)
+    beside = scatter_parts(chips, owners, TOK_MB, D) == 1
     (
         grad_mixer_part, grad_rows, gate_terms_mixer, grad_query_pre, grad_key_value, *more_parts
     ) = mixer_backward(
         grad_all, mixer_meta, row_lengths, query_full, key_value_full, output_weight,
-        (*fixed, *tables), (keys, values, queries, mixture, info), back_lists[3], chips, owners, 6,
-    )
+        (*fixed, *tables), (keys, values, queries, mixture, info),
+        Riders(chips, owners, back_jobs[2:], scatter=(feed_part, False) if beside else None), 6,
+    )
+    if not beside:
+        more_parts = scatter_sum(feed_part, chips, owners, False, 30) + more_parts
+    feed_sum, *more_parts = more_parts
     grad_input_parts += more_parts
+    result = (second + feed_sum).astype(BF16)[:, None]
     grad_output = product("lrc,lrd->lcd", mixture_gated, grad_rows)
     grad_query = [
         product("rd,rc->dc", rows_mixer[l], grad_query_pre[l]).astype(BF16) for l in range(count)
@@ -1379,11 +1539,7 @@
         ],
     )
     *more_parts, terms, grad_key_value_w = more_parts
-    grad_query = jnp.stack(more_parts, axis=1)
-    grad_key_value_w = jnp.sum(
-        grad_key_value_w.astype(F32).reshape(n_dp, owners, slice_rows, 2, hc), axis=1
-    )
-    grad_key_value_w = jnp.transpose(grad_key_value_w, (1, 2, 0, 3)).reshape(slice_rows, 2 * att)
+    grad_query, grad_key_value_w = rejoin(more_parts, grad_key_value_w, owners)
     grad_logits_mixer = gate_grads(
         own_of(gates_mixer, True), at_home(terms), attention_routes[:, 0]
     )
@@ -1404,7 +1560,6 @@
     last = last[: slice_rows * 18].reshape(slice_rows, 18)
     grad_gains, grad_router = last[:, :2], last[:, 2:]
 
-    grad_query = jnp.transpose(grad_query.astype(F32), (1, 2, 0, 3)).reshape(count, depth, att)
     grad_input = put_together(grad_input_parts, count, starts, tiles)
     return (
         result, grad_tokens, grad_gains, grad_router, grad_key_value_w, grad_query,

time: 1440 us -> 1280 us (0.89)
  Pallas kernels: 1260 us -> 1110 us
  local copies, waits for them, and re-layouts: 53.8 us -> 38.5 us
    pallas_call x3, Pallas kernels: 506 us -> 334 us  [gather_all(): pl.pallas_call(functools.partial(gather_kernel, chips, first, second, ord...]
    pallas_call x3 -> x5, Pallas kernels: 269 us -> 419 us  [the longest x2 162 us: feed(): pl.pallas_call(functools.partial(feed_kernel, count, l, last, at_once, tu...]
    pallas_call x4 -> x3, Pallas kernels: 458 us -> 332 us  [call(): pl.pallas_call(functools.partial(scatter_kernel, chips, first, second, by...]
where the time goes in v3:
time: 1280 us; the launch traced here: 1270 us
  Pallas kernels  1110 us (87%)
  matrix products  92.1 us (7%)
  local copies, waits for them, and re-layouts  38.5 us (3%)
  other arithmetic  25.5 us (2%)
    pallas_call x3, Pallas kernels, gather_all(): pl.pallas_call(functools.partial(gather_kernel, chips, first, second, ord...  334 us
    pallas_call x3, Pallas kernels, call(): pl.pallas_call(functools.partial(scatter_kernel, chips, first, second, by...  332 us
    pallas_call x2, Pallas kernels, feed(): pl.pallas_call(functools.partial(feed_kernel, count, l, last, at_once, tu...  162 us
    pallas_call x1, Pallas kernels, mixer_forward(): pl.pallas_call(functools.partial(mixer_forward_kernel, count, riders), gr...  139 us
    pallas_call x1, Pallas kernels, mixer_backward(): pl.pallas_call(functools.partial(mixer_backward_kernel, count, riders), g...  115 us
    dot_general x13, matrix products, product(): return jnp.einsum(pattern, operand, factor, preferred_element_type=F32)  92.1 us

profile of v3, /device:TPU:1, one launch (start us, length us, event | category | flops | bytes accessed | tf_op | source)
XLA Modules:
  0.0 1270.3 jit_solution(12303679800619935976)
XLA Ops:
  16.2 3.3 slice_bitcast_fusion
  19.5 124.2 %shard_map.196 = (bf16[2,32,64,2048]{3,2,1,0:T(8,128)(2,1)}, f32[32,16,128]{2,1,0:T(8,128)}, bf16[8,4,2,64,256]{4,3,2,1,0:T(8,128)(2,1)}, bf16[2048,256]{1,0:T(8,128)(2,1)}, bf16[2048,256]{1,0:T(8,128)(2,1)}) custom-call(bf16[2,64,2048]{2,1,0:T(8,128)(2,1)} %bitcast.171, f32[1,16,128]{2,1,0:T(8,128)} %fusion.60.refs_1_, bf16[2,64,2048]{2,1,0:T(8,128)(2,1)} %bitcast.174, ...), custom_call_target="tpu_custom_call" | custom-call | tf_op jit(solution)/shard_map/pallas_call | solution.py:404
  158.7 138.7 %shard_map.197 = (bf16[16,256,2048]{2,1,0:T(8,128)(2,1)}, bf16[16,256,2048]{2,1,0:T(8,128)(2,1)}, bf16[2,1536,2048]{2,1,0:T(8,128)(2,1)}, bf16[16,256,256]{2,1,0...) custom-call(s32[16]{0:T(128)} %convert_element_type.180.refs_0_, ...), custom_call_target="tpu_custom_call" | custom-call | tf_op jit(solution)/shard_map/pallas_call | solution.py:1136
  297.4 98.8 %shard_map.198 = (f32[2,64,2048]{2,1,0:T(8,128)}, bf16[2048,768]{1,0:T(8,128)(2,1)}) custom-call(bf16[2,32,64,2048]{3,2,1,0:T(8,128)(2,1)} %bitcast.165, bf16[2,256,11264]{2,1,0:T(8,128)(2,1)} %refs_10_.1), custom_call_target="tpu_custom_call" | custom-call | tf_op jit(solution)/shard_map/pallas_call | solution.py:636
  398.7 106.1 %shard_map.199 = (bf16[32,2,64,2048]{3,2,1,0:T(8,128)(2,1)}, bf16[2048,768]{1,0:T(8,128)(2,1)}) custom-call(bf16[2,64,2048]{2,1,0:T(8,128)(2,1)} %multiply_convert_fusion.refs_0_, bf16[2,256,11264]{2,1,0:T(8,128)(2,1)} %refs_10_.1), custom_call_target="tpu_custom_call" | custom-call | tf_op jit(solution)/shard_map/pallas_call | solution.py:404
  504.8 67.2 %shard_map.200 = (bf16[1536,2048]{1,0:T(8,128)(2,1)}, bf16[1536,2048]{1,0:T(8,128)(2,1)}, bf16[1536,2048]{1,0:T(8,128)(2,1)}, bf16[1536,2048]{1,0:T(8,128)(2,1)}...) custom-call(s32[1]{0:T(128)} %dynamic_slice.11.refs_0_, ...), custom_call_target="tpu_custom_call" | custom-call | tf_op jit(solution)/shard_map/pallas_call | solution.py:1208
  572.1 3.4 slice_bitcast_fusion.3
  575.4 9.9 convolution_convert_fusion.3.refs_12_
  585.4 6.5 convolution_convert_fusion.2.refs_1_
  591.9 94.8 %shard_map.201 = (bf16[16,256,2048]{2,1,0:T(8,128)(2,1)}, bf16[16,256,2048]{2,1,0:T(8,128)(2,1)}, bf16[1536,2048]{1,0:T(8,128)(2,1)}, bf16[1536,2048]{1,0:T(8,12...) custom-call(s32[1]{0:T(128)} %dynamic_slice.11.refs_0_, ...), custom_call_target="tpu_custom_call" | custom-call | tf_op jit(solution)/shard_map/pallas_call | solution.py:1208
  686.7 3.8 slice_add_fusion
  694.0 101.6 %shard_map.202 = (f32[2,64,2048]{2,1,0:T(8,128)}, bf16[8,256,768]{2,1,0:T(8,128)(2,1)}, f32[32,8,128]{2,1,0:T(8,128)}) custom-call(bf16[32,2,64,2048]{3,2,1,0:T(8,128)(2,1)} %bitcast.166, bf16[2048,768]{1,0:T(8,128)(2,1)} %convolution_convert_fusion.2.refs_1_, f32[32,8,128]{2,1,0:T(8,128)} %pad.41.refs_2_), custom_call_target="tpu_custom_call" | custom-call | tf_op jit(solution)/shard_map/pallas_call | solution.py:636
  805.0 15.6 %fusion = f32[2,704,2048]{2,1,0:T(8,128)} fusion(bf16[1,1536,2048]{2,1,0:T(8,128)(2,1)} %bitcast.201, bf16[1,1536,2048]{2,1,0:T(8,128)(2,1)} %bitcast.200, bf16[1,1536,704]{2,1,0:T(8,128)(2,1)} %slice_bitcast_fusion.2, bf16[1,1536,704]{2,1,0:T(8,128)(2,1)S(1)} %copy-done.10), kind=kOutput, calls=%fused_computation | convolution fusion | flops 8866824192 | bytes 28442624 | tf_op jit(solution)/shard_map/lrf,lrd->lfd/dot_general | solution.py:1313
  820.6 9.3 convolution_convert_fusion.1.refs_1_
  829.9 9.7 convolution_convert_fusion.refs_16_
  839.6 103.5 %shard_map.203 = (bf16[2,32,64,2048]{3,2,1,0:T(8,128)(2,1)}, bf16[8,256,768]{2,1,0:T(8,128)(2,1)}) custom-call(bf16[2,64,2048]{2,1,0:T(8,128)(2,1)} %fusion.59.refs_0_, bf16[2048,768]{1,0:T(8,128)(2,1)} %convolution_convert_fusion.1.refs_1_), custom_call_target="tpu_custom_call" | custom-call | tf_op jit(solution)/shard_map/pallas_call | solution.py:404
  943.1 115.1 %shard_map.204 = (bf16[16,256,2048]{2,1,0:T(8,128)(2,1)}, bf16[2,1536,2048]{2,1,0:T(8,128)(2,1)}, f32[16,256,8]{2,1,0:T(8,128)}, bf16[2,1536,256]{2,1,0:T(8,128)...) custom-call(s32[16]{0:T(128)} %convert_element_type.180.refs_0_, ...), custom_call_target="tpu_custom_call" | custom-call | tf_op jit(solution)/shard_map/pallas_call | solution.py:1171
  1058.2 14.8 %bitcast_convert_fusion = bf16[2048,512]{1,0:T(8,128)(2,1)} fusion(bf16[16,256,2048]{2,1,0:T(8,128)(2,1)} %get-tuple-element.107, bf16[16,256,512]{2,1,0:T(8,128)(2,1)} %get-tuple-element.108), kind=kOutput, calls=%fused_computation.13 | convolution fusion | flops 8590983168 | bytes 23068672 | tf_op jit(solution)/shard_map/std,stc->dc/dot_general | solution.py:1313
  1076.5 5.9 fusion.16.refs_2_
  1082.4 5.7 fusion.13.refs_1_
  1088.1 131.4 %shard_map.205 = (f32[2,64,2048]{2,1,0:T(8,128)}, bf16[8,256,256]{2,1,0:T(8,128)(2,1)}, bf16[8,256,256]{2,1,0:T(8,128)(2,1)}, f32[32,8,128]{2,1,0:T(8,128)}, bf16[32,64,512]{2,1,0:T(8,128)(2,1)}) custom-call(bf16[2,32,64,2048]{3,2,1,0:T(8,128)(2,1)} %bitcast.164, bf16[2048,256]{1,0:T(8,128)(2,1)} %fusion.13.refs_1_, bf16[2048,256]{1,0:T(8,128)(2,1)} %fusion.16.refs_2_, ...), custom_call_target="tpu_custom_call" | custom-call | tf_op jit(solution)/shard_map/pallas_call | solution.py:636
  1227.6 14.1 %shard_map.206 = f32[32,16,128]{2,1,0:T(8,128)} custom-call(f32[32,16,128]{2,1,0:T(8,128)} %bitcast.178), custom_call_target="tpu_custom_call" | custom-call | tf_op jit(solution)/shard_map/pallas_call | solution.py:774
  1244.2 9.9 fusion.76
  1257.6 12.2 shard_map.208
  (140 shorter events, 61.1 us)
Async XLA Ops:
  12.7 2.6 copy-start.7
  143.7 3.1 copy-start.14
  151.0 3.7 copy-start.12
  297.4 98.9 %copy-start.5 = (bf16[2,1,64,2048]{3,2,1,0:T(8,128)(2,1)S(1)}, bf16[2,1,64,2048]{3,2,1,0:T(8,128)(2,1)}, u32[]{:S(2)}) copy-start(bf16[2,1,64,2048]{3,2,1,0:T(8,128)(2,1)} %param.13) | copy-start | bytes 1572868
  572.0 3.4 copy-start.20
  572.1 13.3 %slice-start = ((s8[6291456]{0:T(1024)(128)(4,1)}), s8[4194304]{0:T(1024)(128)(4,1)S(1)}, s32[]{:S(2)}) async-start(s8[6291456]{0:T(1024)(128)(4,1)} %bitcast.202), calls=%async_computation | async-start | bytes 8388608
  575.4 9.9 slice-start.1
  575.4 9.9 copy-start.19
  694.0 103.8 %copy-start.16 = (s32[2,1,64,2]{2,3,1,0:T(2,128)S(1)}, s32[2,1,64,2]{2,3,1,0:T(2,128)}, u32[]{:S(2)}) copy-start(s32[2,1,64,2]{2,3,1,0:T(2,128)} %param.16) | copy-start | bytes 3076
  694.0 103.9 %copy-start.9 = (bf16[2,64,2048]{2,1,0:T(8,128)(2,1)S(1)}, bf16[2,64,2048]{2,1,0:T(8,128)(2,1)}, u32[]{:S(2)}) copy-start(bf16[2,64,2048]{2,1,0:T(8,128)(2,1)} %multiply_convert_fusion.refs_0_) | copy-start | bytes 1572868
  798.1 4.4 copy-start.11
  802.5 2.5 copy-start.10
  820.6 9.3 copy-start.18
  1076.5 5.9 copy-start.21
  1088.1 133.7 %copy-start.17 = (s32[2,1,64,2]{2,3,1,0:T(2,128)S(1)}, s32[2,1,64,2]{2,3,1,0:T(2,128)}, u32[]{:S(2)}) copy-start(s32[2,1,64,2]{2,3,1,0:T(2,128)} %param.15) | copy-start | bytes 3076
  1088.1 133.7 %copy-start.15 = (f32[2048]{0:T(1024)S(1)}, f32[2048]{0:T(1024)}, u32[]{:S(2)}) copy-start(f32[2048]{0:T(1024)} %get-tuple-element.159) | copy-start | bytes 24580
  1221.7 2.3 copy-start.6
  1221.7 2.3 copy-start.8
  1221.7 2.3 copy-start.13
  1225.6 18.6 %copy-start.4 = (bf16[2,1536,256]{2,1,0:T(8,128)(2,1)S(1)}, bf16[2,1536,256]{2,1,0:T(8,128)(2,1)}, u32[]{:S(2)}) copy-start(bf16[2,1536,256]{2,1,0:T(8,128)(2,1)} %get-tuple-element.117) | copy-start | bytes 4718596
  1244.2 9.9 copy-start.1
  1244.2 9.9 copy-start.2
  1244.2 9.9 copy-start.3
  1254.1 3.5 copy-start

commit v4 on v3

--- a/solution.py
+++ b/solution.py
@@ -2,6 +2,7 @@
 
 import jax
 import jax.numpy as jnp
+import numpy as np
 from jax import lax
 from jax.experimental import pallas as pl
 from jax.experimental.pallas import tpu as pltpu
@@ -106,8 +107,8 @@
             job.pick(self.srcs[j], dp), job.put(self.outs[j], dp), self.own.at[j]
         )
 
-    def start(self):
-        for j in range(len(self.jobs)):
+    def start(self, chosen=None):
+        for j in range(len(self.jobs)) if chosen is None else chosen:
             for i, d in self.peers():
                 self.copy(j, i, d).start()
             self.stay(j).start()
@@ -131,6 +132,133 @@
             return []
         sem = pltpu.SemaphoreType.DMA
         return [sem((len(jobs),)), sem((len(jobs), n_dp)), sem((len(jobs), n_dp))]
+
+
+class Work:
+    def __init__(self, a, b, dtype, l=None, keep=None, slot=None):
+        self.ins, self.l, self.keep, self.slot = (a, b), l, keep, slot
+        (self.k, self.m), self.n = a.shape[-2:], b.shape[-1]
+        shape = (keep or self.m, self.n)
+        self.shape = jax.ShapeDtypeStruct(shape if slot is None else (slot[1],) + shape, dtype)
+
+    def run(self, a_ref, b_ref, out_ref):
+        if self.l is not None:
+            a_ref = a_ref.at[self.l] if len(a_ref.shape) == 3 else a_ref
+            b_ref = b_ref.at[self.l] if len(b_ref.shape) == 3 else b_ref
+        k, m, n, keep = self.k, self.m, self.n, self.keep
+
+        def body(a, b, out):
+            value = lax.dot_general(
+                a[...], b[...], (((0,), (0,)), ((), ())), preferred_element_type=F32
+            )
+            out[...] = value[: out.shape[0]].astype(out.dtype)
+
+        if keep is None:
+            blk = 256 if k <= 8192 else 128
+            specs = [pl.BlockSpec((k, blk), lambda i: (0, i)), pl.BlockSpec((k, n), lambda i: (0, 0))]
+            out = pl.BlockSpec((blk, n), lambda i: (i, 0))
+            grid = m // blk
+        else:
+            blk = 512
+            specs = [pl.BlockSpec((k, m), lambda i: (0, 0)), pl.BlockSpec((k, blk), lambda i: (0, i))]
+            out = pl.BlockSpec((keep, blk), lambda i: (0, i))
+            grid = n // blk
+        pltpu.emit_pipeline(body, grid=(grid,), in_specs=specs, out_specs=[out])(
+            a_ref, b_ref, out_ref
+        )
+
+
+class Works:
+    def __init__(self, works, ins, outs):
+        self.works, self.ins, self.outs = works, ins, outs
+
+    def run(self, i):
+        if i < len(self.works):
+            slot = self.works[i].slot
+            out = self.outs[i] if slot is None else self.outs[i - slot[0]].at[slot[0]]
+            self.works[i].run(*self.ins[2 * i : 2 * i + 2], out)
+
+    @staticmethod
+    def shapes(works):
+        return [work.shape for work in works if work.slot is None or work.slot[0] == 0]
+
+    @staticmethod
+    def taken(works, refs):
+        return [
+            refs.pop(0) if work.slot is None or work.slot[0] == 0 else None for work in works
+        ]
+
+    @staticmethod
+    def arrays(works):
+        return [a for work in works for a in work.ins]
+
+
+class Fold:
+    def __init__(self, me, x_ref, out_ref, refs):
+        self.me, self.x_ref, self.out_ref = me, x_ref, out_ref
+        self.here, self.got, self.sem, self.send, self.recv, self.send_dp, self.recv_dp = refs
+
+    @staticmethod
+    def scratch(n_dp, owners, rows, columns):
+        sem = pltpu.SemaphoreType.DMA
+        return [
+            pltpu.VMEM((n_dp, rows, columns), BF16),
+            pltpu.VMEM((max(owners - 1, 1), n_dp, rows, columns), BF16),
+            sem((2,)), sem((owners,)), sem((owners,)), sem((n_dp,)), sem((n_dp,)),
+        ]
+
+    def first(self, i):
+        me = self.me
+        e = (me.ex + i) % me.owners
+        slot = me.owners - 1 - i
+        return remote(
+            self.x_ref.at[:, e], self.got.at[slot], self.send.at[i], self.recv.at[slot], (me.dp, e)
+        )
+
+    def second(self, i):
+        me = self.me
+        d = (me.dp + i) % me.n_dp
+        return remote(
+            self.here.at[d], self.out_ref.at[me.dp], self.send_dp.at[i], self.recv_dp.at[me.dp],
+            (d, me.ex),
+        )
+
+    def load(self):
+        return pltpu.make_async_copy(self.x_ref.at[:, self.me.ex], self.here, self.sem.at[0])
+
+    def stay(self):
+        dp = self.me.dp
+        return pltpu.make_async_copy(self.here.at[dp], self.out_ref.at[dp], self.sem.at[1])
+
+    def begin(self):
+        self.load().start()
+        for i in range(1, self.me.owners):
+            self.first(i).start()
+
+    def turn(self):
+        self.load().wait()
+        total = self.here[...].astype(F32)
+        for slot in range(self.me.owners - 1):
+            there = self.got.at[slot]
+            remote(
+                there, there, self.send.at[0], self.recv.at[slot], (self.me.dp, self.me.ex)
+            ).wait_recv()
+            total = total + self.got[slot].astype(F32)
+        self.here[...] = total.astype(BF16)
+        self.stay().start()
+        for i in range(1, self.me.n_dp):
+            self.second(i).start()
+
+    def finish(self):
+        me = self.me
+        self.stay().wait()
+        for i in range(1, me.owners):
+            self.first(i).wait_send()
+        for i in range(1, me.n_dp):
+            d = (me.dp + i) % me.n_dp
+            there = self.out_ref.at[d]
+            remote(there, there, self.send_dp.at[i], self.recv_dp.at[d], (d, me.ex)).wait_recv()
+            self.second(i).wait_send()
 
 
 class Mail:
@@ -329,15 +457,17 @@
     return [refs.pop(0) for _ in range(number)]
 
 
-def gather_kernel(chips, first, second, orders, jobs, mails, *refs):
+def gather_kernel(chips, first, second, orders, jobs, mails, works, *refs):
     me = Place(chips, first, second)
     refs = list(refs)
     x_refs = taken(refs, len(orders))
     mail_srcs = taken(refs, len(mails))
     srcs = taken(refs, len(jobs))
+    work_ins = taken(refs, 2 * len(works))
     out_refs = taken(refs, len(orders))
     mail_outs = taken(refs, len(mails))
     outs = taken(refs, len(jobs))
+    works = Works(works, work_ins, Works.taken(works, refs))
     gathers = [
         Gather(me, by_row, x_ref, out_ref, taken(refs, 3))
         for by_row, x_ref, out_ref in zip(orders, x_refs, out_refs)
@@ -359,6 +489,7 @@
     rest = [stage for stages in zip(*[gather.across() for gather in gathers]) for stage in stages]
     for stage in rest[:2]:
         stage()
+    works.run(0)
     if mails:
         j = 0
         load.landed(j)
@@ -372,8 +503,9 @@
         ]
         for copy in spreads:
             copy.start()
-    for stage in rest[2:]:
+    for i, stage in enumerate(rest[2:]):
         stage()
+        works.run(1 + i)
     if mails:
         mail.finish()
         for i in range(1, me.owners):
@@ -387,7 +519,7 @@
     load.finish(skip=(0,) if mails else ())
 
 
-def gather_all(xs, orders, chips, owners, collective_id, jobs=(), mails=()):
+def gather_all(xs, orders, chips, owners, collective_id, jobs=(), mails=(), works=()):
     first, second = expert_factors(owners)
     blocks = chips * 2 * owners
     sem = pltpu.SemaphoreType.DMA
@@ -397,20 +529,23 @@
         shape = (2, blocks) + rest if by_row else (blocks, 2) + rest
         shapes.append(jax.ShapeDtypeStruct(shape, x.dtype))
     shapes += Mail.shapes(mails, blocks) + [job.out_shape for job in jobs]
-    ins = list(xs) + list(mails) + [job.src for job in jobs]
+    shapes += Works.shapes(works)
+    ins = list(xs) + list(mails) + [job.src for job in jobs] + Works.arrays(works)
     scratch = Gather.scratch(chips, first, second) * len(xs)
     if mails:
         scratch += [sem((owners,)), sem((owners,))] + Mail.scratch(mails, blocks)
     return pl.pallas_call(
         functools.partial(
             gather_kernel, chips, first, second, orders, jobs,
-            [jax.ShapeDtypeStruct(a.shape, a.dtype) for a in mails],
+            [jax.ShapeDtypeStruct(a.shape, a.dtype) for a in mails], works,
         ),
         out_shape=shapes,
         in_specs=[ANY] * len(ins),
         out_specs=[ANY] * len(shapes),
         scratch_shapes=scratch + Load.scratch(jobs, chips * 2),
-        compiler_params=pltpu.CompilerParams(collective_id=collective_id, has_side_effects=True),
+        compiler_params=pltpu.CompilerParams(
+            collective_id=collective_id, has_side_effects=True, vmem_limit_bytes=60 * 2**20
+        ),
     )(*ins)
 
 
@@ -600,61 +735,92 @@
 
 def scatter_parts(chips, owners, half, full):
     parts = 1
-    while chips * owners * half * (full // parts) * 8 > 20 * 2**20:
+    while chips * owners * half * (full // parts) * 8 > 16 * 2**20:
         parts *= 2
     return parts
 
 
-def scatter_kernel(chips, first, second, by_row, column, width, jobs, mails, *refs):
+def scatter_kernel(chips, first, second, by_row, column, width, jobs, mails, works, fold, *refs):
     me = Place(chips, first, second)
     refs = list(refs)
     (p_ref,) = taken(refs, 1)
-    srcs, mail_srcs = taken(refs, len(jobs)), taken(refs, len(mails))
+    ready = [j for j, job in enumerate(jobs) if not isinstance(job.src, int)]
+    given, mail_srcs = taken(refs, len(ready)), taken(refs, len(mails))
+    work_ins = taken(refs, 2 * len(works))
     (out_ref,) = taken(refs, 1)
     outs, mail_outs = taken(refs, len(jobs)), taken(refs, len(mails))
+    work_outs = Works.taken(works, refs)
+    folded = taken(refs, 0 if fold is None else 1)
     scatter = Scatter(me, by_row, column, width, p_ref, out_ref, taken(refs, 15))
     mail = Mail(mails, me, mail_srcs, mail_outs, taken(refs, 3) if mails else ())
+    if fold is not None:
+        x_ref = work_outs[fold].reshape(
+            me.n_dp, me.owners, folded[0].shape[1], folded[0].shape[2]
+        )
+        folding = Fold(me, x_ref, folded[0], taken(refs, 7))
+    srcs = [given.pop(0) if j in ready else work_outs[job.src] for j, job in enumerate(jobs)]
     load = Load(jobs, me, srcs, outs, refs)
+    doing = Works(works, work_ins, work_outs)
     me.greet("all" if mails else "dp" if jobs else "near")
     scatter.begin()
     mail.start()
-    load.start()
-    for stage in scatter.stages():
-        stage()
+    load.start(ready)
+    stages = scatter.stages()
+    for i in range(max(len(stages), len(works))):
+        if i < len(stages):
+            stages[i]()
+        if fold is not None and i == fold + 1:
+            folding.turn()
+        doing.run(i)
+        load.start([j for j, job in enumerate(jobs) if j not in ready and job.src == i])
+        if i == fold:
+            folding.begin()
     mail.finish()
     load.finish()
+    if fold is not None:
+        folding.finish()
     scatter.finish()
 
 
-def scatter_sum(p, chips, owners, by_row, collective_id, jobs=(), mails=()):
+def scatter_sum(p, chips, owners, by_row, collective_id, jobs=(), mails=(), works=(), fold=None):
     first, second = expert_factors(owners)
     half, full = p.shape[2:]
     parts = scatter_parts(chips, owners, half, full)
     width = full // parts
-
-    def call(part, jobs, mails):
+    n_dp = chips * 2
+
+    def call(part, jobs, mails, works, fold):
+        extra_shapes, extra_scratch = [], []
+        if fold is not None:
+            rows, columns = works[fold].shape.shape
+            cut = (n_dp, rows // (n_dp * owners), columns)
+            extra_shapes = [jax.ShapeDtypeStruct(cut, BF16)]
+            extra_scratch = Fold.scratch(n_dp, owners, cut[1], columns)
+        shapes = [jax.ShapeDtypeStruct((2, half, width), F32)]
+        shapes += [job.out_shape for job in jobs] + Mail.shapes(mails, n_dp * owners)
+        shapes += Works.shapes(works) + extra_shapes
+        ins = [p] + [job.src for job in jobs if not isinstance(job.src, int)]
+        ins += list(mails) + Works.arrays(works)
         return pl.pallas_call(
             functools.partial(
                 scatter_kernel, chips, first, second, by_row, part * width, width, jobs,
-                [jax.ShapeDtypeStruct(a.shape, a.dtype) for a in mails],
+                [jax.ShapeDtypeStruct(a.shape, a.dtype) for a in mails], works, fold,
             ),
-            out_shape=[jax.ShapeDtypeStruct((2, half, width), F32)]
-            + [job.out_shape for job in jobs]
-            + Mail.shapes(mails, chips * 2 * owners),
-            in_specs=[ANY] * (1 + len(jobs) + len(mails)),
-            out_specs=[pl.BlockSpec(memory_space=pltpu.VMEM)] + [ANY] * (len(jobs) + len(mails)),
+            out_shape=shapes,
+            in_specs=[ANY] * len(ins),
+            out_specs=[pl.BlockSpec(memory_space=pltpu.VMEM)] + [ANY] * (len(shapes) - 1),
             scratch_shapes=Scatter.scratch(chips, first, second, half, width)
-            + Mail.scratch(mails, chips * 2 * owners)
-            + Load.scratch(jobs, chips * 2),
+            + Mail.scratch(mails, n_dp * owners)
+            + extra_scratch
+            + Load.scratch(jobs, n_dp),
             compiler_params=pltpu.CompilerParams(
                 collective_id=collective_id + part, has_side_effects=True,
                 vmem_limit_bytes=60 * 2**20,
             ),
-        )(p, *[job.src for job in jobs], *mails)
-
-    calls = [
-        call(part, () if part else jobs, () if part else mails) for part in range(parts)
-    ]
+        )(*ins)
+
+    calls = [call(0, jobs, mails, works, fold)]
+    calls += [call(part, (), (), (), None) for part in range(1, parts)]
     whole = calls[0][0] if parts == 1 else jnp.concatenate([c[0] for c in calls], axis=-1)
     return [whole] + list(calls[0][1:])
 
@@ -730,12 +896,11 @@
             if isinstance(rider, Gather):
                 along, across = rider.along(), rider.across()
                 along.insert(len(along) - 1, load.start)
-                plan += [(1 + i // 2, stage) for i, stage in enumerate(along)]
-                begin = 2 + len(along) // 2
-                plan += [
-                    (begin + i * (self.steps - 1 - begin) // len(across), stage)
-                    for i, stage in enumerate(across)
-                ]
+                unit = max(1, (self.steps - 4) // self.chips)
+                spots = [unit * (i + 1) for i in range(self.chips - 1)]
+                spots.insert(len(spots) - 1, spots[max(0, len(spots) - 2)])
+                spots += [unit * (i + 1) + 2 for i in range(self.chips)]
+                plan += list(zip(spots, along + across))
             else:
                 stages = rider.stages()
                 plan += [
@@ -905,10 +1070,10 @@
 
 def mixer_forward_kernel(count, riders, *refs):
     (
-        length_ref, x_ref, meta_ref, gain_ref, router_ref, wq_ref, wkv_ref, wo_ref,
+        length_ref, x_ref, meta_ref, gain_ref, router_ref, *wq_refs, wkv_ref, wo_ref,
         tri_ref, eye_ref, upper_ref, lower_ref,
         normed_ref, part_ref, rows_ref, key_ref, value_ref, query_ref, mix_ref, gated_ref, info_ref, gates_ref,
-    ) = riders.board(refs, 12, 10)
+    ) = riders.board(refs, 11 + count, 10)
     hc = key_ref.shape[2]
     x = x_ref[0].astype(F32)
     inverse = lax.rsqrt(jnp.mean(x * x, axis=1, keepdims=True) + EPSILON)
@@ -934,7 +1099,7 @@
     for l in range(count):
         rows_ref[l] = rows[l * per : (l + 1) * per]
     table = dot(seats.take, upper) + dot(seats.take, lower)
-    query = [dot(rows[l * per : (l + 1) * per], wq_ref[l]) for l in range(count)]
+    query = [dot(rows[l * per : (l + 1) * per], wq_refs[l][...]) for l in range(count)]
     query = query[0] if count == 1 else jnp.concatenate(query, axis=0)
     query = (turned(query, table[:, :HD], table[:, HD:]) * HD ** (-0.5)).astype(BF16)
     query_ref[0] = query
@@ -962,10 +1127,10 @@
 
 def mixer_backward_kernel(count, riders, *refs):
     (
-        length_ref, grad_ref, meta_ref, wq_ref, wkv_ref, wo_ref, tri_ref, eye_ref,
+        length_ref, grad_ref, meta_ref, *wq_refs, wkv_ref, wo_ref, tri_ref, eye_ref,
         upper_ref, lower_ref, key_ref, value_ref, query_ref, mix_ref, info_ref,
         part_ref, rows_ref, terms_ref, grad_query_ref, grad_key_value_ref,
-    ) = riders.board(refs, 15, 5)
+    ) = riders.board(refs, 14 + count, 5)
     hc = key_ref.shape[2]
     seats = Seats(meta_ref[0], first_expert(count), count, tri_ref[...], eye_ref[...])
     per = seats.per
@@ -1009,7 +1174,8 @@
     grad_key_value = jnp.concatenate([grad_key, joined(grad_value)], axis=1).astype(BF16)
     grad_key_value_ref[0] = grad_key_value
     back = [
-        dot_nt(grad_query[l * per : (l + 1) * per], wq_ref[l]).astype(BF16) for l in range(count)
+        dot_nt(grad_query[l * per : (l + 1) * per], wq_refs[l][...]).astype(BF16)
+        for l in range(count)
     ]
     back = back[0] if count == 1 else jnp.concatenate(back, axis=0)
     part_ref[0] = (dot(seats.put, back) + dot_nt(grad_key_value, wkv_ref[...])).astype(BF16)
@@ -1041,11 +1207,11 @@
         rows_ref[here] = dot(take, x_ref[g]).astype(BF16)
         cot_rows_ref[here] = dot(jnp.where(valid, take, 0.0).astype(BF16), cot_ref[g]).astype(BF16)
         gate_ref[here] = jnp.broadcast_to(gate[mine], (per, LANES))
-    wide = wd_ref.shape[0]
+    wide = wd_ref.shape[1]
     rows, cot_rows, gate = rows_ref[...], cot_rows_ref[...], gate_ref[...][:, 0:1]
     gate_part = dot(rows, wg_ref[...])
     up_part = dot(rows, wu_ref[...])
-    grad_plain = dot_nt(cot_rows, wd_ref[...])
+    grad_plain = dot_nt(cot_rows, wd_ref[0])
     sigmoid = 1.0 / (1.0 + jnp.exp(-gate_part))
     silu = gate_part * sigmoid
     active = silu * up_part
@@ -1063,7 +1229,7 @@
         grad_active * up_part * sigmoid * (1.0 + gate_part * (1.0 - sigmoid))
     ).astype(BF16)
     grad_gate_ref[...], grad_up_ref[...] = grad_gate, grad_up
-    out = dot(gated, wd_ref[...]).astype(BF16)
+    out = dot(gated, wd_ref[0]).astype(BF16)
     back = (dot_nt(grad_gate, wg_ref[...]) + dot_nt(grad_up, wu_ref[...])).astype(BF16)
     if last:
         out_ref, dx_ref = refs[11:]
@@ -1099,9 +1265,9 @@
 
 
 def constants(slots):
-    at = jnp.arange(slots)
+    at = np.arange(slots)
     earlier = (at[:, None] < at[None, :]) & (at[:, None] // TOK_MB == at[None, :] // TOK_MB)
-    return earlier.astype(BF16), (at[:, None] == at[None, :]).astype(BF16)
+    return jnp.asarray(earlier, BF16), jnp.asarray(np.eye(slots), BF16)
 
 
 def mixer_tables(slots):
@@ -1116,7 +1282,7 @@
 def mixer_forward(x, meta, lengths, gain, router, wq, wkv, wo, fixed, riders, collective_id):
     seqs, slots, _ = x.shape
     riders.steps = seqs
-    count, _, hc = wq.shape
+    count, hc = len(wq), wq[0].shape[1]
     seats = slots // TOK_MB * CAP * count
     per = seats // count
 
@@ -1132,7 +1298,7 @@
         by_row(slots, D), by_row(slots, D), by_expert(D), by_row(slots, hc), by_row(slots, hc),
         by_row(seats, hc), by_row(seats, hc, F32), by_expert(hc), by_row(seats, 8, F32), by_row(slots, 8, F32),
     ]
-    fixed_in = [gain, router, wq, wkv, wo, *fixed]
+    fixed_in = [gain, router, *wq, wkv, wo, *fixed]
     return pl.pallas_call(
         functools.partial(mixer_forward_kernel, count, riders),
         grid=(seqs,),
@@ -1152,7 +1318,7 @@
 ):
     seqs, slots, _ = grad.shape
     riders.steps = seqs
-    count, _, hc = wq.shape
+    count, hc = len(wq), wq[0].shape[1]
     seats = slots // TOK_MB * CAP * count
     per = seats // count
 
@@ -1167,7 +1333,7 @@
     outs = [
         by_row(slots, D), by_expert(D), by_row(slots, 8, F32), by_expert(hc), by_row(slots, 2 * hc)
     ]
-    fixed_in = [wq, wkv, wo, *fixed]
+    fixed_in = [*wq, wkv, wo, *fixed]
     return pl.pallas_call(
         functools.partial(mixer_backward_kernel, count, riders),
         grid=(seqs,),
@@ -1185,7 +1351,7 @@
 
 def feed(x, cot, meta, router, wg, wu, wd, fixed, offset, offsets, l, count, before, riders, collective_id):
     groups, slots, _ = x.shape
-    wide, _ = wd.shape
+    _, wide, _ = wd.shape
     per = slots // TOK_MB * CAP
     last = l == count - 1
     at_once = 2 if last else 4
@@ -1212,7 +1378,9 @@
         in_specs=[SMEM]
         + [step_block(a.shape, at_once) for a in (x, cot, meta)]
         + [
-            pl.BlockSpec(a.shape, lambda i, n=a.ndim: (0,) * n, pipeline_mode=pl.Buffered(1))
+            pl.BlockSpec((1, wide, D), lambda i: (l, 0, 0), pipeline_mode=pl.Buffered(1))
+            if a is wd
+            else pl.BlockSpec(a.shape, lambda i, n=a.ndim: (0,) * n, pipeline_mode=pl.Buffered(1))
             for a in fixed_in
         ]
         + [of_rows(D)[1]] * len(before)
@@ -1223,26 +1391,23 @@
     )(offset.reshape(1), x, cot, meta, *fixed_in, *before, *riders.ins)
 
 
-def rejoin_kernel(owners, *refs):
+def rejoin_kernel(*refs):
     *parts, key_value, query_out, key_value_out = refs
     for l, part in enumerate(parts):
         n_dp, _, hc = part.shape
         for d in range(n_dp):
             query_out[l, :, d * hc : (d + 1) * hc] = part[d].astype(F32)
     for d in range(n_dp):
-        total = key_value[d * owners].astype(F32)
-        for e in range(1, owners):
-            total = total + key_value[d * owners + e].astype(F32)
         for half in range(2):
             at = (half * n_dp + d) * hc
-            key_value_out[:, at : at + hc] = total[:, half * hc : (half + 1) * hc]
-
-
-def rejoin(parts, key_value, owners):
+            key_value_out[:, at : at + hc] = key_value[d, :, half * hc : (half + 1) * hc].astype(F32)
+
+
+def rejoin(parts, key_value):
     n_dp, depth, hc = parts[0].shape
     rows = key_value.shape[1]
     return pl.pallas_call(
-        functools.partial(rejoin_kernel, owners),
+        rejoin_kernel,
         out_shape=[
             jax.ShapeDtypeStruct((len(parts), depth, n_dp * hc), F32),
             jax.ShapeDtypeStruct((rows, 2 * n_dp * hc), F32),
@@ -1367,10 +1532,10 @@
             lambda out, d: out.at[pl.ds(pl.multiple_of(d * depth, depth), depth)],
         )
 
-    def back_job(grad):
+    def back_job(grad, columns):
         return Job(
             grad,
-            jax.ShapeDtypeStruct((n_dp, depth, grad.shape[1]), BF16),
+            jax.ShapeDtypeStruct((n_dp, depth, columns), BF16),
             lambda src, d: src.at[pl.ds(pl.multiple_of(d * depth, depth), depth)],
             lambda out, d: out.at[d],
         )
@@ -1391,11 +1556,11 @@
     )
     small = jnp.pad(small, ((0, -small.shape[0] % 8), (0, 0)))[None]
     tokens_all, small, *resharded = gather_all(
-        [tokens[:, 0]], [True], chips, owners, 1,
+        [tokens.reshape(mb, TOK_MB, D)], [True], chips, owners, 1,
         [key_value_job] + [query_job(l) for l in range(count)], [small],
     )
     tokens_all = tokens_all.reshape(seqs, slots, D)
-    query_full = jnp.stack(resharded[1:])
+    query_full = resharded[1:]
     key_value_full = jnp.transpose(resharded[0], (0, 1, 3, 2, 4)).reshape(D, 2 * hc)
     group_slots = mb * TOK_MB * 2
     groups = devices // 2
@@ -1433,7 +1598,7 @@
     ) = mixer_forward(
         tokens_all, mixer_meta, row_lengths, gain_mixer[None], routers(router_mixer), query_full,
         key_value_full, output_weight, (*fixed, *tables),
-        Riders(chips, owners, input_jobs[0][:1], gather=(cotangent[:, 0], False)), 2,
+        Riders(chips, owners, input_jobs[0][:1], gather=(cotangent.reshape(mb, TOK_MB, D), False)), 2,
     )
     cot_all = cot_all.reshape(groups, group_slots, D)
     mixer_sum, *more_parts = scatter_sum(
@@ -1450,7 +1615,7 @@
     input_parts += more_parts
     feed_all = feed_all.reshape(groups, group_slots, D)
     feed_fixed = constants(group_slots)
-    before, back_jobs, actives, cots, gate_terms_feed = [], [], [], [], 0.0
+    before, back_jobs, works, actives, cots, gate_terms_feed = [], [], [], [], [], 0.0
     for l in range(count):
         carried = [job for jobs in input_jobs[l + 1 : l + 2] for job in jobs[l == 0 :]]
         carried += back_jobs[:1]
@@ -1459,20 +1624,20 @@
             terms, gates_feed, *more_parts,
         ) = feed(
             feed_all, cot_all, feed_meta, routers(router_feed), input_parts[2 * l], input_parts[2 * l + 1],
-            down_full[l], feed_fixed, offset, offsets, l, count, before, Riders(chips, owners, carried),
+            down_full, feed_fixed, offset, offsets, l, count, before, Riders(chips, owners, carried),
             60 + l,
         )
         before += [feed_part, grad_feed_part]
         grad_input_parts = more_parts[len(carried) - len(back_jobs[:1]) :]
         input_parts += more_parts[: len(carried) - len(back_jobs[:1])]
-        for grad in (grad_gate, grad_up):
-            back_jobs.append(back_job(product("rd,rf->df", rows_feed, grad).astype(BF16)))
+        works += [Work(rows_feed, grad, BF16) for grad in (grad_gate, grad_up)]
+        if l < count - 1:
+            first_grad = product("rd,rf->df", rows_feed, grad_gate).astype(BF16)
+            back_jobs.append(back_job(first_grad, wide))
+            works.pop(-2)
         actives.append(active_gated[:, :share])
         cots.append(cot_rows)
         gate_terms_feed = gate_terms_feed + terms
-    if count > 1:
-        back_jobs = back_jobs[1:]
-    grad_down = product("lrf,lrd->lfd", jnp.stack(actives), jnp.stack(cots))
 
     def home_parts(terms, by_row):
         terms = terms[..., :2]
@@ -1494,11 +1659,12 @@
             gates.reshape(devices, mb, TOK_MB, 2), me, 0, keepdims=False
         )
 
-    grad_normed_feed, *more_parts, terms = scatter_sum(
-        grad_feed_part.reshape(devices, mb, TOK_MB, D), chips, owners, False, 20, back_jobs[:1],
-        [home_parts(gate_terms_feed, False)],
+    grad_normed_feed, first_part, terms, _, *later = scatter_sum(
+        grad_feed_part.reshape(devices, mb, TOK_MB, D), chips, owners, False, 20,
+        [back_job(0, wide)], [home_parts(gate_terms_feed, False)], works,
     )
-    grad_input_parts += more_parts
+    grad_input_parts.append(first_part)
+    later = [back_job(grad, wide) for grad in later]
     grad_logits_feed = gate_grads(
         own_of(gates_feed, False), at_home(terms), feedforward_routes[:, 0]
     )
@@ -1507,9 +1673,10 @@
     grad_second = grad_second + own_cotangent
 
     grad_all, *more_parts = gather_all(
-        [grad_second.astype(BF16)], [True], chips, owners, 5, back_jobs[1:2]
+        [grad_second.astype(BF16)], [True], chips, owners, 5, later[:1]
     )
-    grad_input_parts += more_parts
+    grad_down = product("lrf,lrd->lfd", jnp.stack(actives), jnp.stack(cots))
+    grad_input_parts += more_parts[:1]
     grad_all = grad_all.reshape(seqs, slots, D)
     feed_part = feed_part.reshape(devices, mb, TOK_MB, D)
     beside = scatter_parts(chips, owners, TOK_MB, D) == 1
@@ -1518,28 +1685,30 @@
     ) = mixer_backward(
         grad_all, mixer_meta, row_lengths, query_full, key_value_full, output_weight,
         (*fixed, *tables), (keys, values, queries, mixture, info),
-        Riders(chips, owners, back_jobs[2:], scatter=(feed_part, False) if beside else None), 6,
+        Riders(chips, owners, later[1:], scatter=(feed_part, False) if beside else None), 6,
     )
     if not beside:
         more_parts = scatter_sum(feed_part, chips, owners, False, 30) + more_parts
     feed_sum, *more_parts = more_parts
     grad_input_parts += more_parts
     result = (second + feed_sum).astype(BF16)[:, None]
-    grad_output = product("lrc,lrd->lcd", mixture_gated, grad_rows)
-    grad_query = [
-        product("rd,rc->dc", rows_mixer[l], grad_query_pre[l]).astype(BF16) for l in range(count)
-    ]
-    grad_key_value_w = product("std,stc->dc", mixer_all, grad_key_value).astype(BF16)
     grad_normed_mixer, *more_parts = scatter_sum(
         grad_mixer_part.reshape(mb, devices, TOK_MB, D), chips, owners, True, 40,
-        [back_job(grad) for grad in grad_query],
-        [
-            home_parts(gate_terms_mixer, True),
-            grad_key_value_w.reshape(devices, slice_rows, 2 * hc),
+        [back_job(l, hc) for l in range(count)],
+        [home_parts(gate_terms_mixer, True)],
+        [Work(rows_mixer, grad_query_pre, BF16, l=l) for l in range(count)]
+        + [
+            Work(mixer_all.reshape(seqs * slots, D), grad_key_value.reshape(seqs * slots, 2 * hc), BF16)
+        ]
+        + [
+            Work(mixture_gated, grad_rows, F32, l=l, keep=hc, slot=(l, count)) for l in range(count)
         ],
+        fold=count,
     )
-    *more_parts, terms, grad_key_value_w = more_parts
-    grad_query, grad_key_value_w = rejoin(more_parts, grad_key_value_w, owners)
+    query_parts, terms = more_parts[:count], more_parts[count]
+    grad_output = more_parts[-2]
+    grad_key_value_w = more_parts[-1]
+    grad_query, grad_key_value_w = rejoin(query_parts, grad_key_value_w)
     grad_logits_mixer = gate_grads(
         own_of(gates_mixer, True), at_home(terms), attention_routes[:, 0]
     )

time: 1280 us -> 1240 us (0.969)
  matrix products: 92.1 us -> 29.2 us
  Pallas kernels: 1110 us -> 1130 us
    dot_general x13 -> x6, matrix products: 92.1 us -> 29.2 us  [product(): return jnp.einsum(pattern, operand, factor, preferred_element_type=F32)]
    pallas_call x3, Pallas kernels: 332 us -> 374 us  [call(): pl.pallas_call(functools.partial(scatter_kernel, chips, first, second, by...]
    pallas_call x1, Pallas kernels: 139 us -> 119 us  [mixer_forward(): pl.pallas_call(functools.partial(mixer_forward_kernel, count, riders), gr...]
where the time goes in v4:
time: 1240 us; the launch traced here: 1230 us
  Pallas kernels  1130 us (91%)
  local copies, waits for them, and re-layouts  48.5 us (4%)
  matrix products  29.2 us (2%)
  other arithmetic  22.9 us (2%)
    pallas_call x3, Pallas kernels, call(): pl.pallas_call(functools.partial(scatter_kernel, chips, first, second, by...  374 us
    pallas_call x3, Pallas kernels, gather_all(): pl.pallas_call(functools.partial(gather_kernel, chips, first, second, ord...  332 us
    pallas_call x2, Pallas kernels, feed(): pl.pallas_call(functools.partial(feed_kernel, count, l, last, at_once, tu...  161 us
    pallas_call x1, Pallas kernels, mixer_forward(): pl.pallas_call(functools.partial(mixer_forward_kernel, count, riders), gr...  119 us
    pallas_call x1, Pallas kernels, mixer_backward(): pl.pallas_call(functools.partial(mixer_backward_kernel, count, riders), g...  115 us
    dot_general x6, matrix products, product(): return jnp.einsum(pattern, operand, factor, preferred_element_type=F32)  29.2 us

profile of v4, /device:TPU:1, one launch (start us, length us, event | category | flops | bytes accessed | tf_op | source)
XLA Modules:
  0.0 1234.5 jit_solution(4446202431118606353)
XLA Ops:
  6.3 123.9 %shard_map.232 = (bf16[2,32,64,2048]{3,2,1,0:T(8,128)(2,1)}, f32[32,16,128]{2,1,0:T(8,128)}, bf16[8,4,2,64,256]{4,3,2,1,0:T(8,128)(2,1)}, bf16[2048,256]{1,0:T(8,128)(2,1)}, bf16[2048,256]{1,0:T(8,128)(2,1)}) custom-call(bf16[2,64,2048]{2,1,0:T(8,128)(2,1)} %bitcast.139, f32[1,16,128]{2,1,0:T(8,128)} %fusion.41.refs_1_, bf16[2,64,2048]{2,1,0:T(8,128)(2,1)} %bitcast.142, ...), custom_call_target="tpu_custom_call" | custom-call | tf_op jit(solution)/shard_map/pallas_call | solution.py:537
  140.1 2.2 copy.60
  144.1 118.6 %shard_map.233 = (bf16[16,256,2048]{2,1,0:T(8,128)(2,1)}, bf16[16,256,2048]{2,1,0:T(8,128)(2,1)}, bf16[2,1536,2048]{2,1,0:T(8,128)(2,1)}, bf16[16,256,256]{2,1,0...) custom-call(s32[16]{0:T(128)} %convert_element_type.142.refs_0_, ...), custom_call_target="tpu_custom_call" | custom-call | tf_op jit(solution)/shard_map/pallas_call | solution.py:1302
  262.8 100.7 %shard_map.234 = (f32[2,64,2048]{2,1,0:T(8,128)}, bf16[2048,768]{1,0:T(8,128)(2,1)}) custom-call(bf16[2,32,64,2048]{3,2,1,0:T(8,128)(2,1)} %bitcast.131, bf16[2,256,11264]{2,1,0:T(8,128)(2,1)} %refs_10_.2), custom_call_target="tpu_custom_call" | custom-call | tf_op jit(solution)/shard_map/pallas_call | solution.py:804
  366.1 105.3 %shard_map.235 = (bf16[32,2,64,2048]{3,2,1,0:T(8,128)(2,1)}, bf16[2048,768]{1,0:T(8,128)(2,1)}) custom-call(bf16[2,64,2048]{2,1,0:T(8,128)(2,1)} %multiply_convert_fusion.refs_0_, bf16[2,256,11264]{2,1,0:T(8,128)(2,1)} %refs_10_.2), custom_call_target="tpu_custom_call" | custom-call | tf_op jit(solution)/shard_map/pallas_call | solution.py:537
  474.1 3.5 broadcast_in_dim.13
  477.6 6.2 constant_dynamic-update-slice_fusion.refs_7_
  486.0 67.0 %shard_map.236 = (bf16[1536,2048]{1,0:T(8,128)(2,1)}, bf16[1536,2048]{1,0:T(8,128)(2,1)}, bf16[1536,2048]{1,0:T(8,128)(2,1)}, bf16[1536,2048]{1,0:T(8,128)(2,1)}...) custom-call(s32[1]{0:T(128)} %dynamic_slice.11.refs_0_, ...), custom_call_target="tpu_custom_call" | custom-call | tf_op jit(solution)/shard_map/pallas_call | solution.py:1374
  553.1 9.3 convolution_convert_fusion.refs_12_
  562.4 94.3 %shard_map.237 = (bf16[16,256,2048]{2,1,0:T(8,128)(2,1)}, bf16[16,256,2048]{2,1,0:T(8,128)(2,1)}, bf16[1536,2048]{1,0:T(8,128)(2,1)}, bf16[1536,2048]{1,0:T(8,12...) custom-call(s32[1]{0:T(128)} %dynamic_slice.11.refs_0_, ...), custom_call_target="tpu_custom_call" | custom-call | tf_op jit(solution)/shard_map/pallas_call | solution.py:1374
  660.6 15.8 %fusion = f32[2,704,2048]{2,1,0:T(8,128)} fusion(bf16[1,1536,2048]{2,1,0:T(8,128)(2,1)} %bitcast.167, bf16[1,1536,2048]{2,1,0:T(8,128)(2,1)} %bitcast.166, bf16[1,1536,704]{2,1,0:T(8,128)(2,1)S(1)} %slice_bitcast_fusion, bf16[1,1536,704]{2,1,0:T(8,128)(2,1)} %slice_bitcast_fusion.1), kind=kOutput, calls=%fused_computation | convolution fusion | flops 8866824192 | bytes 28442624 | tf_op jit(solution)/shard_map/lrf,lrd->lfd/dot_general | solution.py:1478
  676.4 3.8 slice_add_fusion
  680.2 2.8 reshape.307
  683.7 129.7 %shard_map.238 = (f32[2,64,2048]{2,1,0:T(8,128)}, bf16[8,256,768]{2,1,0:T(8,128)(2,1)}, f32[32,8,128]{2,1,0:T(8,128)}, bf16[2048,768]{1,0:T(8,128)(2,1)}, bf16[2...) custom-call(bf16[32,2,64,2048]{3,2,1,0:T(8,128)(2,1)} %bitcast.136, f32[32,8,128]{2,1,0:T(8,128)} %pad.41.refs_1_, ...), custom_call_target="tpu_custom_call" | custom-call | tf_op jit(solution)/shard_map/pallas_call | solution.py:804
  817.7 2.6 fusion.40.refs_0_
  820.2 102.6 %shard_map.239 = (bf16[2,32,64,2048]{3,2,1,0:T(8,128)(2,1)}, bf16[8,256,768]{2,1,0:T(8,128)(2,1)}) custom-call(bf16[2,64,2048]{2,1,0:T(8,128)(2,1)} %fusion.40.refs_0_, bf16[2048,768]{1,0:T(8,128)(2,1)} %get-tuple-element.98.refs_1_), custom_call_target="tpu_custom_call" | custom-call | tf_op jit(solution)/shard_map/pallas_call | solution.py:537
  922.8 115.5 %shard_map.240 = (bf16[16,256,2048]{2,1,0:T(8,128)(2,1)}, bf16[2,1536,2048]{2,1,0:T(8,128)(2,1)}, f32[16,256,8]{2,1,0:T(8,128)}, bf16[2,1536,256]{2,1,0:T(8,128)...) custom-call(s32[16]{0:T(128)} %convert_element_type.142.refs_0_, ...), custom_call_target="tpu_custom_call" | custom-call | tf_op jit(solution)/shard_map/pallas_call | solution.py:1337
  1038.3 12.4 %shard_map.244 = f32[2,256,11264]{2,1,0:T(8,128)} custom-call(bf16[8,256,768]{2,1,0:T(8,128)(2,1)S(1)} %copy-done, bf16[8,256,768]{2,1,0:T(8,128)(2,1)} %get-tuple-element.126.refs_1_, bf16[8,256,768]{2,1,0:T(8,128)(2,1)} %get-tuple-element.127.refs_2_, bf16[8,256,768]{2,1,0:T(8,128)(2,1)} %get-tuple-element.128.refs_3_), custom_call_target="tpu_custom_call" | custom-call | tf_op jit(solution)/shard_map/pallas_call | solution.py:1467
  1050.7 2.7 reshape.313
  1054.2 143.7 %shard_map.241 = (f32[2,64,2048]{2,1,0:T(8,128)}, bf16[8,256,256]{2,1,0:T(8,128)(2,1)}, bf16[8,256,256]{2,1,0:T(8,128)(2,1)}, f32[32,8,128]{2,1,0:T(8,128)}, bf1...) custom-call(bf16[2,32,64,2048]{3,2,1,0:T(8,128)(2,1)} %bitcast.135, ...), custom_call_target="tpu_custom_call" | custom-call | tf_op jit(solution)/shard_map/pallas_call | solution.py:804
  1201.3 2.6 shard_map.243
  1212.2 14.3 %shard_map.242 = f32[32,16,128]{2,1,0:T(8,128)} custom-call(f32[32,16,128]{2,1,0:T(8,128)} %bitcast.146), custom_call_target="tpu_custom_call" | custom-call | tf_op jit(solution)/shard_map/pallas_call | solution.py:939
  1229.1 3.2 fusion.23
  1232.3 2.0 copy.97
  (128 shorter events, 46.5 us)
Async XLA Ops:
  132.3 683.3 %copy-start.4 = (f32[2048,18]{1,0:T(8,128)}, f32[2048,18]{1,0:T(8,128)S(1)}, u32[]{:S(2)}) copy-start(f32[2048,18]{1,0:T(8,128)S(1)} %reshape.298) | copy-start | bytes 442372
  132.3 7.8 copy-start.16
  262.7 100.7 %copy-start.10 = (bf16[2,1,64,2048]{3,2,1,0:T(8,128)(2,1)S(1)}, bf16[2,1,64,2048]{3,2,1,0:T(8,128)(2,1)}, u32[]{:S(2)}) copy-start(bf16[2,1,64,2048]{3,2,1,0:T(8,128)(2,1)} %param.17) | copy-start | bytes 1572868
  365.0 452.6 %copy-start.6 = (f32[2,64,2048]{2,1,0:T(8,128)}, f32[2,64,2048]{2,1,0:T(8,128)S(1)}, u32[]{:S(2)}) copy-start(f32[2,64,2048]{2,1,0:T(8,128)S(1)} %get-tuple-element.167) | copy-start | bytes 3145732
  366.1 105.3 %copy-start.23 = (s32[8]{0:T(128)S(1)}, s32[8]{0:T(128)}, u32[]{:S(2)}) copy-start(s32[8]{0:T(128)} %constant.55.clone) | copy-start | bytes 100
  477.6 7.5 copy-start.17
  656.7 2.4 copy-start.15
  683.7 131.9 %copy-start.20 = (s32[2,1,64,2]{2,3,1,0:T(2,128)S(1)}, s32[2,1,64,2]{2,3,1,0:T(2,128)}, u32[]{:S(2)}) copy-start(s32[2,1,64,2]{2,3,1,0:T(2,128)} %param.20) | copy-start | bytes 3076
  813.4 4.2 copy-start.22
  817.5 105.3 %copy-start.8 = (f32[2,64,2048]{2,1,0:T(8,128)}, f32[2,64,2048]{2,1,0:T(8,128)S(1)}, u32[]{:S(2)}) copy-start(f32[2,64,2048]{2,1,0:T(8,128)S(1)} %get-tuple-element.184) | copy-start | bytes 3145732
  922.8 115.5 %copy-start = (bf16[8,256,768]{2,1,0:T(8,128)(2,1)S(1)}, bf16[8,256,768]{2,1,0:T(8,128)(2,1)}, u32[]{:S(2)}) copy-start(bf16[8,256,768]{2,1,0:T(8,128)(2,1)} %get-tuple-element.125.refs_0_) | copy-start | bytes 9437188
  1054.2 152.0 %copy-start.11 = (bf16[2,1,64,2048]{3,2,1,0:T(8,128)(2,1)S(1)}, bf16[2,1,64,2048]{3,2,1,0:T(8,128)(2,1)}, u32[]{:S(2)}) copy-start(bf16[2,1,64,2048]{3,2,1,0:T(8,128)(2,1)} %param.17) | copy-start | bytes 1572868
  1054.2 152.0 %copy-start.19 = (f32[2048]{0:T(1024)S(1)}, f32[2048]{0:T(1024)}, u32[]{:S(2)}) copy-start(f32[2048]{0:T(1024)} %get-tuple-element.165) | copy-start | bytes 24580
  1054.2 152.3 %copy-start.13 = (bf16[2,64,2048]{2,1,0:T(8,128)(2,1)S(1)}, bf16[2,64,2048]{2,1,0:T(8,128)(2,1)}, u32[]{:S(2)}) copy-start(bf16[2,64,2048]{2,1,0:T(8,128)(2,1)} %multiply_convert_fusion.refs_0_) | copy-start | bytes 1572868
  1054.2 152.6 %copy-start.5 = (f32[2048,18]{1,0:T(8,128)S(1)}, f32[2048,18]{1,0:T(8,128)}, u32[]{:S(2)}) copy-start(f32[2048,18]{1,0:T(8,128)} %copy-done.4) | copy-start | bytes 442372
  1197.8 8.3 copy-start.21
  1197.8 1.2 copy-start.1
  1199.1 1.2 copy-start.2
  1200.3 1.0 copy-start.3
  1201.3 5.4 copy-start.18
  1208.4 20.7 %copy-start.7 = (f32[2,64,2048]{2,1,0:T(8,128)S(1)}, f32[2,64,2048]{2,1,0:T(8,128)}, u32[]{:S(2)}) copy-start(f32[2,64,2048]{2,1,0:T(8,128)} %copy-done.6) | copy-start | bytes 3145732
  1208.4 20.7 %copy-start.9 = (f32[2,64,2048]{2,1,0:T(8,128)S(1)}, f32[2,64,2048]{2,1,0:T(8,128)}, u32[]{:S(2)}) copy-start(f32[2,64,2048]{2,1,0:T(8,128)} %copy-done.8) | copy-start | bytes 3145732
  1208.4 20.7 %copy-start.12 = (bf16[2,1,64,2048]{3,2,1,0:T(8,128)(2,1)S(1)}, bf16[2,1,64,2048]{3,2,1,0:T(8,128)(2,1)}, u32[]{:S(2)}) copy-start(bf16[2,1,64,2048]{3,2,1,0:T(8,128)(2,1)} %param.28) | copy-start | bytes 1572868
  1229.1 3.2 copy-start.14

commit v5 on v4

--- a/solution.py
+++ b/solution.py
@@ -826,12 +826,13 @@
 
 
 class Riders:
-    def __init__(self, chips, owners, jobs=(), gather=None, scatter=None):
-        self.chips, self.owners, self.jobs = chips, owners, jobs
+    def __init__(self, chips, owners, jobs=(), gather=None, scatter=None, works=()):
+        self.chips, self.owners, self.jobs, self.works = chips, owners, jobs, works
         self.factors = expert_factors(owners)
         self.orders = [order for pair in (gather, scatter) if pair for order in pair[1:]]
         self.has = gather is not None, scatter is not None
         self.ins = [pair[0] for pair in (gather, scatter) if pair] + [job.src for job in jobs]
+        self.ins += Works.arrays(works)
         self.out_shapes, self.out_specs, self.scratch = [], [], []
         blocks = chips * 2 * owners
         if gather:
@@ -848,8 +849,8 @@
             self.out_specs.append(pl.BlockSpec(shape.shape, lambda i: (0, 0, 0)))
             self.scratch += Scatter.scratch(chips, *self.factors, half, full)
             self.full = full
-        self.out_shapes += [job.out_shape for job in jobs]
-        self.out_specs += [ANY] * len(jobs)
+        self.out_shapes += [job.out_shape for job in jobs] + Works.shapes(works)
+        self.out_specs += [ANY] * (len(jobs) + len(works))
         self.scratch += Load.scratch(jobs, chips * 2)
         self.ins_specs = [ANY] * len(self.ins)
         self.count = len(self.ins)
@@ -866,7 +867,7 @@
         own = taken(refs, ins)
         given = taken(refs, self.count)
         own += taken(refs, outs)
-        results = taken(refs, self.count)
+        results = taken(refs, len(self.out_shapes))
         own += taken(refs, scratch)
         if not self.count:
             return own
@@ -880,7 +881,9 @@
                 me, orders.pop(0), 0, self.full, given.pop(0), results.pop(0), taken(refs, 15)
             )
             staged.append(rider)
-        load = Load(self.jobs, me, given, results, refs)
+        n = len(self.jobs)
+        load = Load(self.jobs, me, given[:n], results[:n], refs)
+        works = Works(self.works, given[n:], results[n:])
         step, steps = pl.program_id(0), pl.num_programs(0)
 
         @pl.when(step == 0)
@@ -913,6 +916,8 @@
         def finish():
             @pl.when(step == steps - 1)
             def _():
+                for i in range(len(self.works)):
+                    works.run(i)
                 for rider in staged:
                     rider.finish()
                 load.finish()
@@ -1624,12 +1629,15 @@
             terms, gates_feed, *more_parts,
         ) = feed(
             feed_all, cot_all, feed_meta, routers(router_feed), input_parts[2 * l], input_parts[2 * l + 1],
-            down_full, feed_fixed, offset, offsets, l, count, before, Riders(chips, owners, carried),
-            60 + l,
+            down_full, feed_fixed, offset, offsets, l, count, before,
+            Riders(chips, owners, carried, works=works), 60 + l,
         )
         before += [feed_part, grad_feed_part]
         grad_input_parts = more_parts[len(carried) - len(back_jobs[:1]) :]
         input_parts += more_parts[: len(carried) - len(back_jobs[:1])]
+        done = more_parts[len(carried) :]
+        grad_input_parts = grad_input_parts[: len(back_jobs[:1])]
+        works = []
         works += [Work(rows_feed, grad, BF16) for grad in (grad_gate, grad_up)]
         if l < count - 1:
             first_grad = product("rd,rf->df", rows_feed, grad_gate).astype(BF16)
@@ -1659,12 +1667,12 @@
             gates.reshape(devices, mb, TOK_MB, 2), me, 0, keepdims=False
         )
 
-    grad_normed_feed, first_part, terms, _, *later = scatter_sum(
+    grad_normed_feed, first_part, terms, *later = scatter_sum(
         grad_feed_part.reshape(devices, mb, TOK_MB, D), chips, owners, False, 20,
-        [back_job(0, wide)], [home_parts(gate_terms_feed, False)], works,
+        [back_job(done[0] if done else 0, wide)], [home_parts(gate_terms_feed, False)], works,
     )
     grad_input_parts.append(first_part)
-    later = [back_job(grad, wide) for grad in later]
+    later = [back_job(grad, wide) for grad in (later if done else later[1:])]
     grad_logits_feed = gate_grads(
         own_of(gates_feed, False), at_home(terms), feedforward_routes[:, 0]
     )

time: 1240 us -> 1220 us (0.984)
  Pallas kernels: 1130 us -> 1110 us
    pallas_call x3, Pallas kernels: 374 us -> 343 us  [call(): pl.pallas_call(functools.partial(scatter_kernel, chips, first, second, by...]
where the time goes in v5:
time: 1220 us
  Pallas kernels  1110 us (91%)
  local copies, waits for them, and re-layouts  48.4 us (4%)
  matrix products  29.2 us (2%)
  other arithmetic  23 us (2%)
    pallas_call x3, Pallas kernels, call(): pl.pallas_call(functools.partial(scatter_kernel, chips, first, second, by...  343 us
    pallas_call x3, Pallas kernels, gather_all(): pl.pallas_call(functools.partial(gather_kernel, chips, first, second, ord...  332 us
    pallas_call x2, Pallas kernels, feed(): pl.pallas_call(functools.partial(feed_kernel, count, l, last, at_once, tu...  173 us
    pallas_call x1, Pallas kernels, mixer_forward(): pl.pallas_call(functools.partial(mixer_forward_kernel, count, riders), gr...  119 us
    pallas_call x1, Pallas kernels, mixer_backward(): pl.pallas_call(functools.partial(mixer_backward_kernel, count, riders), g...  115 us
    dot_general x6, matrix products, product(): return jnp.einsum(pattern, operand, factor, preferred_element_type=F32)  29.2 us

profile of v5, /device:TPU:1, one launch (start us, length us, event | category | flops | bytes accessed | tf_op | source)
XLA Modules:
  0.0 1215.4 jit_solution(17093747672304421842)
XLA Ops:
  6.3 123.9 %shard_map.232 = (bf16[2,32,64,2048]{3,2,1,0:T(8,128)(2,1)}, f32[32,16,128]{2,1,0:T(8,128)}, bf16[8,4,2,64,256]{4,3,2,1,0:T(8,128)(2,1)}, bf16[2048,256]{1,0:T(8,128)(2,1)}, bf16[2048,256]{1,0:T(8,128)(2,1)}) custom-call(bf16[2,64,2048]{2,1,0:T(8,128)(2,1)} %bitcast.139, f32[1,16,128]{2,1,0:T(8,128)} %fusion.41.refs_1_, bf16[2,64,2048]{2,1,0:T(8,128)(2,1)} %bitcast.142, ...), custom_call_target="tpu_custom_call" | custom-call | tf_op jit(solution)/shard_map/pallas_call | solution.py:537
  140.1 2.2 copy.60
  144.1 118.6 %shard_map.233 = (bf16[16,256,2048]{2,1,0:T(8,128)(2,1)}, bf16[16,256,2048]{2,1,0:T(8,128)(2,1)}, bf16[2,1536,2048]{2,1,0:T(8,128)(2,1)}, bf16[16,256,256]{2,1,0...) custom-call(s32[16]{0:T(128)} %convert_element_type.142.refs_0_, ...), custom_call_target="tpu_custom_call" | custom-call | tf_op jit(solution)/shard_map/pallas_call | solution.py:1307
  262.7 100.7 %shard_map.234 = (f32[2,64,2048]{2,1,0:T(8,128)}, bf16[2048,768]{1,0:T(8,128)(2,1)}) custom-call(bf16[2,32,64,2048]{3,2,1,0:T(8,128)(2,1)} %bitcast.131, bf16[2,256,11264]{2,1,0:T(8,128)(2,1)} %refs_10_.2), custom_call_target="tpu_custom_call" | custom-call | tf_op jit(solution)/shard_map/pallas_call | solution.py:804
  366.1 105.3 %shard_map.235 = (bf16[32,2,64,2048]{3,2,1,0:T(8,128)(2,1)}, bf16[2048,768]{1,0:T(8,128)(2,1)}) custom-call(bf16[2,64,2048]{2,1,0:T(8,128)(2,1)} %multiply_convert_fusion.refs_0_, bf16[2,256,11264]{2,1,0:T(8,128)(2,1)} %refs_10_.2), custom_call_target="tpu_custom_call" | custom-call | tf_op jit(solution)/shard_map/pallas_call | solution.py:537
  473.7 3.5 broadcast_in_dim.13
  477.2 6.2 constant_dynamic-update-slice_fusion.refs_7_
  485.6 67.0 %shard_map.236 = (bf16[1536,2048]{1,0:T(8,128)(2,1)}, bf16[1536,2048]{1,0:T(8,128)(2,1)}, bf16[1536,2048]{1,0:T(8,128)(2,1)}, bf16[1536,2048]{1,0:T(8,128)(2,1)}...) custom-call(s32[1]{0:T(128)} %dynamic_slice.11.refs_0_, ...), custom_call_target="tpu_custom_call" | custom-call | tf_op jit(solution)/shard_map/pallas_call | solution.py:1379
  552.6 9.3 convolution_convert_fusion.refs_12_
  561.9 105.8 %shard_map.237 = (bf16[16,256,2048]{2,1,0:T(8,128)(2,1)}, bf16[16,256,2048]{2,1,0:T(8,128)(2,1)}, bf16[1536,2048]{1,0:T(8,128)(2,1)}, bf16[1536,2048]{1,0:T(8,12...) custom-call(s32[1]{0:T(128)} %dynamic_slice.11.refs_0_, ...), custom_call_target="tpu_custom_call" | custom-call | tf_op jit(solution)/shard_map/pallas_call | solution.py:1379
  671.7 15.8 %fusion = f32[2,704,2048]{2,1,0:T(8,128)} fusion(bf16[1,1536,2048]{2,1,0:T(8,128)(2,1)} %bitcast.167, bf16[1,1536,2048]{2,1,0:T(8,128)(2,1)} %bitcast.166, bf16[1,1536,704]{2,1,0:T(8,128)(2,1)S(1)} %slice_bitcast_fusion, bf16[1,1536,704]{2,1,0:T(8,128)(2,1)} %slice_bitcast_fusion.1), kind=kOutput, calls=%fused_computation | convolution fusion | flops 8866824192 | bytes 28442624 | tf_op jit(solution)/shard_map/lrf,lrd->lfd/dot_general | solution.py:1483
  687.4 3.8 slice_add_fusion
  691.2 2.8 reshape.307
  694.7 99.8 %shard_map.238 = (f32[2,64,2048]{2,1,0:T(8,128)}, bf16[8,256,768]{2,1,0:T(8,128)(2,1)}, f32[32,8,128]{2,1,0:T(8,128)}, bf16[2048,768]{1,0:T(8,128)(2,1)}, bf16[2048,768]{1,0:T(8,128)(2,1)}) custom-call(bf16[32,2,64,2048]{3,2,1,0:T(8,128)(2,1)} %bitcast.133, bf16[2048,768]{1,0:T(8,128)(2,1)} %get-tuple-element.91.refs_1_, f32[32,8,128]{2,1,0:T(8,128)} %pad.41.refs_2_, ...), custom_call_target="tpu_custom_call" | custom-call | tf_op jit(solution)/shard_map/pallas_call | solution.py:804
  798.8 2.6 fusion.40.refs_0_
  801.4 103.1 %shard_map.239 = (bf16[2,32,64,2048]{3,2,1,0:T(8,128)(2,1)}, bf16[8,256,768]{2,1,0:T(8,128)(2,1)}) custom-call(bf16[2,64,2048]{2,1,0:T(8,128)(2,1)} %fusion.40.refs_0_, bf16[2048,768]{1,0:T(8,128)(2,1)} %get-tuple-element.100.refs_1_), custom_call_target="tpu_custom_call" | custom-call | tf_op jit(solution)/shard_map/pallas_call | solution.py:537
  904.5 115.4 %shard_map.240 = (bf16[16,256,2048]{2,1,0:T(8,128)(2,1)}, bf16[2,1536,2048]{2,1,0:T(8,128)(2,1)}, f32[16,256,8]{2,1,0:T(8,128)}, bf16[2,1536,256]{2,1,0:T(8,128)...) custom-call(s32[16]{0:T(128)} %convert_element_type.142.refs_0_, ...), custom_call_target="tpu_custom_call" | custom-call | tf_op jit(solution)/shard_map/pallas_call | solution.py:1342
  1020.0 12.4 %shard_map.244 = f32[2,256,11264]{2,1,0:T(8,128)} custom-call(bf16[8,256,768]{2,1,0:T(8,128)(2,1)S(1)} %copy-done, bf16[8,256,768]{2,1,0:T(8,128)(2,1)} %get-tuple-element.128.refs_1_, bf16[8,256,768]{2,1,0:T(8,128)(2,1)} %get-tuple-element.129.refs_2_, bf16[8,256,768]{2,1,0:T(8,128)(2,1)} %get-tuple-element.130.refs_3_), custom_call_target="tpu_custom_call" | custom-call | tf_op jit(solution)/shard_map/pallas_call | solution.py:1472
  1032.4 2.7 reshape.313
  1035.8 142.8 %shard_map.241 = (f32[2,64,2048]{2,1,0:T(8,128)}, bf16[8,256,256]{2,1,0:T(8,128)(2,1)}, bf16[8,256,256]{2,1,0:T(8,128)(2,1)}, f32[32,8,128]{2,1,0:T(8,128)}, bf1...) custom-call(bf16[2,32,64,2048]{3,2,1,0:T(8,128)(2,1)} %bitcast.136, ...), custom_call_target="tpu_custom_call" | custom-call | tf_op jit(solution)/shard_map/pallas_call | solution.py:804
  1182.1 2.6 shard_map.243
  1193.0 14.4 %shard_map.242 = f32[32,16,128]{2,1,0:T(8,128)} custom-call(f32[32,16,128]{2,1,0:T(8,128)} %bitcast.146), custom_call_target="tpu_custom_call" | custom-call | tf_op jit(solution)/shard_map/pallas_call | solution.py:944
  1209.9 3.2 fusion.23
  1213.1 2.0 copy.97
  (128 shorter events, 46.4 us)
Async XLA Ops:
  132.3 664.5 %copy-start.4 = (f32[2048,18]{1,0:T(8,128)}, f32[2048,18]{1,0:T(8,128)S(1)}, u32[]{:S(2)}) copy-start(f32[2048,18]{1,0:T(8,128)S(1)} %reshape.298) | copy-start | bytes 442372
  132.3 7.8 copy-start.16
  262.7 100.7 %copy-start.10 = (bf16[2,1,64,2048]{3,2,1,0:T(8,128)(2,1)S(1)}, bf16[2,1,64,2048]{3,2,1,0:T(8,128)(2,1)}, u32[]{:S(2)}) copy-start(bf16[2,1,64,2048]{3,2,1,0:T(8,128)(2,1)} %param.17) | copy-start | bytes 1572868
  365.0 433.8 %copy-start.6 = (f32[2,64,2048]{2,1,0:T(8,128)}, f32[2,64,2048]{2,1,0:T(8,128)S(1)}, u32[]{:S(2)}) copy-start(f32[2,64,2048]{2,1,0:T(8,128)S(1)} %get-tuple-element.169) | copy-start | bytes 3145732
  366.1 105.3 %copy-start.23 = (s32[8]{0:T(128)S(1)}, s32[8]{0:T(128)}, u32[]{:S(2)}) copy-start(s32[8]{0:T(128)} %constant.55.clone) | copy-start | bytes 100
  477.2 7.5 copy-start.17
  667.7 2.4 copy-start.15
  694.7 102.0 %copy-start.20 = (s32[2,1,64,2]{2,3,1,0:T(2,128)S(1)}, s32[2,1,64,2]{2,3,1,0:T(2,128)}, u32[]{:S(2)}) copy-start(s32[2,1,64,2]{2,3,1,0:T(2,128)} %param.20) | copy-start | bytes 3076
  794.5 4.2 copy-start.22
  798.7 105.8 %copy-start.8 = (f32[2,64,2048]{2,1,0:T(8,128)}, f32[2,64,2048]{2,1,0:T(8,128)S(1)}, u32[]{:S(2)}) copy-start(f32[2,64,2048]{2,1,0:T(8,128)S(1)} %get-tuple-element.186) | copy-start | bytes 3145732
  904.5 115.5 %copy-start = (bf16[8,256,768]{2,1,0:T(8,128)(2,1)S(1)}, bf16[8,256,768]{2,1,0:T(8,128)(2,1)}, u32[]{:S(2)}) copy-start(bf16[8,256,768]{2,1,0:T(8,128)(2,1)} %get-tuple-element.127.refs_0_) | copy-start | bytes 9437188
  1035.8 151.2 %copy-start.11 = (bf16[2,1,64,2048]{3,2,1,0:T(8,128)(2,1)S(1)}, bf16[2,1,64,2048]{3,2,1,0:T(8,128)(2,1)}, u32[]{:S(2)}) copy-start(bf16[2,1,64,2048]{3,2,1,0:T(8,128)(2,1)} %param.17) | copy-start | bytes 1572868
  1035.8 151.2 %copy-start.19 = (f32[2048]{0:T(1024)S(1)}, f32[2048]{0:T(1024)}, u32[]{:S(2)}) copy-start(f32[2048]{0:T(1024)} %get-tuple-element.167) | copy-start | bytes 24580
  1035.8 151.5 %copy-start.13 = (bf16[2,64,2048]{2,1,0:T(8,128)(2,1)S(1)}, bf16[2,64,2048]{2,1,0:T(8,128)(2,1)}, u32[]{:S(2)}) copy-start(bf16[2,64,2048]{2,1,0:T(8,128)(2,1)} %multiply_convert_fusion.refs_0_) | copy-start | bytes 1572868
  1035.8 151.7 %copy-start.5 = (f32[2048,18]{1,0:T(8,128)S(1)}, f32[2048,18]{1,0:T(8,128)}, u32[]{:S(2)}) copy-start(f32[2048,18]{1,0:T(8,128)} %copy-done.4) | copy-start | bytes 442372
  1178.6 8.3 copy-start.21
  1178.6 1.2 copy-start.1
  1179.9 1.2 copy-start.2
  1181.1 1.0 copy-start.3
  1182.1 5.4 copy-start.18
  1189.2 20.8 %copy-start.7 = (f32[2,64,2048]{2,1,0:T(8,128)S(1)}, f32[2,64,2048]{2,1,0:T(8,128)}, u32[]{:S(2)}) copy-start(f32[2,64,2048]{2,1,0:T(8,128)} %copy-done.6) | copy-start | bytes 3145732
  1189.2 20.8 %copy-start.9 = (f32[2,64,2048]{2,1,0:T(8,128)S(1)}, f32[2,64,2048]{2,1,0:T(8,128)}, u32[]{:S(2)}) copy-start(f32[2,64,2048]{2,1,0:T(8,128)} %copy-done.8) | copy-start | bytes 3145732
  1189.2 20.8 %copy-start.12 = (bf16[2,1,64,2048]{3,2,1,0:T(8,128)(2,1)S(1)}, bf16[2,1,64,2048]{3,2,1,0:T(8,128)(2,1)}, u32[]{:S(2)}) copy-start(bf16[2,1,64,2048]{3,2,1,0:T(8,128)(2,1)} %param.28) | copy-start | bytes 1572868
  1209.9 3.2 copy-start.14
